TPU v7x, 128 devices: a whole 4x4x4 slice. The times are simulated.
128 devices in a mesh: leaf: 16 (over z_hi, x, core), col: 8 (over y, z_lo).
Axes of the slice: x: 4, y: 4, z: 4 (z_hi: 2, z_lo: 2; z = z_hi * 2 + z_lo), core: 2. Of those that a mesh axis runs over, the one named last changes fastest.
Arguments:
- features: bfloat16 [48, 1048576], P(None, ('leaf', 'col')), may hold values from -12 to 12
- targets: bfloat16 [1048576], P(('leaf', 'col')), may hold values from -6 to 6
- owner: int32 [1048576], P(('leaf', 'col')), may hold values from 0 to 127, as said below
- length_scales: float32 [48], replicated, may hold values from 4 to 12
- ridge: float32 [1], replicated, may hold values from 0.0005 to 2
- leaf_pivots: int32 [16, 256], P('leaf'), may hold values from 0 to 65535, as said below
- parent_pivots: int32 [8, 256], replicated, may hold values from 0 to 511, as said below
- top_pivots: int32 [4, 256], replicated, may hold values from 0 to 511, as said below
Outputs:
- leaf_reduced: float32 [16, 256, 512], P('leaf', 'col')
- top_reduced: float32 [16, 256, 256], P('leaf', 'col')
- top_rhs: float32 [16, 256], P('leaf')
Inputs may be any that keep to these rules, and one draw needn't show every extreme that they name: `owner`: each block of 8192 consecutive samples names every block exactly 64 times. `leaf_pivots`: entries of a row are distinct. `parent_pivots`: entries of a row are distinct. `top_pivots`: entries of a row are distinct.
All inputs are finite; a program needn't handle non-finite values.
Results may differ from a plain program's by a relative error of at most 0.0029.
Values may be sent and summed in bfloat16 or wider, within the bound.
A program may use at most 64 MiB of HBM per device.

v0:
```python
import math

import jax
import jax.numpy as jnp
from jax import lax
from jax.sharding import PartitionSpec as P

RANK = 256


def from_partner(shard, axis, apart):
    return lax.ppermute(shard, axis, [(i, i ^ 1 << apart) for i in range(lax.axis_size(axis))])


def kernel(points, skel, inverse):
    left = points.astype(jnp.float32) * inverse[:, None]
    right = skel * inverse[:, None]
    cross = lax.dot_general(left, right, (((0,), (0,)), ((), ())), precision=lax.Precision.HIGHEST)
    dist = jnp.sum(left * left, 0)[:, None] + jnp.sum(right * right, 0)[None, :] - 2.0 * cross
    return jnp.exp(-0.5 * jnp.maximum(dist, 0.0))


def accumulate(points, values, own_skel, other_skel, inverse, width):
    count = points.shape[1] // width
    rank = own_skel.shape[1]
    contract = (((0,), (0,)), ((), ()))

    def step(index, carry):
        gram, couple, rhs = carry
        block = lax.dynamic_slice_in_dim(points, index * width, width, 1)
        target = lax.dynamic_slice_in_dim(values, index * width, width, 0)
        basis = kernel(block, own_skel, inverse).astype(jnp.bfloat16)
        across = kernel(block, other_skel, inverse).astype(jnp.bfloat16)
        gram = gram + lax.dot_general(basis, basis, contract, preferred_element_type=jnp.float32)
        couple = couple + lax.dot_general(
            basis, across, contract, preferred_element_type=jnp.float32
        )
        rhs = rhs + jnp.dot(target[None, :], basis, preferred_element_type=jnp.float32)[0]
        return (gram, couple, rhs)

    zero = jnp.zeros((rank, rank), jnp.float32)
    return lax.fori_loop(0, count, step, (zero, zero, jnp.zeros((rank,), jnp.float32)))


def merge_pair(first, second, first_rhs, second_rhs, first_skel, second_skel, pivots):
    rank = first.shape[0]
    lower = jnp.concatenate([second[:, rank:], second[:, :rank]], 1)
    whole = jnp.concatenate([first, lower], 0)
    chosen = jnp.take(jnp.take(whole, pivots, 0), pivots, 1)
    rhs = jnp.take(jnp.concatenate([first_rhs, second_rhs]), pivots)
    skel = jnp.take(jnp.concatenate([first_skel, second_skel], 1), pivots, 1)
    return (chosen, rhs, skel)


def merge_top(first, second, first_rhs, second_rhs, first_skel, second_skel, pivots, inverse):
    cross = kernel(first_skel, second_skel, inverse)
    whole = jnp.concatenate(
        [jnp.concatenate([first, cross], 1), jnp.concatenate([cross.T, second], 1)], 0
    )
    chosen = jnp.take(jnp.take(whole, pivots, 0), pivots, 1)
    rhs = jnp.take(jnp.concatenate([first_rhs, second_rhs]), pivots)
    return (chosen, rhs)


def arrange(joined, order, source, width):
    count = order.shape[0] // width

    def block(index):
        wanted = lax.dynamic_slice_in_dim(order, index * width, width, 0)
        selector = (source[:, None] == wanted[None, :]).astype(jnp.bfloat16)
        return jnp.dot(joined, selector, preferred_element_type=jnp.float32).astype(jnp.bfloat16)

    blocks = lax.map(block, jnp.arange(count, dtype=jnp.int32))
    return blocks.transpose(1, 0, 2).reshape(joined.shape[0], order.shape[0])


def local(features, targets, owner, length_scales, ridge, leaf_pivots, parent_pivots, top_pivots):
    rows = features.shape[1]
    feats = features.shape[0]
    inverse = 1.0 / length_scales
    columns = lax.axis_size("col")
    slab = RANK // columns
    column = lax.axis_index("col")
    leaf = lax.axis_index("leaf")
    order = jnp.argsort(owner, stable=True)
    source = jnp.arange(rows, dtype=jnp.int32)
    joined = jnp.concatenate([features, targets[None, :]], 0)
    arranged = arrange(joined, order, source, math.gcd(rows, 1024))
    received = lax.all_to_all(arranged, ("leaf", "col"), split_axis=1, concat_axis=1, tiled=True)
    placed = received[:feats]
    values = received[feats]
    pivots = leaf_pivots[0]
    keep = (pivots // rows == column).astype(jnp.float32)
    picker = (source[:, None] == (pivots % rows)[None, :]).astype(jnp.bfloat16)
    picked = jnp.dot(placed, picker, preferred_element_type=jnp.float32) * keep[None, :]
    own_skel = lax.psum(picked.astype(jnp.bfloat16), "col").astype(jnp.float32)
    other_skel = from_partner(own_skel.astype(jnp.bfloat16), "leaf", 0).astype(own_skel.dtype)
    gram, couple, rhs = accumulate(
        placed, values, own_skel, other_skel, inverse, math.gcd(rows, 4096)
    )
    stacked = jnp.concatenate([gram, couple], 1)
    node_rows = rows * columns
    eye = jnp.eye(RANK, 2 * RANK, dtype=jnp.float32)
    stacked, rhs = lax.psum((stacked, rhs), "col")
    stacked = stacked / node_rows + ridge[0] * eye
    rhs = rhs / node_rows
    share = lax.dynamic_slice_in_dim(stacked, column * slab, slab, 0)
    top_piv = lax.dynamic_index_in_dim(top_pivots, leaf // 4, 0, keepdims=False)
    partner, partner_rhs = from_partner((stacked, rhs), "leaf", 0)
    odd = leaf % 2 == 1
    par_piv = lax.dynamic_index_in_dim(parent_pivots, leaf // 2, 0, keepdims=False)
    par_m, par_r, par_s = merge_pair(
        jnp.where(odd, partner, stacked),
        jnp.where(odd, stacked, partner),
        jnp.where(odd, partner_rhs, rhs),
        jnp.where(odd, rhs, partner_rhs),
        jnp.where(odd, other_skel, own_skel),
        jnp.where(odd, own_skel, other_skel),
        par_piv,
    )
    far_m, far_r, far_s = from_partner((par_m, par_r, par_s), "leaf", 1)
    upper = leaf // 2 % 2 == 1
    top_m, top_r = merge_top(
        jnp.where(upper, far_m, par_m),
        jnp.where(upper, par_m, far_m),
        jnp.where(upper, far_r, par_r),
        jnp.where(upper, par_r, far_r),
        jnp.where(upper, far_s, par_s),
        jnp.where(upper, par_s, far_s),
        top_piv,
        inverse,
    )
    top_share = lax.dynamic_slice_in_dim(top_m, column * slab, slab, 0)
    return (share[None], top_share[None], top_r[None])


def solution(mesh):
    return jax.shard_map(
        local,
        mesh=mesh,
        in_specs=(
            P(None, ("leaf", "col")),
            P(("leaf", "col")),
            P(("leaf", "col")),
            P(),
            P(),
            P("leaf", None),
            P(),
            P(),
        ),
        out_specs=(P("leaf", "col", None), P("leaf", "col", None), P("leaf", None)),
        check_vma=False,
    )
```

profile of v0, /device:TPU:1, one launch (start us, length us, event | category | flops | bytes accessed | tf_op | source)
XLA Modules:
  0.0 268.7 jit_solution(8375681655461002481)
XLA Ops:
  7.9 7.5 %sort.17 = (s32[8192]{0:T(1024)}, s32[8192]{0:T(1024)S(1)}) sort(s32[8192]{0:T(1024)} %param.20, s32[8192]{0:T(1024)S(1)} %iota.25), dimensions={0}, to_apply=%region_0.0 | sort | flops 106496 | bytes 131072 | tf_op jit(solution)/shard_map/jit(argsort)/sort | solution.py:85
  15.5 1.2 pad_maximum_fusion
  16.7 53.2 %while.29 = (s32[]{:T(128)}, bf16[8,49,1024]{2,1,0:T(8,128)(2,1)S(1)}, s32[8]{0:T(128)S(1)}, s32[8192]{0:T(1024)S(1)}, bf16[49,8192]{1,0:T(8,128)(2,1)S(1)}, /*index=5*/s32[]{:T(128)}, s32[1]{0:T(128)}, s32[]{:T(128)}, s32[]{:T(128)}) while((s32[]{:T(128)}, bf16[8,49,1024]{2,1,0:T(8,128)(2,1)S(1)}, s32[8]{0:T(128)S(1)}, ...), condition=%wide.region_2.3_spmd.clone, body=%wide.region_1.2_spmd.clone.sunk | while | flops 830522368 | bytes 1044647 | solution.py:73
  18.1 5.4 %fusion.58 = bf16[8,49,1024]{2,1,0:T(8,128)(2,1)S(1)} fusion(bf16[8,49,1024]{2,1,0:T(8,128)(2,1)S(1)} %get-tuple-element.394, s32[]{:T(128)S(6)} %copy.37, bf16[49,8192]{1,0:T(8,128)(2,1)S(1)} %get-tuple-element.406, s32[1024]{0:T(1024)S(1)} %dynamic_slice.64), kind=kOutput, calls=%fused_computation.13.clone.1 | convolution fusion | flops 830522368 | bytes 1036292 | tf_op jit(solution)/shard_map/while/body/eval_jaxpr/dot_general | solution.py:71
  24.8 5.4 %fusion.58 = bf16[8,49,1024]{2,1,0:T(8,128)(2,1)S(1)} fusion(bf16[8,49,1024]{2,1,0:T(8,128)(2,1)S(1)} %get-tuple-element.394, s32[]{:T(128)S(6)} %copy.37, bf16[49,8192]{1,0:T(8,128)(2,1)S(1)} %get-tuple-element.406, s32[1024]{0:T(1024)S(1)} %dynamic_slice.64), kind=kOutput, calls=%fused_computation.13.clone.1 | convolution fusion | flops 830522368 | bytes 1036292 | tf_op jit(solution)/shard_map/while/body/eval_jaxpr/dot_general | solution.py:71
  31.4 5.4 %fusion.58 = bf16[8,49,1024]{2,1,0:T(8,128)(2,1)S(1)} fusion(bf16[8,49,1024]{2,1,0:T(8,128)(2,1)S(1)} %get-tuple-element.394, s32[]{:T(128)S(6)} %copy.37, bf16[49,8192]{1,0:T(8,128)(2,1)S(1)} %get-tuple-element.406, s32[1024]{0:T(1024)S(1)} %dynamic_slice.64), kind=kOutput, calls=%fused_computation.13.clone.1 | convolution fusion | flops 830522368 | bytes 1036292 | tf_op jit(solution)/shard_map/while/body/eval_jaxpr/dot_general | solution.py:71
  38.0 5.4 %fusion.58 = bf16[8,49,1024]{2,1,0:T(8,128)(2,1)S(1)} fusion(bf16[8,49,1024]{2,1,0:T(8,128)(2,1)S(1)} %get-tuple-element.394, s32[]{:T(128)S(6)} %copy.37, bf16[49,8192]{1,0:T(8,128)(2,1)S(1)} %get-tuple-element.406, s32[1024]{0:T(1024)S(1)} %dynamic_slice.64), kind=kOutput, calls=%fused_computation.13.clone.1 | convolution fusion | flops 830522368 | bytes 1036292 | tf_op jit(solution)/shard_map/while/body/eval_jaxpr/dot_general | solution.py:71
  44.7 5.4 %fusion.58 = bf16[8,49,1024]{2,1,0:T(8,128)(2,1)S(1)} fusion(bf16[8,49,1024]{2,1,0:T(8,128)(2,1)S(1)} %get-tuple-element.394, s32[]{:T(128)S(6)} %copy.37, bf16[49,8192]{1,0:T(8,128)(2,1)S(1)} %get-tuple-element.406, s32[1024]{0:T(1024)S(1)} %dynamic_slice.64), kind=kOutput, calls=%fused_computation.13.clone.1 | convolution fusion | flops 830522368 | bytes 1036292 | tf_op jit(solution)/shard_map/while/body/eval_jaxpr/dot_general | solution.py:71
  51.3 5.4 %fusion.58 = bf16[8,49,1024]{2,1,0:T(8,128)(2,1)S(1)} fusion(bf16[8,49,1024]{2,1,0:T(8,128)(2,1)S(1)} %get-tuple-element.394, s32[]{:T(128)S(6)} %copy.37, bf16[49,8192]{1,0:T(8,128)(2,1)S(1)} %get-tuple-element.406, s32[1024]{0:T(1024)S(1)} %dynamic_slice.64), kind=kOutput, calls=%fused_computation.13.clone.1 | convolution fusion | flops 830522368 | bytes 1036292 | tf_op jit(solution)/shard_map/while/body/eval_jaxpr/dot_general | solution.py:71
  57.9 5.4 %fusion.58 = bf16[8,49,1024]{2,1,0:T(8,128)(2,1)S(1)} fusion(bf16[8,49,1024]{2,1,0:T(8,128)(2,1)S(1)} %get-tuple-element.394, s32[]{:T(128)S(6)} %copy.37, bf16[49,8192]{1,0:T(8,128)(2,1)S(1)} %get-tuple-element.406, s32[1024]{0:T(1024)S(1)} %dynamic_slice.64), kind=kOutput, calls=%fused_computation.13.clone.1 | convolution fusion | flops 830522368 | bytes 1036292 | tf_op jit(solution)/shard_map/while/body/eval_jaxpr/dot_general | solution.py:71
  64.6 5.4 %fusion.58 = bf16[8,49,1024]{2,1,0:T(8,128)(2,1)S(1)} fusion(bf16[8,49,1024]{2,1,0:T(8,128)(2,1)S(1)} %get-tuple-element.394, s32[]{:T(128)S(6)} %copy.37, bf16[49,8192]{1,0:T(8,128)(2,1)S(1)} %get-tuple-element.406, s32[1024]{0:T(1024)S(1)} %dynamic_slice.64), kind=kOutput, calls=%fused_computation.13.clone.1 | convolution fusion | flops 830522368 | bytes 1036292 | tf_op jit(solution)/shard_map/while/body/eval_jaxpr/dot_general | solution.py:71
  70.4 1.0 all_to_all.6
  71.4 1.1 copy.33
  72.5 2.4 reshape.155
  75.0 11.5 %all-to-all-start = ((bf16[128,2,1568]{2,1,0:T(2,128)(2,1)}), bf16[128,2,1568]{2,1,0:T(2,128)(2,1)S(1)}, u32[]{:S(2)}, u32[]{:S(2)}) async-start(bf16[128,2,1568]{2,1,0:T(2,128)(2,1)} %reshape.155), calls=%async_computation | async-start | bytes 1703936 | tf_op jit(solution)/shard_map/all_to_all | solution.py:89
  91.0 11.9 %all-to-all-done = bf16[128,2,1568]{2,1,0:T(2,128)(2,1)S(1)} async-done(((bf16[128,2,1568]{2,1,0:T(2,128)(2,1)}), bf16[128,2,1568]{2,1,0:T(2,128)(2,1)S(1)}, u32[]{:S(2)}, u32[]{:S(2)}) %all-to-all-start) | async-done | bytes 802848 | tf_op jit(solution)/shard_map/all_to_all | solution.py:89
  102.8 1.4 reshape.156
  104.3 1.6 copy.25
  105.9 2.4 slice.17
  108.3 1.6 fusion.30
  109.9 25.5 %psum.21 = bf16[48,256]{1,0:T(8,128)(2,1)S(1)} all-reduce(bf16[48,256]{1,0:T(8,128)(2,1)S(1)} %fusion.30), channel_id=1, replica_groups=mesh['leaf'=16,'col'=8] {'col'}, use_global_device_ids=true, to_apply=%region_3.4 | all-reduce | flops 12288 | bytes 49152 | tf_op jit(solution)/shard_map/psum | solution.py:96
  135.4 7.2 %collective-permute-start = (bf16[48,256]{1,0:T(8,128)(2,1)S(1)}, bf16[48,256]{1,0:T(8,128)(2,1)S(1)}, u32[]{:S(2)}, u32[]{:S(2)}) collective-permute-start(bf16[48,256]{1,0:T(8,128)(2,1)S(1)} %psum.21), channel_id=1, source_target_pairs={{0,8},{8,0},{16,24},{24,16},{32,40},{40,32},{48,56},{56,48},{64,72... | collective-permute-start | bytes 73736 | tf_op jit(solution)/shard_map/ppermute | solution.py:12
  144.1 28.8 %while.30 = (s32[]{:T(128)}, f32[256,256]{1,0:T(8,128)S(1)}, f32[256,256]{1,0:T(8,128)S(1)}, f32[256]{0:T(256)}, bf16[48,8192]{1,0:T(8,128)(2,1)S(1)}, /*index=5...) while((s32[]{:T(128)}, f32[256,256]{1,0:T(8,128)S(1)}, ...), condition=%wide.region_8.9_spmd.clone, body=%wide.region_4.8_spmd.clone.sunk | while | flops 2298310656 | bytes 15186623 | solution.py:42
  145.0 5.6 %fusion.67 = bf16[4096,256]{1,0:T(8,128)(2,1)S(1)} fusion(f32[256]{0:T(256)} %get-tuple-element.382, f32[4096]{0:T(1024)S(1)} %multiply_reduce_fusion.8, f32[48]{0:T(128)S(1)} %get-tuple-element.442, bf16[48,8192]{1,0:T(8,128)(2,1)S(1)} %get-tuple-element.441, s32[]{:T(128)S(6)} %select_n.276, f32[48,256]{1,0:T(8,128)S(1)} %get-tuple-element.443), kind=kOutput, calls=%fused_computation.25.clone.1 | convolution fusion | flops 610676736 | bytes 2557956 | tf_op jit(solution)/shard_map/while/body/eval_jaxpr/dot_general | solution.py:18
  150.6 0.8 convolution_add_fusion.4
  151.5 4.9 %fusion.68 = bf16[4096,256]{1,0:T(8,128)(2,1)S(1)} fusion(f32[256]{0:T(256)S(1)} %copy-done.6, f32[4096]{0:T(1024)S(1)} %multiply_reduce_fusion.8, f32[48]{0:T(128)S(1)} %get-tuple-element.442, bf16[48,8192]{1,0:T(8,128)(2,1)S(1)} %get-tuple-element.441, s32[]{:T(128)S(6)} %select_n.276, f32[48,256]{1,0:T(8,128)S(1)} %get-tuple-element.444), kind=kOutput, calls=%fused_computation.24.clone.1 | convolution fusion | flops 610676736 | bytes 2557956 | tf_op jit(solution)/shard_map/while/body/eval_jaxpr/dot_general | solution.py:18
  156.4 0.8 convolution_add_fusion.5
  159.4 5.6 %fusion.67 = bf16[4096,256]{1,0:T(8,128)(2,1)S(1)} fusion(f32[256]{0:T(256)} %get-tuple-element.382, f32[4096]{0:T(1024)S(1)} %multiply_reduce_fusion.8, f32[48]{0:T(128)S(1)} %get-tuple-element.442, bf16[48,8192]{1,0:T(8,128)(2,1)S(1)} %get-tuple-element.441, s32[]{:T(128)S(6)} %select_n.276, f32[48,256]{1,0:T(8,128)S(1)} %get-tuple-element.443), kind=kOutput, calls=%fused_computation.25.clone.1 | convolution fusion | flops 610676736 | bytes 2557956 | tf_op jit(solution)/shard_map/while/body/eval_jaxpr/dot_general | solution.py:18
  165.0 0.8 convolution_add_fusion.4
  165.8 4.9 %fusion.68 = bf16[4096,256]{1,0:T(8,128)(2,1)S(1)} fusion(f32[256]{0:T(256)S(1)} %copy-done.6, f32[4096]{0:T(1024)S(1)} %multiply_reduce_fusion.8, f32[48]{0:T(128)S(1)} %get-tuple-element.442, bf16[48,8192]{1,0:T(8,128)(2,1)S(1)} %get-tuple-element.441, s32[]{:T(128)S(6)} %select_n.276, f32[48,256]{1,0:T(8,128)S(1)} %get-tuple-element.444), kind=kOutput, calls=%fused_computation.24.clone.1 | convolution fusion | flops 610676736 | bytes 2557956 | tf_op jit(solution)/shard_map/while/body/eval_jaxpr/dot_general | solution.py:18
  170.8 0.8 convolution_add_fusion.5
  172.9 0.9 pad_maximum_fusion.1
  173.8 12.8 %psum.23 = f32[256]{0:T(256)S(1)} all-reduce(f32[256]{0:T(256)} %get-tuple-element.199), channel_id=1, replica_groups=mesh['leaf'=16,'col'=8] {'col'}, use_global_device_ids=true, to_apply=%region_12.15 | all-reduce | flops 256 | bytes 2048 | tf_op jit(solution)/shard_map/psum | solution.py:104
  186.6 3.7 %collective-permute-start.4 = (f32[256]{0:T(256)S(1)}, f32[256]{0:T(256)S(1)}, u32[]{:S(2)}, u32[]{:S(2)}) collective-permute-start(f32[256]{0:T(256)S(1)} %broadcast_multiply_fusion), channel_id=1, source_target_pairs={{0,8},{8,0},{16,24},{24,16},{32,40},{40,32},{48,56},{56,48},{64,72... | collective-permute-start | bytes 3080 | tf_op jit(solution)/shard_map/ppermute | solution.py:12
  191.1 0.9 gather_fusion
  192.1 2.2 gather_fusion.5
  194.8 1.2 collective-permute-start.3
  196.0 1.0 collective-permute-done.5
  197.1 1.9 gather_fusion.6
  199.0 40.0 %all-reduce.2.cloned.1.call-done = f32[256,512]{1,0:T(8,128)} async-done(((f32[256,512]{1,0:T(8,128)}), f32[256,512]{1,0:T(8,128)}) %all-reduce.2.cloned.1.call-update) | async-done | bytes 524304 | tf_op jit(solution)/shard_map/psum | solution.py:104
  239.0 1.2 select_add_fusion.1
  240.2 6.1 %collective-permute-start.1 = (f32[256,512]{1,0:T(8,128)S(1)}, f32[256,512]{1,0:T(8,128)S(1)}, u32[]{:S(2)}, u32[]{:S(2)}) collective-permute-start(f32[256,512]{1,0:T(8,128)S(1)} %select_add_fusion.1), channel_id=1, source_target_pairs={{0,8},{8,0},{16,24},{24,16},{32,40},{40,32},{48,56},{56,48},{64,72... | collective-permute-start | bytes 1572872 | tf_op jit(solution)/shard_map/ppermute | solution.py:12
  248.1 1.0 gather_fusion.1
  249.4 1.0 gather_fusion.2
  250.5 1.3 collective-permute-start.2
  252.6 5.5 %collective-permute-done.2 = f32[256,256]{0,1:T(8,128)S(1)} collective-permute-done((f32[256,256]{0,1:T(8,128)S(1)}, f32[256,256]{0,1:T(8,128)S(1)}, u32[]{:S(2)}, u32[]{:S(2)}) %collective-permute-start.2) | collective-permute-done | bytes 262176 | tf_op jit(solution)/shard_map/ppermute | solution.py:12
  258.7 1.0 gather_fusion.3
  260.0 1.0 gather_fusion.4
  (126 shorter events, 21.8 us)
Async XLA Ops:
  7.2 81.3 %copy-start = (s32[4,256]{1,0:T(4,128)S(1)}, s32[4,256]{1,0:T(4,128)}, u32[]{:S(2)}) copy-start(s32[4,256]{1,0:T(4,128)} %param.25) | copy-start | bytes 12292
  72.5 18.4 %copy-start.14 = (f32[48]{0:T(128)S(1)}, f32[48]{0:T(128)}, u32[]{:S(2)}) copy-start(f32[48]{0:T(128)} %param.21) | copy-start | bytes 580
  72.5 18.4 %copy-start.13 = (s32[1,256]{1,0:T(1,128)S(1)}, s32[1,256]{1,0:T(1,128)}, u32[]{:S(2)}) copy-start(s32[1,256]{1,0:T(1,128)} %param.23) | copy-start | bytes 3076
  75.0 27.8 %all-to-all-start = ((bf16[128,2,1568]{2,1,0:T(2,128)(2,1)}), bf16[128,2,1568]{2,1,0:T(2,128)(2,1)S(1)}, u32[]{:S(2)}, u32[]{:S(2)}) async-start(bf16[128,2,1568]{2,1,0:T(2,128)(2,1)} %reshape.155), calls=%async_computation | async-start | bytes 1703936 | tf_op jit(solution)/shard_map/all_to_all | solution.py:89
  86.5 152.5 %all-reduce.2.cloned.1.call-start = ((), (), s32[]{:S(2)}) async-start(), calls=%async_computation.1 | async-start | bytes 1048576 | tf_op jit(solution)/shard_map/psum | solution.py:104
  87.3 0.6 copy-start.9
  88.5 0.6 copy-start.11
  135.4 8.1 %collective-permute-start = (bf16[48,256]{1,0:T(8,128)(2,1)S(1)}, bf16[48,256]{1,0:T(8,128)(2,1)S(1)}, u32[]{:S(2)}, u32[]{:S(2)}) collective-permute-start(bf16[48,256]{1,0:T(8,128)(2,1)S(1)} %psum.21), channel_id=1, source_target_pairs={{0,8},{8,0},{16,24},{24,16},{32,40},{40,32},{48,56},{56,48},{64,72... | collective-permute-start | bytes 73736 | tf_op jit(solution)/shard_map/ppermute | solution.py:12
  143.5 0.6 copy-start.3
  150.6 0.8 copy-start.6
  156.4 0.9 copy-start.2
  157.3 0.7 copy-start.4
  157.9 0.6 copy-start.5
  165.0 0.8 copy-start.6
  170.8 0.9 copy-start.2
  171.6 0.7 copy-start.4
  172.3 0.6 copy-start.5
  172.9 19.2 %copy-start.7 = (s32[1024]{0:T(1024)S(1)}, s32[1024]{0:T(1024)}, u32[]{:S(2)}) copy-start(s32[1024]{0:T(1024)} %pad_clamp_fusion.2) | copy-start | bytes 12292
  172.9 21.4 %copy-start.10 = (s32[1,256]{1,0:T(1,128)S(1)}, s32[1,256]{1,0:T(1,128)}, u32[]{:S(2)}) copy-start(s32[1,256]{1,0:T(1,128)} %copy-done.9) | copy-start | bytes 3076
  172.9 24.2 %copy-start.8 = (s32[1024]{0:T(1024)S(1)}, s32[1024]{0:T(1024)}, u32[]{:S(2)}) copy-start(s32[1024]{0:T(1024)} %pad_clamp_fusion) | copy-start | bytes 12292
  186.6 5.5 %collective-permute-start.4 = (f32[256]{0:T(256)S(1)}, f32[256]{0:T(256)S(1)}, u32[]{:S(2)}, u32[]{:S(2)}) collective-permute-start(f32[256]{0:T(256)S(1)} %broadcast_multiply_fusion), channel_id=1, source_target_pairs={{0,8},{8,0},{16,24},{24,16},{32,40},{40,32},{48,56},{56,48},{64,72... | collective-permute-start | bytes 3080 | tf_op jit(solution)/shard_map/ppermute | solution.py:12
  191.0 55.3 %copy-start.12 = (s32[1,256]{1,0:T(1,128)S(1)}, s32[1,256]{1,0:T(1,128)}, u32[]{:S(2)}) copy-start(s32[1,256]{1,0:T(1,128)} %copy-done.11) | copy-start | bytes 3076
  194.3 2.7 %collective-permute-start.5 = (f32[256]{0:T(256)S(1)}, f32[256]{0:T(256)S(1)}, u32[]{:S(2)}, u32[]{:S(2)}) collective-permute-start(f32[256]{0:T(256)S(1)} %get-tuple-element.276), channel_id=1, source_target_pairs={{0,16},{8,24},{16,0},{24,8},{32,48},{40,56},{48,32},{56,40},{64,80... | collective-permute-start | bytes 3080 | tf_op jit(solution)/shard_map/ppermute | solution.py:12
  194.8 52.0 %collective-permute-start.3 = (f32[48,256]{0,1:T(8,128)S(1)}, f32[48,256]{0,1:T(8,128)S(1)}, u32[]{:S(2)}, u32[]{:S(2)}) collective-permute-start(f32[48,256]{0,1:T(8,128)S(1)} %select_bitcast_fusion.2), channel_id=1, source_target_pairs={{0,16},{8,24},{16,0},{24,8},{32,48},{40,56},{48,32},{56,40},{64,80... | collective-permute-start | bytes 147464 | tf_op jit(solution)/shard_map/ppermute | solution.py:12
  239.0 8.8 %copy-start.1 = (f32[256,512]{1,0:T(8,128)S(1)}, f32[256,512]{1,0:T(8,128)}, u32[]{:S(2)}) copy-start(f32[256,512]{1,0:T(8,128)} %all-reduce.2.cloned.1.call-done) | copy-start | bytes 1572868
  240.2 7.6 %collective-permute-start.1 = (f32[256,512]{1,0:T(8,128)S(1)}, f32[256,512]{1,0:T(8,128)S(1)}, u32[]{:S(2)}, u32[]{:S(2)}) collective-permute-start(f32[256,512]{1,0:T(8,128)S(1)} %select_add_fusion.1), channel_id=1, source_target_pairs={{0,8},{8,0},{16,24},{24,16},{32,40},{40,32},{48,56},{56,48},{64,72... | collective-permute-start | bytes 1572872 | tf_op jit(solution)/shard_map/ppermute | solution.py:12
  250.5 7.6 %collective-permute-start.2 = (f32[256,256]{0,1:T(8,128)S(1)}, f32[256,256]{0,1:T(8,128)S(1)}, u32[]{:S(2)}, u32[]{:S(2)}) collective-permute-start(f32[256,256]{0,1:T(8,128)S(1)} %select_bitcast_fusion.1), channel_id=1, source_target_pairs={{0,16},{8,24},{16,0},{24,8},{32,48},{40,56},{48,32},{56,40},{64,80... | collective-permute-start | bytes 786440 | tf_op jit(solution)/shard_map/ppermute | solution.py:12
Sparse Core Ops, SparseCore 0:
  173.9 65.0 all-reduce.1
where the time goes:
time: 269 us
  matrix products  69.9 us (26%)
  waiting for transfers between devices  58.6 us (22%)
  blocking collectives  38.3 us (14%)
  local copies, waits for them, and re-layouts  31.7 us (12%)
  starting transfers between devices  31.4 us (12%)
  other arithmetic  17.8 us (7%)
  between operations  15.1 us (6%)
  loops' own time  5.87 us (2%)
    dot_general x8, matrix products, block(): jnp.dot(joined, selector, preferred_element_type=jnp.float32)  42.8 us
    psum x1, waiting for transfers between devices, local(): stacked, rhs = lax.psum((stacked, rhs), 'col')  40 us
    psum x1, blocking collectives, local(): own_skel = lax.psum(picked.astype(jnp.bfloat16), 'col').astype(jnp.float32)  25.5 us
    dot_general x5, matrix products, kernel(): lax.dot_general(left, right, (((0,), (0,)), ((), ())), precision=lax.Prec...  21.5 us
    ppermute x6, starting transfers between devices, from_partner(): lax.ppermute(shard, axis, [(i, i ^ 1 << apart) for i in range(lax.axis_si...  19.8 us
    psum x1, blocking collectives, local(): stacked, rhs = lax.psum((stacked, rhs), 'col')  12.8 us
    all_to_all x1, waiting for transfers between devices, local(): lax.all_to_all(arranged, ('leaf', 'col'), split_axis=1, concat_axis=1, ti...  11.9 us
    all_to_all x1, starting transfers between devices, local(): lax.all_to_all(arranged, ('leaf', 'col'), split_axis=1, concat_axis=1, ti...  11.5 us
  transfers between devices with their start and end apart: 8, of which 5 were waited for; matrix products, arithmetic and copies ran while one was open for 5% of the time, Pallas kernels for 0%

commit v1 on v0

v1 whole, which is shorter than its diff:
```python
import functools
import math

import jax
import jax.numpy as jnp
from jax import lax
from jax.experimental import pallas as pl
from jax.experimental.pallas import tpu as pltpu
from jax.sharding import PartitionSpec as P

F = 48
RANK = 256
ROWS = 8192
LEAVES = 16
COLS = 8
OWNERS = 128
PACKET = 64
PER = ROWS // LEAVES
CHUNK = 256
CHUNKS = ROWS // CHUNK
WINDOW = 40
REGION = PER + WINDOW
WIDE = 64
SLAB = RANK // COLS
NODE = ROWS * COLS
LOG2E = math.log2(math.e)
BF = jnp.bfloat16
F32 = jnp.float32
NT = (((1,), (1,)), ((), ()))
MESH = pl.DeviceIdType.MESH


def dma(count):
    return [pltpu.SemaphoreType.DMA((count,))] * 2


def params(number=None, limit=24):
    if number is None:
        return pltpu.CompilerParams(vmem_limit_bytes=limit * 2**20)
    return pltpu.CompilerParams(
        collective_id=number, has_side_effects=True, vmem_limit_bytes=limit * 2**20
    )


ANYWHERE = pl.BlockSpec(memory_space=pl.ANY)
VMEM = pl.BlockSpec(memory_space=pltpu.VMEM)


def iota(shape, axis):
    return lax.broadcasted_iota(jnp.int32, shape, axis)


def dot(a, b):
    return jnp.dot(a, b, preferred_element_type=F32)


def dot_nt(a, b):
    return lax.dot_general(a, b, NT, preferred_element_type=F32)


def row_pair(two):
    return jnp.concatenate([two[0:1], two[1:2]], 1)


def pack_kernel(
    feat_hbm, target, owner, out_feat, out_aux,
    feat, goals, rows, ybuf, zbuf, table, scal, sem, feat_sem,
):
    bring = pltpu.make_async_copy(feat_hbm, feat, feat_sem)
    bring.start()
    goals[...] = target[...].astype(F32)
    before = (iota((CHUNK, CHUNK), 0) < iota((CHUNK, CHUNK), 1)).astype(F32).astype(BF)
    weights = jnp.concatenate([before, jnp.ones((CHUNK, 128), BF)], 1)
    lane = iota((LEAVES, 128), 1)

    def ranks(t, carry):
        seen, seen_leaf, most = carry
        own = row_pair(owner[pl.ds(2 * t, 2), :])
        leaf = own // 8
        is_own = iota((OWNERS, CHUNK), 0) == own
        is_leaf = iota((LEAVES, CHUNK), 0) == leaf
        is_after = iota((LEAVES, CHUNK), 0) > leaf
        marks = jnp.concatenate(
            [m.astype(F32).astype(BF) for m in (is_own, is_leaf, is_after)], 0
        )
        sums = dot(marks, weights)
        counts = sums[:OWNERS, CHUNK:]
        leaf_counts = sums[OWNERS : OWNERS + LEAVES, CHUNK:]
        base = sums[OWNERS + LEAVES :, CHUNK:]
        prior = sums[:OWNERS, :CHUNK] + jnp.concatenate([seen, seen], 1)
        rank = jnp.sum(jnp.where(is_own, prior, 0.0), 0, keepdims=True)
        place = sums[OWNERS : OWNERS + LEAVES, :CHUNK] + jnp.concatenate([base, base], 1)
        place = jnp.sum(jnp.where(is_leaf, place, 0.0), 0, keepdims=True)
        tag = (own % 8).astype(F32) * PACKET + rank - (PER // 2)
        rows[t, 0:1, :] = place
        rows[t, 1:2, :] = row_pair(goals[pl.ds(2 * t, 2), :])
        rows[t, 2:3, :] = tag
        here = lane == t
        table[0:LEAVES, :] = jnp.where(here, seen_leaf.astype(jnp.int32), table[0:LEAVES, :])
        table[LEAVES : 2 * LEAVES, :] = jnp.where(
            here, base.astype(jnp.int32), table[LEAVES : 2 * LEAVES, :]
        )
        return seen + counts, seen_leaf + leaf_counts, jnp.maximum(most, leaf_counts)

    table[0:LEAVES, :] = jnp.full((LEAVES, 128), PER, jnp.int32)
    zero = jnp.zeros((LEAVES, 128), F32)
    _, _, most = lax.fori_loop(
        0, CHUNKS, ranks, (jnp.zeros((OWNERS, 128), F32), zero, zero), unroll=8
    )
    most = jnp.broadcast_to(jnp.max(most, 0, keepdims=True), (8, 128))
    table[2 * LEAVES :, :] = most.astype(jnp.int32)
    move = pltpu.make_async_copy(table, scal, sem)
    move.start()
    bring.wait()

    def sort(t, _):
        start = pl.multiple_of(t * CHUNK, CHUNK)
        row = iota((16, CHUNK), 0)
        place, goal, tag = rows[t, 0:1, :], rows[t, 1:2, :], rows[t, 2:3, :]
        extra = jnp.where(row == 0, goal, jnp.where(row == 1, tag, 0.0)).astype(BF)
        joined = jnp.concatenate([feat[:, pl.ds(start, CHUNK)], extra], 0)
        chosen = (iota((CHUNK, CHUNK), 0) == place.astype(jnp.int32)).astype(F32).astype(BF)
        ybuf[pl.ds(start, CHUNK), :] = dot_nt(chosen, joined)
        return 0

    lax.fori_loop(0, CHUNKS, sort, 0, unroll=8)
    move.wait()
    widest = scal[2 * LEAVES, 0]

    @pl.when(widest <= WINDOW)
    def quick():
        def merge(t, _):
            for i in range(LEAVES):
                source = t * CHUNK + scal[LEAVES + i, t]
                goal = i * REGION + scal[i, t]
                zbuf[pl.ds(goal, WINDOW), :] = ybuf[pl.ds(source, WINDOW), :]
            return 0

        lax.fori_loop(0, CHUNKS, merge, 0, unroll=2)

    @pl.when(widest > WINDOW)
    def slow():
        def merge(index, _):
            t = index // LEAVES
            i = index % LEAVES
            source = t * CHUNK + scal[LEAVES + i, t]
            first = scal[i, t]
            count = scal[i, t + 1] - first

            def part(k, _):
                rows = ybuf[pl.ds(source + 8 * k, 8), :]
                zbuf[pl.ds(i * REGION + first + 8 * k, 8), :] = rows
                return 0

            lax.fori_loop(0, (count + 7) // 8, part, 0)
            return 0

        lax.fori_loop(0, CHUNKS * LEAVES, merge, 0)

    eye = (iota((WIDE, WIDE), 0) == iota((WIDE, WIDE), 1)).astype(F32).astype(BF)
    for i in range(LEAVES):
        turned = dot_nt(eye, zbuf[i * REGION : i * REGION + PER, :].astype(BF))
        out_feat[i] = turned[:F].astype(BF)
        out_aux[i] = jnp.concatenate(
            [turned[F + r : F + r + 1, 128 * k : 128 * k + 128] for r in range(2) for k in range(4)], 0
        )


def in_hbm(*arrays):
    return [pltpu.with_memory_space_constraint(a, pltpu.HBM) for a in arrays]


def pack(features, targets, owner):
    return pl.pallas_call(
        pack_kernel,
        out_shape=(pltpu.VMEM((LEAVES, F, PER), BF), pltpu.VMEM((LEAVES, 8, 128), F32)),
        in_specs=[ANYWHERE, VMEM, VMEM],
        out_specs=[VMEM] * 2,
        scratch_shapes=[
            pltpu.VMEM((F, ROWS), BF),
            pltpu.VMEM((ROWS // 128, 128), F32),
            pltpu.VMEM((CHUNKS, 8, CHUNK), F32),
            pltpu.VMEM((ROWS + WINDOW, WIDE), F32),
            pltpu.VMEM((LEAVES * REGION, WIDE), F32),
            pltpu.VMEM((40, 128), jnp.int32),
            pltpu.SMEM((40, 128), jnp.int32),
            pltpu.SemaphoreType.DMA,
            pltpu.SemaphoreType.DMA,
        ],
        compiler_params=params(),
        name="pack",
    )(*in_hbm(features, targets, owner))


def split3(x):
    high = x.astype(BF)
    rest = x - high.astype(F32)
    mid = rest.astype(BF)
    return high, mid, (rest - mid.astype(F32)).astype(BF)


def stack16(parts, width):
    row = iota((16, width), 0)
    block = jnp.zeros((16, width), F32)
    for k, part in enumerate(parts):
        block = jnp.where(row == k, part if isinstance(part, float) else part.astype(F32), block)
    return block.astype(BF)


def half_norm(points, scale):
    return jnp.sum(points * points * (0.5 * scale), 0, keepdims=True)


def point_side(points, scale):
    high, mid, low = split3(-half_norm(points, scale))
    return stack16([high, mid, low, 1.0, 1.0, 1.0], points.shape[1])


def skel_side(skel, scale):
    width = skel.shape[1]
    high, mid, low = split3(skel * scale)
    extra = stack16([1.0, 1.0, 1.0, *split3(-half_norm(skel, scale))], width)
    parts = [p.astype(F32) for p in (high, mid, low, extra)]
    fill = jnp.zeros((256 - 3 * F - 16, width), F32)
    return jnp.concatenate([*parts, fill], 0).T.astype(BF)


def select_row(table, row):
    hit = iota(table.shape, 0) == row
    return jnp.sum(jnp.where(hit, table.astype(F32), 0.0), 0, keepdims=True)


def to_column(row):
    return jnp.broadcast_to(row, (128, row.shape[1])).T


def across(column, width):
    return jnp.concatenate([column] * (width // 128), 1)


def place_of(leaf, col):
    return dict(device_id=(leaf, col), device_id_type=MESH)


def mate(k):
    leaf, col = lax.axis_index("leaf"), lax.axis_index("col")
    to = (leaf + k) % LEAVES
    cross = (to // 8 + leaf // 8) % 2
    return place_of(to, col + cross * (1 - 2 * (col % 2)))


def beside(k):
    leaf, col = lax.axis_index("leaf"), lax.axis_index("col")
    return place_of(leaf, (col + k) % COLS)


def cousin(k):
    leaf, col = lax.axis_index("leaf"), lax.axis_index("col")
    return place_of(leaf - leaf % 4 + (leaf + k) % 4, col)


def greet(peers):
    barrier = pltpu.get_barrier_semaphore()
    for peer in peers:
        pl.semaphore_signal(barrier, inc=1, **peer)
    return lambda: pl.semaphore_wait(barrier, len(peers))


def remote(src, dst, sems, k, peer):
    return pltpu.make_async_remote_copy(src, dst, sems[0].at[k], sems[1].at[k], **peer)


def top_index(parent, top, group):
    top_row = select_row(top[...], group)
    below = jnp.concatenate([select_row(parent[...], 2 * group + r) for r in range(2)], 1)
    number = iota((RANK, 2 * RANK), 1)
    below = below + jnp.where(iota((1, 2 * RANK), 1) >= RANK, 2.0 * RANK, 0.0)
    hit = across(to_column(top_row), 2 * RANK) == number.astype(F32)
    index = jnp.sum(jnp.where(hit, below, 0.0), 1, keepdims=True)
    return jnp.broadcast_to(index, (RANK, 128))


def exchange_kernel(
    feat, aux, ridge, pivots_hbm, scales_hbm, parent_hbm, top_hbm, out_share, out_top, out_rhs,
    pivots, scales, parent, top, spare, rx, ra, hot, side, sk, mine, sk4, left, basis, acc,
    rows, columns, fours, index, tops, ps, pr, rs, rr, t4, r4,
    s_f, r_f, s_a, r_a, s_k, r_k, s_4, r_4, s_p, r_p, s_r, r_r, s_t, r_t, s_q, r_q, local,
):
    leaf = lax.axis_index("leaf")
    col = lax.axis_index("col")
    quarter = leaf % 4
    sibling = quarter + 1 - 2 * (quarter % 2)
    ready = greet([mate(k) for k in range(1, LEAVES)] + [beside(k) for k in range(1, COLS)])
    smalls = [
        pltpu.make_async_copy(a, b, local.at[k])
        for k, (a, b) in enumerate(
            [(pivots_hbm, pivots), (scales_hbm, scales), (parent_hbm, parent), (top_hbm, top)]
        )
    ]
    for copy in smalls:
        copy.start()

    def send_feat(k):
        return remote(feat.at[(leaf + k) % LEAVES], rx.at[k], (s_f, r_f), k, mate(k))

    def send_aux(k):
        return remote(aux.at[(leaf + k) % LEAVES], ra.at[k], (s_a, r_a), k, mate(k))

    def begin_aux(k, _):
        send_aux(k).start()
        return 0

    def begin_feat(k, _):
        send_feat(k).start()
        return 0

    rx[0] = feat[leaf]
    ra[0] = aux[leaf]
    ready()
    lax.fori_loop(1, LEAVES, begin_aux, 0)
    lax.fori_loop(1, LEAVES, begin_feat, 0)

    for copy in smalls:
        copy.wait()
    spare[...] = jnp.ones((8, 128), F32)
    spare[0:1, 0:F] = scales[...]
    inverse = 1.0 / to_column(spare[0:1, :])[:F]
    scale = inverse * inverse * LOG2E
    scale2 = across(scale, RANK)
    scale4 = across(scale, PER)

    place = pivots[...]
    within = place % ROWS
    block = within // PACKET
    key = (block // COLS) * PER + (place // ROWS) * PACKET + within % PACKET
    holder = block % COLS
    crossed = (block // COLS) // 8 != leaf // 8
    holder = jnp.where(crossed, holder + 1 - 2 * (holder % 2), holder)
    key = jnp.where(holder == col, key, -PER)
    key = across(to_column(key.astype(F32)), PER)

    def mark(k):
        source = (leaf + LEAVES - k) % LEAVES
        tags = ra[k, 4:8, :]
        tag = jnp.concatenate([tags[r : r + 1] for r in range(4)], 1)
        wanted = tag + (PER // 2 + source * PER).astype(F32)
        hot[k] = (key == wanted).astype(F32).astype(BF)

    def mark_next(k, _):
        send_aux(k).wait_recv()
        mark(k)
        return 0

    mark(0)
    lax.fori_loop(1, LEAVES, mark_next, 0)

    index[...] = top_index(parent, top, leaf // 4)
    index2 = across(index[...], 2 * RANK)
    number = iota((RANK, 2 * RANK), 1)
    base = (quarter * RANK).astype(F32)
    other = (sibling * RANK).astype(F32)
    chosen = index2[:, :RANK] == iota((RANK, RANK), 1).astype(F32) + base
    rows[...] = chosen.astype(F32).astype(BF)
    lanes = number.astype(F32) + jnp.where(number < RANK, base, other - RANK)
    columns[...] = (index2 == lanes).astype(F32).astype(BF)
    chosen = across(index[...], 4 * RANK) == iota((RANK, 4 * RANK), 1).astype(F32)
    fours[...] = chosen.astype(F32).astype(BF)

    def pick(k, total):
        send_feat(k).wait_recv()
        return total + dot_nt(hot[k], rx[k])

    picked = lax.fori_loop(1, LEAVES, pick, dot_nt(hot[0], rx[0]))
    picked = jnp.concatenate([picked, jnp.zeros((RANK, 128 - F), F32)], 1).T[:F]
    sk[0] = picked.astype(BF)

    def send_skel(k):
        return remote(sk.at[0], sk.at[k], (s_k, r_k), k, beside(k))

    for k in range(1, COLS):
        send_skel(k).start()

    def norms(k, _):
        side[k] = point_side(rx[k].astype(F32), scale4)
        return 0

    lax.fori_loop(0, LEAVES, norms, 0, unroll=2)
    for k in range(1, COLS):
        send_skel(k).wait_recv()
        picked = picked + sk[k].astype(F32)
    mine[...] = picked.astype(BF)
    sk4[quarter] = picked.astype(BF)

    def send_four(k):
        return remote(mine, sk4.at[quarter], (s_4, r_4), k, cousin(k))

    for k in (1, 3, 2):
        send_four(k).start()
    left[0:RANK, :] = skel_side(picked, scale2)
    for k in range(1, 4):
        remote(mine, sk4.at[(quarter + 4 - k) % 4], (s_4, r_4), k, cousin(k)).wait_recv()
    left[RANK:, :] = skel_side(sk4[sibling].astype(F32), scale2)

    def block_of(k, slot):
        p = rx[k]
        fill = jnp.zeros((256 - 3 * F - 16, PER), BF)
        right = jnp.concatenate([p, p, p, side[k], fill], 0)
        power = dot(left[...], right)
        basis[slot, 0 : 2 * RANK, :] = jnp.exp2(jnp.minimum(power, 0.0)).astype(BF)
        value = jnp.concatenate([ra[k, r : r + 1, :] for r in range(4)], 1)
        basis[slot, 2 * RANK :, :] = jnp.broadcast_to(value, (16, PER)).astype(BF)

    def gram_of(slot):
        acc[...] += dot_nt(basis[slot], basis[slot, 0:RANK, :])

    acc[...] = jnp.zeros_like(acc)
    block_of(0, 0)

    def two(step, _):
        block_of(2 * step + 1, 1)
        gram_of(0)
        block_of(2 * step + 2, 0)
        gram_of(1)
        return 0

    lax.fori_loop(0, LEAVES // 2 - 1, two, 0)
    block_of(LEAVES - 1, 1)
    gram_of(0)
    gram_of(1)

    gram = acc[0:RANK, :].astype(BF)
    couple = acc[RANK : 2 * RANK, :].T.astype(BF)
    part = jnp.concatenate([gram, couple], 1)
    chosen = dot_nt(dot(rows[...], part).astype(BF), columns[...]).astype(BF)
    rhs = acc[2 * RANK : 2 * RANK + 1, :]
    rhs = jnp.sum(dot_nt(stack16(split3(rhs), RANK), rows[...]), 0, keepdims=True)
    for k in range(COLS):
        cut = slice(k * SLAB, (k + 1) * SLAB)
        ps[k, :, 0 : 2 * RANK] = part[cut]
        ps[k, :, 2 * RANK :] = chosen[cut]
    rs[...] = jnp.zeros_like(rs)
    rs[0:1, :] = rhs[:, :128]
    rs[1:2, :] = rhs[:, 128:]

    def send_part(k):
        return remote(ps.at[(col + k) % COLS], pr.at[k], (s_p, r_p), k, beside(k))

    def send_rhs(k):
        return remote(rs, rr.at[k], (s_r, r_r), k, beside(k))

    for k in range(1, COLS):
        send_part(k).start()
        send_rhs(k).start()

    whole = jnp.concatenate([sk4[k] for k in range(4)], 1)
    points = dot_nt(whole, fours[...])
    fill = jnp.zeros((256 - 3 * F - 16, RANK), BF)
    points_b = points.astype(BF)
    right = jnp.concatenate([points_b, points_b, points_b, point_side(points, scale2), fill], 0)
    value = jnp.exp2(jnp.minimum(dot(skel_side(points, scale2), right), 0.0))
    crossing = (across(index[...], RANK) >= 2.0 * RANK) != (index[...].T[0:1, :] >= 2.0 * RANK)
    square = iota((RANK, RANK), 0) == iota((RANK, RANK), 1)
    tops[...] = jnp.where(crossing, value, 0.0) + jnp.where(square, ridge[0], 0.0)

    total = ps[col].astype(F32)
    rhs = rs[...]
    for k in range(1, COLS):
        send_part(k).wait_recv()
        total = total + pr[k].astype(F32)
    for k in range(1, COLS):
        send_rhs(k).wait_recv()
        rhs = rhs + rr[k]
    total = total * (1.0 / NODE)
    t4[0] = total[:, 2 * RANK :].astype(BF)
    r4[0] = rhs * (1.0 / NODE)

    def send_top(k):
        return remote(t4.at[0], t4.at[k], (s_t, r_t), k, cousin(k))

    def send_top_rhs(k):
        return remote(r4.at[0], r4.at[k], (s_q, r_q), k, cousin(k))

    for k in range(1, 4):
        send_top(k).start()
        send_top_rhs(k).start()
    diagonal = iota((SLAB, 2 * RANK), 0) + col * SLAB == iota((SLAB, 2 * RANK), 1)
    out_share[0] = total[:, : 2 * RANK] + jnp.where(diagonal, ridge[0], 0.0)
    result = total[:, 2 * RANK :] + tops[pl.ds(pl.multiple_of(col * SLAB, SLAB), SLAB), :]
    rhs = r4[0]
    for k in range(1, 4):
        send_top(k).wait_recv()
        send_top_rhs(k).wait_recv()
        result = result + t4[k].astype(F32)
        rhs = rhs + r4[k]
    out_top[0] = result
    out_rhs[...] = jnp.concatenate([rhs[0:1], rhs[1:2]], 1)

    def finish(k, _):
        send_aux(k).wait_send()
        send_feat(k).wait_send()
        return 0

    lax.fori_loop(1, LEAVES, finish, 0)
    for k in range(1, COLS):
        send_skel(k).wait_send()
        send_part(k).wait_send()
        send_rhs(k).wait_send()
    for k in range(1, 4):
        send_four(k).wait_send()
        send_top(k).wait_send()
        send_top_rhs(k).wait_send()


SHAPES = ((1, SLAB, 2 * RANK), (1, SLAB, RANK), (1, RANK))


def exchange(feat, aux, ridge, *smalls):
    return pl.pallas_call(
        exchange_kernel,
        out_shape=tuple(pltpu.VMEM(shape, F32) for shape in SHAPES),
        in_specs=[VMEM, VMEM, pl.BlockSpec(memory_space=pltpu.SMEM)] + [ANYWHERE] * 4,
        out_specs=[VMEM] * 3,
        scratch_shapes=[
            pltpu.VMEM((1, RANK), jnp.int32),
            pltpu.VMEM((1, F), F32),
            pltpu.VMEM((8, RANK), jnp.int32),
            pltpu.VMEM((4, RANK), jnp.int32),
            pltpu.VMEM((8, 128), F32),
            pltpu.VMEM((LEAVES, F, PER), BF),
            pltpu.VMEM((LEAVES, 8, 128), F32),
            pltpu.VMEM((LEAVES, RANK, PER), BF),
            pltpu.VMEM((LEAVES, 16, PER), BF),
            pltpu.VMEM((COLS, F, RANK), BF),
            pltpu.VMEM((F, RANK), BF),
            pltpu.VMEM((4, F, RANK), BF),
            pltpu.VMEM((2 * RANK, 256), BF),
            pltpu.VMEM((2, 2 * RANK + 16, PER), BF),
            pltpu.VMEM((2 * RANK + 16, RANK), F32),
            pltpu.VMEM((RANK, RANK), BF),
            pltpu.VMEM((RANK, 2 * RANK), BF),
            pltpu.VMEM((RANK, 4 * RANK), BF),
            pltpu.VMEM((RANK, 128), F32),
            pltpu.VMEM((RANK, RANK), F32),
            pltpu.VMEM((COLS, SLAB, 3 * RANK), BF),
            pltpu.VMEM((COLS, SLAB, 3 * RANK), BF),
            pltpu.VMEM((8, 128), F32),
            pltpu.VMEM((COLS, 8, 128), F32),
            pltpu.VMEM((4, SLAB, RANK), BF),
            pltpu.VMEM((4, 8, 128), F32),
            *dma(LEAVES),
            *dma(LEAVES),
            *dma(COLS),
            *dma(4),
            *dma(COLS),
            *dma(COLS),
            *dma(4),
            *dma(4),
            pltpu.SemaphoreType.DMA((4,)),
        ],
        compiler_params=params(0, 40),
        name="exchange",
    )(feat, aux, ridge, *in_hbm(*smalls))


def emit_kernel(*refs):
    ins, outs, sem = refs[:3], refs[3:6], refs[6]
    copies = [pltpu.make_async_copy(a, b, sem.at[k]) for k, (a, b) in enumerate(zip(ins, outs))]
    for copy in copies:
        copy.start()
    for copy in copies:
        copy.wait()


def emit(results):
    return pl.pallas_call(
        emit_kernel,
        out_shape=tuple(jax.ShapeDtypeStruct(shape, F32) for shape in SHAPES),
        in_specs=[VMEM] * 3,
        out_specs=[ANYWHERE] * 3,
        scratch_shapes=[pltpu.SemaphoreType.DMA((3,))],
        compiler_params=params(),
        name="emit",
    )(*results)


def local(features, targets, owner, length_scales, ridge, leaf_pivots, parent_pivots, top_pivots):
    feat, aux = pack(
        features, targets.reshape(ROWS // 128, 128), owner.reshape(ROWS // 128, 128)
    )
    return tuple(
        emit(
            exchange(
                feat, aux, ridge, leaf_pivots, length_scales.reshape(1, F), parent_pivots, top_pivots
            )
        )
    )


def solution(mesh):
    return jax.shard_map(
        local,
        mesh=mesh,
        in_specs=(
            P(None, ("leaf", "col")),
            P(("leaf", "col")),
            P(("leaf", "col")),
            P(),
            P(),
            P("leaf", None),
            P(),
            P(),
        ),
        out_specs=(P("leaf", "col", None), P("leaf", "col", None), P("leaf", None)),
        check_vma=False,
    )
```

time: 269 us -> 56.8 us (0.21)
  matrix products: 69.9 us -> 0 us
  waiting for transfers between devices: 58.6 us -> 0 us
  Pallas kernels: 0 us -> 55.3 us
  blocking collectives: 38.3 us -> 0 us
  local copies, waits for them, and re-layouts: 31.7 us -> 0 us
  starting transfers between devices: 31.4 us -> 0 us
  other arithmetic: 17.8 us -> 0 us
  between operations: 15.1 us -> 1.29 us
  loops' own time: 5.87 us -> 0 us
    dot_general x20 -> x0, matrix products: 69.9 us -> none  [the longest x8 42.8 us: block(): jnp.dot(joined, selector, preferred_element_type=jnp.float32)]
    pallas_call x0 -> x3, Pallas kernels: none -> 55.3 us  [the longest x1 47 us: exchange(): pl.pallas_call(exchange_kernel, out_shape=tuple((pltpu.VMEM(shape, F32) f...]
    psum x1 -> x0, waiting for transfers between devices: 40 us -> none  [local(): stacked, rhs = lax.psum((stacked, rhs), 'col')]
    psum x2 -> x0, blocking collectives: 38.3 us -> none  [the longest x1 25.5 us: local(): own_skel = lax.psum(picked.astype(jnp.bfloat16), 'col').astype(jnp.float32)]
    ppermute x6 -> x0, starting transfers between devices: 19.8 us -> none  [from_partner(): lax.ppermute(shard, axis, [(i, i ^ 1 << apart) for i in range(lax.axis_si...]
    all_to_all x1 -> x0, waiting for transfers between devices: 11.9 us -> none  [local(): lax.all_to_all(arranged, ('leaf', 'col'), split_axis=1, concat_axis=1, ti...]
    all_to_all x1 -> x0, starting transfers between devices: 11.5 us -> none  [local(): lax.all_to_all(arranged, ('leaf', 'col'), split_axis=1, concat_axis=1, ti...]
    gather x7 -> x0, local copies, waits for them, and re-layouts: 8.92 us -> none  [the longest x1 2.21 us: merge_pair(): rhs = jnp.take(jnp.concatenate([first_rhs, second_rhs]), pivots)]
  transfers between devices with their start and end apart: 8 -> 0, of which waited for: 5 -> 0; matrix products, arithmetic and copies ran while one was open for 5% -> 0% of each run, Pallas kernels for 0% -> 0%
where the time goes in v1:
time: 56.8 us; the launch traced here: 56.6 us
  Pallas kernels  55.3 us (97%)
  between operations  1.29 us (2%)
    pallas_call x1, Pallas kernels, exchange(): pl.pallas_call(exchange_kernel, out_shape=tuple((pltpu.VMEM(shape, F32) f...  47 us
    pallas_call x1, Pallas kernels, pack(): pl.pallas_call(pack_kernel, out_shape=(pltpu.VMEM((LEAVES, F, PER), BF),...  7.7 us

profile of v1, /device:TPU:1, one launch (start us, length us, event | category | flops | bytes accessed | tf_op | source)
XLA Modules:
  0.0 56.6 jit_solution(12585993318237307822)
XLA Ops:
  1.3 7.7 %pack.1 = (bf16[16,48,512]{2,1,0:T(8,128)(2,1)S(1)}, f32[16,8,128]{2,1,0:T(8,128)S(1)}) custom-call(bf16[48,8192]{1,0:T(8,128)(2,1)} %feat_hbm.1, bf16[64,128]{1,0:T(8,128)(2,1)} %bitcast.4, s32[64,128]{1,0:T(8,128)} %bitcast.3), custom_call_target="tpu_custom_call" | custom-call | tf_op jit(solution)/shard_map/pack/pallas_call | solution.py:174
  9.0 47.0 %exchange.1 = (f32[1,32,512]{2,1,0:T(8,128)S(1)}, f32[1,32,256]{2,1,0:T(8,128)S(1)}, f32[1,256]{1,0:T(1,128)S(1)}) custom-call(bf16[16,48,512]{2,1,0:T(8,128)(2,1)S(1)} %get-tuple-element.8.feat, f32[16,8,128]{2,1,0:T(8,128)S(1)} %get-tuple-element.9.aux, f32[1]{0:T(128)S(6)} %copy.11.ridge, s32[1,256]{1,0:T(1,128)} %pivots_hbm.1, f32[1,48]{1,0:T(1,128)} %bitcast.5, ...), custom_call_target="tpu_custom_call" | custom-call | tf_op jit(solution)/shard_map/exchange/pallas_call | solution.py:518
  55.9 0.7 %emit.1 = (f32[1,32,512]{2,1,0:T(8,128)}, f32[1,32,256]{2,1,0:T(8,128)}, f32[1,256]{1,0:T(1,128)}) custom-call(f32[1,32,512]{2,1,0:T(8,128)S(1)} %get-tuple-element.10.refs_0_, f32[1,32,256]{2,1,0:T(8,128)S(1)} %get-tuple-element.11.refs_1_, f32[1,256]{1,0:T(1,128)S(1)} %get-tuple-element.12.refs_2_), custom_call_target="tpu_custom_call" | custom-call | tf_op jit(solution)/shard_map/emit/pallas_call | solution.py:575

commit v2 on v1

--- a/solution.py
+++ b/solution.py
@@ -63,8 +63,7 @@
 
 
 def pack_kernel(
-    feat_hbm, target, owner, out_feat, out_aux,
-    feat, goals, rows, ybuf, zbuf, table, scal, sem, feat_sem,
+    feat_hbm, target, owner, zbuf, feat, goals, rows, ybuf, table, scal, sem, feat_sem
 ):
     bring = pltpu.make_async_copy(feat_hbm, feat, feat_sem)
     bring.start()
@@ -105,7 +104,7 @@
     table[0:LEAVES, :] = jnp.full((LEAVES, 128), PER, jnp.int32)
     zero = jnp.zeros((LEAVES, 128), F32)
     _, _, most = lax.fori_loop(
-        0, CHUNKS, ranks, (jnp.zeros((OWNERS, 128), F32), zero, zero), unroll=8
+        0, CHUNKS, ranks, (jnp.zeros((OWNERS, 128), F32), zero, zero), unroll=4
     )
     most = jnp.broadcast_to(jnp.max(most, 0, keepdims=True), (8, 128))
     table[2 * LEAVES :, :] = most.astype(jnp.int32)
@@ -123,7 +122,7 @@
         ybuf[pl.ds(start, CHUNK), :] = dot_nt(chosen, joined)
         return 0
 
-    lax.fori_loop(0, CHUNKS, sort, 0, unroll=8)
+    lax.fori_loop(0, CHUNKS, sort, 0, unroll=4)
     move.wait()
     widest = scal[2 * LEAVES, 0]
 
@@ -157,14 +156,6 @@
 
         lax.fori_loop(0, CHUNKS * LEAVES, merge, 0)
 
-    eye = (iota((WIDE, WIDE), 0) == iota((WIDE, WIDE), 1)).astype(F32).astype(BF)
-    for i in range(LEAVES):
-        turned = dot_nt(eye, zbuf[i * REGION : i * REGION + PER, :].astype(BF))
-        out_feat[i] = turned[:F].astype(BF)
-        out_aux[i] = jnp.concatenate(
-            [turned[F + r : F + r + 1, 128 * k : 128 * k + 128] for r in range(2) for k in range(4)], 0
-        )
-
 
 def in_hbm(*arrays):
     return [pltpu.with_memory_space_constraint(a, pltpu.HBM) for a in arrays]
@@ -173,15 +164,14 @@
 def pack(features, targets, owner):
     return pl.pallas_call(
         pack_kernel,
-        out_shape=(pltpu.VMEM((LEAVES, F, PER), BF), pltpu.VMEM((LEAVES, 8, 128), F32)),
+        out_shape=pltpu.VMEM((LEAVES * REGION, WIDE), F32),
         in_specs=[ANYWHERE, VMEM, VMEM],
-        out_specs=[VMEM] * 2,
+        out_specs=VMEM,
         scratch_shapes=[
             pltpu.VMEM((F, ROWS), BF),
             pltpu.VMEM((ROWS // 128, 128), F32),
             pltpu.VMEM((CHUNKS, 8, CHUNK), F32),
             pltpu.VMEM((ROWS + WINDOW, WIDE), F32),
-            pltpu.VMEM((LEAVES * REGION, WIDE), F32),
             pltpu.VMEM((40, 128), jnp.int32),
             pltpu.SMEM((40, 128), jnp.int32),
             pltpu.SemaphoreType.DMA,
@@ -259,11 +249,8 @@
     return place_of(leaf - leaf % 4 + (leaf + k) % 4, col)
 
 
-def greet(peers):
-    barrier = pltpu.get_barrier_semaphore()
-    for peer in peers:
-        pl.semaphore_signal(barrier, inc=1, **peer)
-    return lambda: pl.semaphore_wait(barrier, len(peers))
+def each(count, step, unroll=1):
+    lax.fori_loop(1, count, lambda k, _: (step(k), 0)[1], 0, unroll=unroll)
 
 
 def remote(src, dst, sems, k, peer):
@@ -281,16 +268,18 @@
 
 
 def exchange_kernel(
-    feat, aux, ridge, pivots_hbm, scales_hbm, parent_hbm, top_hbm, out_share, out_top, out_rhs,
-    pivots, scales, parent, top, spare, rx, ra, hot, side, sk, mine, sk4, left, basis, acc,
-    rows, columns, fours, index, tops, ps, pr, rs, rr, t4, r4,
-    s_f, r_f, s_a, r_a, s_k, r_k, s_4, r_4, s_p, r_p, s_r, r_r, s_t, r_t, s_q, r_q, local,
+    merged, ridge, pivots_hbm, scales_hbm, parent_hbm, top_hbm, out_share, out_top, out_rhs,
+    pivots, scales, parent, top, spare, feat, aux, rx, ra, hot, side, sk, mine, sk4, left,
+    even, odd, acc, rows, columns, fours, index, tops, ps, pr, pt, qr, rs, rr, t4, r4,
+    s_f, r_f, s_a, r_a, s_k, r_k, s_4, r_4, s_p, r_p, s_o, r_o, s_r, r_r, s_t, r_t, s_q, r_q, local,
 ):
     leaf = lax.axis_index("leaf")
     col = lax.axis_index("col")
     quarter = leaf % 4
     sibling = quarter + 1 - 2 * (quarter % 2)
-    ready = greet([mate(k) for k in range(1, LEAVES)] + [beside(k) for k in range(1, COLS)])
+    barrier = pltpu.get_barrier_semaphore()
+    each(LEAVES, lambda k: pl.semaphore_signal(barrier, inc=1, **mate(k)))
+    each(COLS, lambda k: pl.semaphore_signal(barrier, inc=1, **beside(k)))
     smalls = [
         pltpu.make_async_copy(a, b, local.at[k])
         for k, (a, b) in enumerate(
@@ -300,25 +289,29 @@
     for copy in smalls:
         copy.start()
 
+    eye = (iota((WIDE, WIDE), 0) == iota((WIDE, WIDE), 1)).astype(F32).astype(BF)
+
+    def turn(k, _):
+        start = pl.multiple_of((leaf + k) % LEAVES * REGION, 8)
+        turned = dot_nt(eye, merged[pl.ds(start, PER), :].astype(BF))
+        feat[k] = turned[:F].astype(BF)
+        aux[k] = jnp.concatenate(
+            [turned[F + r : F + r + 1, 128 * k : 128 * k + 128] for r in range(2) for k in range(4)], 0
+        )
+        return 0
+
     def send_feat(k):
-        return remote(feat.at[(leaf + k) % LEAVES], rx.at[k], (s_f, r_f), k, mate(k))
+        return remote(feat.at[k], rx.at[k], (s_f, r_f), k, mate(k))
 
     def send_aux(k):
-        return remote(aux.at[(leaf + k) % LEAVES], ra.at[k], (s_a, r_a), k, mate(k))
-
-    def begin_aux(k, _):
-        send_aux(k).start()
-        return 0
-
-    def begin_feat(k, _):
-        send_feat(k).start()
-        return 0
-
-    rx[0] = feat[leaf]
-    ra[0] = aux[leaf]
-    ready()
-    lax.fori_loop(1, LEAVES, begin_aux, 0)
-    lax.fori_loop(1, LEAVES, begin_feat, 0)
+        return remote(aux.at[k], ra.at[k], (s_a, r_a), k, mate(k))
+
+    lax.fori_loop(0, LEAVES, turn, 0, unroll=4)
+    rx[0] = feat[0]
+    ra[0] = aux[0]
+    pl.semaphore_wait(barrier, LEAVES + COLS - 2)
+    each(LEAVES, lambda k: send_aux(k).start())
+    each(LEAVES, lambda k: send_feat(k).start())
 
     for copy in smalls:
         copy.wait()
@@ -347,12 +340,11 @@
         hot[k] = (key == wanted).astype(F32).astype(BF)
 
     def mark_next(k, _):
-        send_aux(k).wait_recv()
+        pl.when(k > 0)(lambda: send_aux(k).wait_recv())
         mark(k)
         return 0
 
-    mark(0)
-    lax.fori_loop(1, LEAVES, mark_next, 0)
+    lax.fori_loop(0, LEAVES, mark_next, 0)
 
     index[...] = top_index(parent, top, leaf // 4)
     index2 = across(index[...], 2 * RANK)
@@ -366,91 +358,97 @@
     chosen = across(index[...], 4 * RANK) == iota((RANK, 4 * RANK), 1).astype(F32)
     fours[...] = chosen.astype(F32).astype(BF)
 
-    def pick(k, total):
-        send_feat(k).wait_recv()
-        return total + dot_nt(hot[k], rx[k])
-
-    picked = lax.fori_loop(1, LEAVES, pick, dot_nt(hot[0], rx[0]))
+    def pick(j, total):
+        for r in range(4):
+            k = 4 * j + r
+            if r:
+                send_feat(k).wait_recv()
+            else:
+                pl.when(k > 0)(lambda: send_feat(k).wait_recv())
+        for r in range(4):
+            total = total + dot_nt(hot[4 * j + r], rx[4 * j + r])
+        return total
+
+    picked = lax.fori_loop(0, LEAVES // 4, pick, jnp.zeros((RANK, F), F32))
     picked = jnp.concatenate([picked, jnp.zeros((RANK, 128 - F), F32)], 1).T[:F]
     sk[0] = picked.astype(BF)
 
     def send_skel(k):
         return remote(sk.at[0], sk.at[k], (s_k, r_k), k, beside(k))
 
-    for k in range(1, COLS):
-        send_skel(k).start()
+    each(COLS, lambda k: send_skel(k).start())
 
     def norms(k, _):
         side[k] = point_side(rx[k].astype(F32), scale4)
         return 0
 
-    lax.fori_loop(0, LEAVES, norms, 0, unroll=2)
-    for k in range(1, COLS):
+    lax.fori_loop(0, LEAVES, norms, 0)
+
+    def add_skel(k, total):
         send_skel(k).wait_recv()
-        picked = picked + sk[k].astype(F32)
+        return total + sk[k].astype(F32)
+
+    picked = lax.fori_loop(1, COLS, add_skel, picked)
     mine[...] = picked.astype(BF)
     sk4[quarter] = picked.astype(BF)
 
     def send_four(k):
         return remote(mine, sk4.at[quarter], (s_4, r_4), k, cousin(k))
 
-    for k in (1, 3, 2):
-        send_four(k).start()
+    each(4, lambda k: send_four(k).start())
     left[0:RANK, :] = skel_side(picked, scale2)
-    for k in range(1, 4):
-        remote(mine, sk4.at[(quarter + 4 - k) % 4], (s_4, r_4), k, cousin(k)).wait_recv()
+    each(4, lambda k: remote(mine, sk4.at[(quarter + 4 - k) % 4], (s_4, r_4), k, cousin(k)).wait_recv())
     left[RANK:, :] = skel_side(sk4[sibling].astype(F32), scale2)
 
-    def block_of(k, slot):
+    def block_of(k, half):
         p = rx[k]
         fill = jnp.zeros((256 - 3 * F - 16, PER), BF)
-        right = jnp.concatenate([p, p, p, side[k], fill], 0)
-        power = dot(left[...], right)
-        basis[slot, 0 : 2 * RANK, :] = jnp.exp2(jnp.minimum(power, 0.0)).astype(BF)
+        power = dot(left[...], jnp.concatenate([p, p, p, side[k], fill], 0))
+        half[0 : 2 * RANK, :] = jnp.exp2(jnp.minimum(power, 0.0)).astype(BF)
         value = jnp.concatenate([ra[k, r : r + 1, :] for r in range(4)], 1)
-        basis[slot, 2 * RANK :, :] = jnp.broadcast_to(value, (16, PER)).astype(BF)
-
-    def gram_of(slot):
-        acc[...] += dot_nt(basis[slot], basis[slot, 0:RANK, :])
+        half[2 * RANK :, :] = jnp.broadcast_to(value, (16, PER)).astype(BF)
+
+    def gram_of(half):
+        acc[...] += dot_nt(half[...], half[0:RANK, :])
+
+    def two(j, _):
+        block_of(2 * j, even)
+        gram_of(odd)
+        block_of(2 * j + 1, odd)
+        gram_of(even)
+        return 0
 
     acc[...] = jnp.zeros_like(acc)
-    block_of(0, 0)
-
-    def two(step, _):
-        block_of(2 * step + 1, 1)
-        gram_of(0)
-        block_of(2 * step + 2, 0)
-        gram_of(1)
-        return 0
-
-    lax.fori_loop(0, LEAVES // 2 - 1, two, 0)
-    block_of(LEAVES - 1, 1)
-    gram_of(0)
-    gram_of(1)
+    odd[...] = jnp.zeros_like(odd)
+    lax.fori_loop(0, LEAVES // 2, two, 0)
+    gram_of(odd)
 
     gram = acc[0:RANK, :].astype(BF)
     couple = acc[RANK : 2 * RANK, :].T.astype(BF)
     part = jnp.concatenate([gram, couple], 1)
-    chosen = dot_nt(dot(rows[...], part).astype(BF), columns[...]).astype(BF)
+    for k in range(COLS):
+        ps[k] = part[k * SLAB : (k + 1) * SLAB]
+
+    def send_part(k):
+        return remote(ps.at[(col + k) % COLS], pr.at[k], (s_p, r_p), k, beside(k))
+
+    def send_chosen(k):
+        return remote(pt.at[(col + k) % COLS], qr.at[k], (s_o, r_o), k, beside(k))
+
+    def send_rhs(k):
+        return remote(rs, rr.at[k], (s_r, r_r), k, beside(k))
+
+    each(COLS, lambda k: send_part(k).start())
     rhs = acc[2 * RANK : 2 * RANK + 1, :]
     rhs = jnp.sum(dot_nt(stack16(split3(rhs), RANK), rows[...]), 0, keepdims=True)
-    for k in range(COLS):
-        cut = slice(k * SLAB, (k + 1) * SLAB)
-        ps[k, :, 0 : 2 * RANK] = part[cut]
-        ps[k, :, 2 * RANK :] = chosen[cut]
     rs[...] = jnp.zeros_like(rs)
     rs[0:1, :] = rhs[:, :128]
     rs[1:2, :] = rhs[:, 128:]
-
-    def send_part(k):
-        return remote(ps.at[(col + k) % COLS], pr.at[k], (s_p, r_p), k, beside(k))
-
-    def send_rhs(k):
-        return remote(rs, rr.at[k], (s_r, r_r), k, beside(k))
-
-    for k in range(1, COLS):
-        send_part(k).start()
-        send_rhs(k).start()
+    chosen = dot_nt(dot(rows[...], part).astype(BF), columns[...]).astype(BF)
+    for k in range(COLS):
+        pt[k] = chosen[k * SLAB : (k + 1) * SLAB]
+    each(COLS, lambda k: send_chosen(k).start())
+    each(COLS, lambda k: send_rhs(k).start())
 
     whole = jnp.concatenate([sk4[k] for k in range(4)], 1)
     points = dot_nt(whole, fours[...])
@@ -462,16 +460,21 @@
     square = iota((RANK, RANK), 0) == iota((RANK, RANK), 1)
     tops[...] = jnp.where(crossing, value, 0.0) + jnp.where(square, ridge[0], 0.0)
 
-    total = ps[col].astype(F32)
-    rhs = rs[...]
-    for k in range(1, COLS):
+    def add_part(k, total):
         send_part(k).wait_recv()
-        total = total + pr[k].astype(F32)
-    for k in range(1, COLS):
+        return total + pr[k].astype(F32)
+
+    def add_chosen(k, totals):
+        send_chosen(k).wait_recv()
         send_rhs(k).wait_recv()
-        rhs = rhs + rr[k]
-    total = total * (1.0 / NODE)
-    t4[0] = total[:, 2 * RANK :].astype(BF)
+        return totals[0] + qr[k].astype(F32), totals[1] + rr[k]
+
+    total = lax.fori_loop(1, COLS, add_part, ps[col].astype(F32))
+    diagonal = iota((SLAB, 2 * RANK), 0) + col * SLAB == iota((SLAB, 2 * RANK), 1)
+    out_share[0] = total * (1.0 / NODE) + jnp.where(diagonal, ridge[0], 0.0)
+    chosen, rhs = lax.fori_loop(1, COLS, add_chosen, (pt[col].astype(F32), rs[...]))
+    chosen = chosen * (1.0 / NODE)
+    t4[0] = chosen.astype(BF)
     r4[0] = rhs * (1.0 / NODE)
 
     def send_top(k):
@@ -480,45 +483,35 @@
     def send_top_rhs(k):
         return remote(r4.at[0], r4.at[k], (s_q, r_q), k, cousin(k))
 
-    for k in range(1, 4):
-        send_top(k).start()
-        send_top_rhs(k).start()
-    diagonal = iota((SLAB, 2 * RANK), 0) + col * SLAB == iota((SLAB, 2 * RANK), 1)
-    out_share[0] = total[:, : 2 * RANK] + jnp.where(diagonal, ridge[0], 0.0)
-    result = total[:, 2 * RANK :] + tops[pl.ds(pl.multiple_of(col * SLAB, SLAB), SLAB), :]
-    rhs = r4[0]
-    for k in range(1, 4):
+    each(4, lambda k: send_top(k).start())
+    each(4, lambda k: send_top_rhs(k).start())
+    result = chosen + tops[pl.ds(pl.multiple_of(col * SLAB, SLAB), SLAB), :]
+
+    def add_top(k, totals):
         send_top(k).wait_recv()
         send_top_rhs(k).wait_recv()
-        result = result + t4[k].astype(F32)
-        rhs = rhs + r4[k]
+        return totals[0] + t4[k].astype(F32), totals[1] + r4[k]
+
+    result, rhs = lax.fori_loop(1, 4, add_top, (result, r4[0]))
     out_top[0] = result
     out_rhs[...] = jnp.concatenate([rhs[0:1], rhs[1:2]], 1)
 
-    def finish(k, _):
-        send_aux(k).wait_send()
-        send_feat(k).wait_send()
-        return 0
-
-    lax.fori_loop(1, LEAVES, finish, 0)
-    for k in range(1, COLS):
-        send_skel(k).wait_send()
-        send_part(k).wait_send()
-        send_rhs(k).wait_send()
-    for k in range(1, 4):
-        send_four(k).wait_send()
-        send_top(k).wait_send()
-        send_top_rhs(k).wait_send()
+    def finish(sends):
+        return lambda k: [send(k).wait_send() for send in sends]
+
+    each(LEAVES, finish((send_aux, send_feat)))
+    each(COLS, finish((send_skel, send_part, send_chosen, send_rhs)))
+    each(4, finish((send_four, send_top, send_top_rhs)))
 
 
 SHAPES = ((1, SLAB, 2 * RANK), (1, SLAB, RANK), (1, RANK))
 
 
-def exchange(feat, aux, ridge, *smalls):
+def exchange(merged, ridge, *smalls):
     return pl.pallas_call(
         exchange_kernel,
         out_shape=tuple(pltpu.VMEM(shape, F32) for shape in SHAPES),
-        in_specs=[VMEM, VMEM, pl.BlockSpec(memory_space=pltpu.SMEM)] + [ANYWHERE] * 4,
+        in_specs=[VMEM, pl.BlockSpec(memory_space=pltpu.SMEM)] + [ANYWHERE] * 4,
         out_specs=[VMEM] * 3,
         scratch_shapes=[
             pltpu.VMEM((1, RANK), jnp.int32),
@@ -528,21 +521,26 @@
             pltpu.VMEM((8, 128), F32),
             pltpu.VMEM((LEAVES, F, PER), BF),
             pltpu.VMEM((LEAVES, 8, 128), F32),
+            pltpu.VMEM((LEAVES, F, PER), BF),
+            pltpu.VMEM((LEAVES, 8, 128), F32),
             pltpu.VMEM((LEAVES, RANK, PER), BF),
             pltpu.VMEM((LEAVES, 16, PER), BF),
             pltpu.VMEM((COLS, F, RANK), BF),
             pltpu.VMEM((F, RANK), BF),
             pltpu.VMEM((4, F, RANK), BF),
             pltpu.VMEM((2 * RANK, 256), BF),
-            pltpu.VMEM((2, 2 * RANK + 16, PER), BF),
+            pltpu.VMEM((2 * RANK + 16, PER), BF),
+            pltpu.VMEM((2 * RANK + 16, PER), BF),
             pltpu.VMEM((2 * RANK + 16, RANK), F32),
             pltpu.VMEM((RANK, RANK), BF),
             pltpu.VMEM((RANK, 2 * RANK), BF),
             pltpu.VMEM((RANK, 4 * RANK), BF),
             pltpu.VMEM((RANK, 128), F32),
             pltpu.VMEM((RANK, RANK), F32),
-            pltpu.VMEM((COLS, SLAB, 3 * RANK), BF),
-            pltpu.VMEM((COLS, SLAB, 3 * RANK), BF),
+            pltpu.VMEM((COLS, SLAB, 2 * RANK), BF),
+            pltpu.VMEM((COLS, SLAB, 2 * RANK), BF),
+            pltpu.VMEM((COLS, SLAB, RANK), BF),
+            pltpu.VMEM((COLS, SLAB, RANK), BF),
             pltpu.VMEM((8, 128), F32),
             pltpu.VMEM((COLS, 8, 128), F32),
             pltpu.VMEM((4, SLAB, RANK), BF),
@@ -553,13 +551,14 @@
             *dma(4),
             *dma(COLS),
             *dma(COLS),
+            *dma(COLS),
             *dma(4),
             *dma(4),
             pltpu.SemaphoreType.DMA((4,)),
         ],
         compiler_params=params(0, 40),
         name="exchange",
-    )(feat, aux, ridge, *in_hbm(*smalls))
+    )(merged, ridge, *in_hbm(*smalls))
 
 
 def emit_kernel(*refs):
@@ -584,16 +583,9 @@
 
 
 def local(features, targets, owner, length_scales, ridge, leaf_pivots, parent_pivots, top_pivots):
-    feat, aux = pack(
-        features, targets.reshape(ROWS // 128, 128), owner.reshape(ROWS // 128, 128)
-    )
-    return tuple(
-        emit(
-            exchange(
-                feat, aux, ridge, leaf_pivots, length_scales.reshape(1, F), parent_pivots, top_pivots
-            )
-        )
-    )
+    merged = pack(features, targets.reshape(ROWS // 128, 128), owner.reshape(ROWS // 128, 128))
+    smalls = (leaf_pivots, length_scales.reshape(1, F), parent_pivots, top_pivots)
+    return tuple(emit(exchange(merged, ridge, *smalls)))
 
 
 def solution(mesh):

time: 56.8 us -> 57.3 us (level)
  no operation moved by 1% of the time
where the time goes in v2:
time: 57.3 us; the launch traced here: 57.1 us
  Pallas kernels  55.8 us (97%)
  between operations  1.29 us (2%)
    pallas_call x1, Pallas kernels, exchange(): pl.pallas_call(exchange_kernel, out_shape=tuple((pltpu.VMEM(shape, F32) f...  47.3 us
    pallas_call x1, Pallas kernels, pack(): pl.pallas_call(pack_kernel, out_shape=pltpu.VMEM((LEAVES * REGION, WIDE),...  7.9 us

profile of v2, /device:TPU:1, one launch (start us, length us, event | category | flops | bytes accessed | tf_op | source)
XLA Modules:
  0.0 57.1 jit_solution(17886486887105496796)
XLA Ops:
  1.3 7.9 %pack.1.merged = f32[8832,64]{1,0:T(8,128)S(1)} custom-call(bf16[48,8192]{1,0:T(8,128)(2,1)} %feat_hbm.1, bf16[64,128]{1,0:T(8,128)(2,1)} %bitcast.4, s32[64,128]{1,0:T(8,128)} %bitcast.3), custom_call_target="tpu_custom_call" | custom-call | tf_op jit(solution)/shard_map/pack/pallas_call | solution.py:165
  9.2 47.3 %exchange.1 = (f32[1,32,512]{2,1,0:T(8,128)S(1)}, f32[1,32,256]{2,1,0:T(8,128)S(1)}, f32[1,256]{1,0:T(1,128)S(1)}) custom-call(f32[8832,64]{1,0:T(8,128)S(1)} %pack.1.merged, f32[1]{0:T(128)S(6)} %copy.11.ridge, s32[1,256]{1,0:T(1,128)} %pivots_hbm.1, f32[1,48]{1,0:T(1,128)} %bitcast.5, s32[8,256]{1,0:T(8,128)} %parent_hbm.1, s32[4,256]{1,0:T(4,128)} %top_hbm.1), custom_call_target="tpu_custom_call" | custom-call | tf_op jit(solution)/shard_map/exchange/pallas_call | solution.py:511
  56.5 0.7 %emit.1 = (f32[1,32,512]{2,1,0:T(8,128)}, f32[1,32,256]{2,1,0:T(8,128)}, f32[1,256]{1,0:T(1,128)}) custom-call(f32[1,32,512]{2,1,0:T(8,128)S(1)} %get-tuple-element.6.refs_0_, f32[1,32,256]{2,1,0:T(8,128)S(1)} %get-tuple-element.7.refs_1_, f32[1,256]{1,0:T(1,128)S(1)} %get-tuple-element.8.refs_2_), custom_call_target="tpu_custom_call" | custom-call | tf_op jit(solution)/shard_map/emit/pallas_call | solution.py:574

commit v3 on v2

--- a/solution.py
+++ b/solution.py
@@ -104,7 +104,7 @@
     table[0:LEAVES, :] = jnp.full((LEAVES, 128), PER, jnp.int32)
     zero = jnp.zeros((LEAVES, 128), F32)
     _, _, most = lax.fori_loop(
-        0, CHUNKS, ranks, (jnp.zeros((OWNERS, 128), F32), zero, zero), unroll=4
+        0, CHUNKS, ranks, (jnp.zeros((OWNERS, 128), F32), zero, zero), unroll=16
     )
     most = jnp.broadcast_to(jnp.max(most, 0, keepdims=True), (8, 128))
     table[2 * LEAVES :, :] = most.astype(jnp.int32)
@@ -122,7 +122,7 @@
         ybuf[pl.ds(start, CHUNK), :] = dot_nt(chosen, joined)
         return 0
 
-    lax.fori_loop(0, CHUNKS, sort, 0, unroll=4)
+    lax.fori_loop(0, CHUNKS, sort, 0, unroll=8)
     move.wait()
     widest = scal[2 * LEAVES, 0]
 
@@ -135,7 +135,7 @@
                 zbuf[pl.ds(goal, WINDOW), :] = ybuf[pl.ds(source, WINDOW), :]
             return 0
 
-        lax.fori_loop(0, CHUNKS, merge, 0, unroll=2)
+        lax.fori_loop(0, CHUNKS, merge, 0, unroll=4)
 
     @pl.when(widest > WINDOW)
     def slow():
@@ -270,8 +270,9 @@
 def exchange_kernel(
     merged, ridge, pivots_hbm, scales_hbm, parent_hbm, top_hbm, out_share, out_top, out_rhs,
     pivots, scales, parent, top, spare, feat, aux, rx, ra, hot, side, sk, mine, sk4, left,
-    even, odd, acc, rows, columns, fours, index, tops, ps, pr, pt, qr, rs, rr, t4, r4,
-    s_f, r_f, s_a, r_a, s_k, r_k, s_4, r_4, s_p, r_p, s_o, r_o, s_r, r_r, s_t, r_t, s_q, r_q, local,
+    even, odd, other_even, other_odd, gram, couple, rows, columns, fours, index, tops,
+    pg, gr, pc, cr, pt, qr, rs, rr, t4, r4,
+    s_f, r_f, s_a, r_a, s_k, r_k, s_4, r_4, s_p, r_p, s_c, r_c, s_o, r_o, s_r, r_r, s_t, r_t, s_q, r_q, local,
 ):
     leaf = lax.axis_index("leaf")
     col = lax.axis_index("col")
@@ -291,14 +292,13 @@
 
     eye = (iota((WIDE, WIDE), 0) == iota((WIDE, WIDE), 1)).astype(F32).astype(BF)
 
-    def turn(k, _):
+    def turn(k):
         start = pl.multiple_of((leaf + k) % LEAVES * REGION, 8)
         turned = dot_nt(eye, merged[pl.ds(start, PER), :].astype(BF))
         feat[k] = turned[:F].astype(BF)
         aux[k] = jnp.concatenate(
-            [turned[F + r : F + r + 1, 128 * k : 128 * k + 128] for r in range(2) for k in range(4)], 0
+            [turned[F + r : F + r + 1, 128 * c : 128 * c + 128] for r in range(2) for c in range(4)], 0
         )
-        return 0
 
     def send_feat(k):
         return remote(feat.at[k], rx.at[k], (s_f, r_f), k, mate(k))
@@ -306,12 +306,19 @@
     def send_aux(k):
         return remote(aux.at[k], ra.at[k], (s_a, r_a), k, mate(k))
 
-    lax.fori_loop(0, LEAVES, turn, 0, unroll=4)
+    def four(j, _):
+        for r in range(1, 5):
+            turn((4 * j + r) % LEAVES)
+        pl.when(j == 0)(lambda: pl.semaphore_wait(barrier, LEAVES + COLS - 2))
+        for send in (send_aux, send_feat):
+            for r in range(1, 4):
+                send(4 * j + r).start()
+            pl.when(j < 3)(lambda: send(4 * j + 4).start())
+        return 0
+
+    lax.fori_loop(0, LEAVES // 4, four, 0)
     rx[0] = feat[0]
     ra[0] = aux[0]
-    pl.semaphore_wait(barrier, LEAVES + COLS - 2)
-    each(LEAVES, lambda k: send_aux(k).start())
-    each(LEAVES, lambda k: send_feat(k).start())
 
     for copy in smalls:
         copy.wait()
@@ -397,40 +404,53 @@
 
     each(4, lambda k: send_four(k).start())
     left[0:RANK, :] = skel_side(picked, scale2)
-    each(4, lambda k: remote(mine, sk4.at[(quarter + 4 - k) % 4], (s_4, r_4), k, cousin(k)).wait_recv())
-    left[RANK:, :] = skel_side(sk4[sibling].astype(F32), scale2)
-
-    def block_of(k, half):
+
+    def block_of(k, out, begin):
         p = rx[k]
         fill = jnp.zeros((256 - 3 * F - 16, PER), BF)
-        power = dot(left[...], jnp.concatenate([p, p, p, side[k], fill], 0))
-        half[0 : 2 * RANK, :] = jnp.exp2(jnp.minimum(power, 0.0)).astype(BF)
+        right = jnp.concatenate([p, p, p, side[k], fill], 0)
+        power = dot(left[begin : begin + RANK, :], right)
+        out[0:RANK, :] = jnp.exp2(jnp.minimum(power, 0.0)).astype(BF)
+
+    def own_of(k, out):
+        block_of(k, out, 0)
         value = jnp.concatenate([ra[k, r : r + 1, :] for r in range(4)], 1)
-        half[2 * RANK :, :] = jnp.broadcast_to(value, (16, PER)).astype(BF)
-
-    def gram_of(half):
-        acc[...] += dot_nt(half[...], half[0:RANK, :])
-
-    def two(j, _):
-        block_of(2 * j, even)
-        gram_of(odd)
-        block_of(2 * j + 1, odd)
-        gram_of(even)
+        out[RANK:, :] = jnp.broadcast_to(value, (16, PER)).astype(BF)
+
+    def gram_of(u):
+        gram[...] += dot_nt(u[...], u[0:RANK, :])
+
+    def couple_of(v, u):
+        couple[...] += dot_nt(v[...], u[0:RANK, :])
+
+    last = LEAVES // 2 - 1
+
+    def own_two(j, _):
+        own_of(2 * j, even.at[j])
+        gram_of(odd.at[(j + last) % (last + 1)])
+        own_of(2 * j + 1, odd.at[j])
+        gram_of(even.at[j])
         return 0
 
-    acc[...] = jnp.zeros_like(acc)
-    odd[...] = jnp.zeros_like(odd)
-    lax.fori_loop(0, LEAVES // 2, two, 0)
-    gram_of(odd)
-
-    gram = acc[0:RANK, :].astype(BF)
-    couple = acc[RANK : 2 * RANK, :].T.astype(BF)
-    part = jnp.concatenate([gram, couple], 1)
-    for k in range(COLS):
-        ps[k] = part[k * SLAB : (k + 1) * SLAB]
-
-    def send_part(k):
-        return remote(ps.at[(col + k) % COLS], pr.at[k], (s_p, r_p), k, beside(k))
+    def other_two(j, _):
+        block_of(2 * j, other_even, RANK)
+        couple_of(other_odd, odd.at[(j + last) % (last + 1)])
+        block_of(2 * j + 1, other_odd, RANK)
+        couple_of(other_even, even.at[j])
+        return 0
+
+    gram[...] = jnp.zeros_like(gram)
+    couple[...] = jnp.zeros_like(couple)
+    odd[last] = jnp.zeros((RANK + 16, PER), BF)
+    other_odd[...] = jnp.zeros_like(other_odd)
+    lax.fori_loop(0, last + 1, own_two, 0)
+    gram_of(odd.at[last])
+
+    def send_gram(k):
+        return remote(pg.at[(col + k) % COLS], gr.at[k], (s_p, r_p), k, beside(k))
+
+    def send_couple(k):
+        return remote(pc.at[(col + k) % COLS], cr.at[k], (s_c, r_c), k, beside(k))
 
     def send_chosen(k):
         return remote(pt.at[(col + k) % COLS], qr.at[k], (s_o, r_o), k, beside(k))
@@ -438,17 +458,33 @@
     def send_rhs(k):
         return remote(rs, rr.at[k], (s_r, r_r), k, beside(k))
 
-    each(COLS, lambda k: send_part(k).start())
-    rhs = acc[2 * RANK : 2 * RANK + 1, :]
+    part = gram[0:RANK, :].astype(BF)
+    for k in range(COLS):
+        pg[k] = part[k * SLAB : (k + 1) * SLAB]
+    rhs = gram[RANK : RANK + 1, :]
     rhs = jnp.sum(dot_nt(stack16(split3(rhs), RANK), rows[...]), 0, keepdims=True)
     rs[...] = jnp.zeros_like(rs)
     rs[0:1, :] = rhs[:, :128]
     rs[1:2, :] = rhs[:, 128:]
-    chosen = dot_nt(dot(rows[...], part).astype(BF), columns[...]).astype(BF)
+    each(COLS, lambda k: send_gram(k).start())
+    each(COLS, lambda k: send_rhs(k).start())
+    tops[...] = dot_nt(dot(rows[...], part).astype(BF), columns[:, 0:RANK])
+
+    each(4, lambda k: remote(mine, sk4.at[(quarter + 4 - k) % 4], (s_4, r_4), k, cousin(k)).wait_recv())
+    left[RANK:, :] = skel_side(sk4[sibling].astype(F32), scale2)
+    lax.fori_loop(0, last + 1, other_two, 0)
+    couple_of(other_odd, odd.at[last])
+
+    part = couple[...].astype(BF)
+    chosen = dot_nt(dot_nt(rows[...], part).astype(BF), columns[:, RANK:]) + tops[...]
+    chosen = chosen.astype(BF)
     for k in range(COLS):
         pt[k] = chosen[k * SLAB : (k + 1) * SLAB]
     each(COLS, lambda k: send_chosen(k).start())
-    each(COLS, lambda k: send_rhs(k).start())
+    part = couple[...].T.astype(BF)
+    for k in range(COLS):
+        pc[k] = part[k * SLAB : (k + 1) * SLAB]
+    each(COLS, lambda k: send_couple(k).start())
 
     whole = jnp.concatenate([sk4[k] for k in range(4)], 1)
     points = dot_nt(whole, fours[...])
@@ -460,18 +496,11 @@
     square = iota((RANK, RANK), 0) == iota((RANK, RANK), 1)
     tops[...] = jnp.where(crossing, value, 0.0) + jnp.where(square, ridge[0], 0.0)
 
-    def add_part(k, total):
-        send_part(k).wait_recv()
-        return total + pr[k].astype(F32)
-
     def add_chosen(k, totals):
         send_chosen(k).wait_recv()
         send_rhs(k).wait_recv()
         return totals[0] + qr[k].astype(F32), totals[1] + rr[k]
 
-    total = lax.fori_loop(1, COLS, add_part, ps[col].astype(F32))
-    diagonal = iota((SLAB, 2 * RANK), 0) + col * SLAB == iota((SLAB, 2 * RANK), 1)
-    out_share[0] = total * (1.0 / NODE) + jnp.where(diagonal, ridge[0], 0.0)
     chosen, rhs = lax.fori_loop(1, COLS, add_chosen, (pt[col].astype(F32), rs[...]))
     chosen = chosen * (1.0 / NODE)
     t4[0] = chosen.astype(BF)
@@ -485,6 +514,20 @@
 
     each(4, lambda k: send_top(k).start())
     each(4, lambda k: send_top_rhs(k).start())
+
+    def add_gram(k, total):
+        send_gram(k).wait_recv()
+        return total + gr[k].astype(F32)
+
+    def add_couple(k, total):
+        send_couple(k).wait_recv()
+        return total + cr[k].astype(F32)
+
+    total = lax.fori_loop(1, COLS, add_gram, pg[col].astype(F32))
+    diagonal = iota((SLAB, RANK), 0) + col * SLAB == iota((SLAB, RANK), 1)
+    out_share[0, :, 0:RANK] = total * (1.0 / NODE) + jnp.where(diagonal, ridge[0], 0.0)
+    total = lax.fori_loop(1, COLS, add_couple, pc[col].astype(F32))
+    out_share[0, :, RANK:] = total * (1.0 / NODE)
     result = chosen + tops[pl.ds(pl.multiple_of(col * SLAB, SLAB), SLAB), :]
 
     def add_top(k, totals):
@@ -500,7 +543,7 @@
         return lambda k: [send(k).wait_send() for send in sends]
 
     each(LEAVES, finish((send_aux, send_feat)))
-    each(COLS, finish((send_skel, send_part, send_chosen, send_rhs)))
+    each(COLS, finish((send_skel, send_gram, send_couple, send_chosen, send_rhs)))
     each(4, finish((send_four, send_top, send_top_rhs)))
 
 
@@ -529,16 +572,21 @@
             pltpu.VMEM((F, RANK), BF),
             pltpu.VMEM((4, F, RANK), BF),
             pltpu.VMEM((2 * RANK, 256), BF),
-            pltpu.VMEM((2 * RANK + 16, PER), BF),
-            pltpu.VMEM((2 * RANK + 16, PER), BF),
-            pltpu.VMEM((2 * RANK + 16, RANK), F32),
+            pltpu.VMEM((LEAVES // 2, RANK + 16, PER), BF),
+            pltpu.VMEM((LEAVES // 2, RANK + 16, PER), BF),
+            pltpu.VMEM((RANK, PER), BF),
+            pltpu.VMEM((RANK, PER), BF),
+            pltpu.VMEM((RANK + 16, RANK), F32),
+            pltpu.VMEM((RANK, RANK), F32),
             pltpu.VMEM((RANK, RANK), BF),
             pltpu.VMEM((RANK, 2 * RANK), BF),
             pltpu.VMEM((RANK, 4 * RANK), BF),
             pltpu.VMEM((RANK, 128), F32),
             pltpu.VMEM((RANK, RANK), F32),
-            pltpu.VMEM((COLS, SLAB, 2 * RANK), BF),
-            pltpu.VMEM((COLS, SLAB, 2 * RANK), BF),
+            pltpu.VMEM((COLS, SLAB, RANK), BF),
+            pltpu.VMEM((COLS, SLAB, RANK), BF),
+            pltpu.VMEM((COLS, SLAB, RANK), BF),
+            pltpu.VMEM((COLS, SLAB, RANK), BF),
             pltpu.VMEM((COLS, SLAB, RANK), BF),
             pltpu.VMEM((COLS, SLAB, RANK), BF),
             pltpu.VMEM((8, 128), F32),
@@ -549,6 +597,7 @@
             *dma(LEAVES),
             *dma(COLS),
             *dma(4),
+            *dma(COLS),
             *dma(COLS),
             *dma(COLS),
             *dma(COLS),

time: 57.3 us -> 54.1 us (0.944)
  Pallas kernels: 55.8 us -> 52.6 us
    pallas_call x1, Pallas kernels: 47.3 us -> 45.3 us  [exchange(): pl.pallas_call(exchange_kernel, out_shape=tuple((pltpu.VMEM(shape, F32) f...]
    pallas_call x1, Pallas kernels: 7.9 us -> 6.63 us  [pack(): pl.pallas_call(pack_kernel, out_shape=pltpu.VMEM((LEAVES * REGION, WIDE),...]
where the time goes in v3:
time: 54.1 us; the launch traced here: 53.9 us
  Pallas kernels  52.6 us (97%)
  between operations  1.29 us (2%)
    pallas_call x1, Pallas kernels, exchange(): pl.pallas_call(exchange_kernel, out_shape=tuple((pltpu.VMEM(shape, F32) f...  45.3 us
    pallas_call x1, Pallas kernels, pack(): pl.pallas_call(pack_kernel, out_shape=pltpu.VMEM((LEAVES * REGION, WIDE),...  6.63 us

profile of v3, /device:TPU:1, one launch (start us, length us, event | category | flops | bytes accessed | tf_op | source)
XLA Modules:
  0.0 53.9 jit_solution(5813838348846262130)
XLA Ops:
  1.3 6.6 %pack.1.merged = f32[8832,64]{1,0:T(8,128)S(1)} custom-call(bf16[48,8192]{1,0:T(8,128)(2,1)} %feat_hbm.1, bf16[64,128]{1,0:T(8,128)(2,1)} %bitcast.4, s32[64,128]{1,0:T(8,128)} %bitcast.3), custom_call_target="tpu_custom_call" | custom-call | tf_op jit(solution)/shard_map/pack/pallas_call | solution.py:165
  7.9 45.3 %exchange.1 = (f32[1,32,512]{2,1,0:T(8,128)S(1)}, f32[1,32,256]{2,1,0:T(8,128)S(1)}, f32[1,256]{1,0:T(1,128)S(1)}) custom-call(f32[8832,64]{1,0:T(8,128)S(1)} %pack.1.merged, f32[1]{0:T(128)S(6)} %copy.11.ridge, s32[1,256]{1,0:T(1,128)} %pivots_hbm.1, f32[1,48]{1,0:T(1,128)} %bitcast.5, s32[8,256]{1,0:T(8,128)} %parent_hbm.1, s32[4,256]{1,0:T(4,128)} %top_hbm.1), custom_call_target="tpu_custom_call" | custom-call | tf_op jit(solution)/shard_map/exchange/pallas_call | solution.py:554
  53.3 0.7 %emit.1 = (f32[1,32,512]{2,1,0:T(8,128)}, f32[1,32,256]{2,1,0:T(8,128)}, f32[1,256]{1,0:T(1,128)}) custom-call(f32[1,32,512]{2,1,0:T(8,128)S(1)} %get-tuple-element.6.refs_0_, f32[1,32,256]{2,1,0:T(8,128)S(1)} %get-tuple-element.7.refs_1_, f32[1,256]{1,0:T(1,128)S(1)} %get-tuple-element.8.refs_2_), custom_call_target="tpu_custom_call" | custom-call | tf_op jit(solution)/shard_map/emit/pallas_call | solution.py:623

commit v4 on v3

--- a/solution.py
+++ b/solution.py
@@ -20,6 +20,8 @@
 CHUNKS = ROWS // CHUNK
 WINDOW = 40
 REGION = PER + WINDOW
+SLOTS = 16
+WHICH = 50
 WIDE = 64
 SLAB = RANK // COLS
 NODE = ROWS * COLS
@@ -62,14 +64,13 @@
     return jnp.concatenate([two[0:1], two[1:2]], 1)
 
 
-def pack_kernel(
-    feat_hbm, target, owner, zbuf, feat, goals, rows, ybuf, table, scal, sem, feat_sem
-):
-    bring = pltpu.make_async_copy(feat_hbm, feat, feat_sem)
-    bring.start()
+def ordering():
+    return (iota((CHUNK, CHUNK), 0) < iota((CHUNK, CHUNK), 1)).astype(F32).astype(BF)
+
+
+def rank_all(target, owner, goals, rows, table):
     goals[...] = target[...].astype(F32)
-    before = (iota((CHUNK, CHUNK), 0) < iota((CHUNK, CHUNK), 1)).astype(F32).astype(BF)
-    weights = jnp.concatenate([before, jnp.ones((CHUNK, 128), BF)], 1)
+    weights = jnp.concatenate([ordering(), jnp.ones((CHUNK, 128), BF)], 1)
     lane = iota((LEAVES, 128), 1)
 
     def ranks(t, carry):
@@ -94,6 +95,7 @@
         rows[t, 0:1, :] = place
         rows[t, 1:2, :] = row_pair(goals[pl.ds(2 * t, 2), :])
         rows[t, 2:3, :] = tag
+        rows[t, 3:4, :] = own.astype(F32) * PACKET + rank
         here = lane == t
         table[0:LEAVES, :] = jnp.where(here, seen_leaf.astype(jnp.int32), table[0:LEAVES, :])
         table[LEAVES : 2 * LEAVES, :] = jnp.where(
@@ -108,22 +110,27 @@
     )
     most = jnp.broadcast_to(jnp.max(most, 0, keepdims=True), (8, 128))
     table[2 * LEAVES :, :] = most.astype(jnp.int32)
-    move = pltpu.make_async_copy(table, scal, sem)
-    move.start()
-    bring.wait()
-
+
+
+def joined_of(feat, rows, t):
+    row = iota((16, CHUNK), 0)
+    goal, tag = rows[t, 1:2, :], rows[t, 2:3, :]
+    extra = jnp.where(row == 0, goal, jnp.where(row == 1, tag, 0.0)).astype(BF)
+    return jnp.concatenate([feat[:, pl.ds(pl.multiple_of(t * CHUNK, CHUNK), CHUNK)], extra], 0)
+
+
+def sort_all(feat, rows, ybuf):
     def sort(t, _):
+        place = rows[t, 0:1, :].astype(jnp.int32)
+        chosen = (iota((CHUNK, CHUNK), 0) == place).astype(F32).astype(BF)
         start = pl.multiple_of(t * CHUNK, CHUNK)
-        row = iota((16, CHUNK), 0)
-        place, goal, tag = rows[t, 0:1, :], rows[t, 1:2, :], rows[t, 2:3, :]
-        extra = jnp.where(row == 0, goal, jnp.where(row == 1, tag, 0.0)).astype(BF)
-        joined = jnp.concatenate([feat[:, pl.ds(start, CHUNK)], extra], 0)
-        chosen = (iota((CHUNK, CHUNK), 0) == place.astype(jnp.int32)).astype(F32).astype(BF)
-        ybuf[pl.ds(start, CHUNK), :] = dot_nt(chosen, joined)
+        ybuf[pl.ds(start, CHUNK), :] = dot_nt(chosen, joined_of(feat, rows, t))
         return 0
 
     lax.fori_loop(0, CHUNKS, sort, 0, unroll=8)
-    move.wait()
+
+
+def merge_all(scal, ybuf, zbuf):
     widest = scal[2 * LEAVES, 0]
 
     @pl.when(widest <= WINDOW)
@@ -155,6 +162,93 @@
             return 0
 
         lax.fori_loop(0, CHUNKS * LEAVES, merge, 0)
+
+
+def pack_kernel(
+    feat_hbm, target, owner, zbuf, feat, goals, rows, ybuf, table, scal, sem, feat_sem
+):
+    bring = pltpu.make_async_copy(feat_hbm, feat, feat_sem)
+    bring.start()
+    rank_all(target, owner, goals, rows, table)
+    move = pltpu.make_async_copy(table, scal, sem)
+    move.start()
+    bring.wait()
+    sort_all(feat, rows, ybuf)
+    move.wait()
+    merge_all(scal, ybuf, zbuf)
+
+
+def merge_kernel(ybuf, table, zbuf, scal, sem):
+    move = pltpu.make_async_copy(table, scal, sem)
+    move.start()
+    move.wait()
+    merge_all(scal, ybuf, zbuf)
+
+
+def prepare_kernel(
+    feat_hbm, target, owner, pivots, ybuf, table, slots, most,
+    feat, goals, rows, held, picks, feat_sem, s_v, r_v, s_s, r_s,
+):
+    leaf = lax.axis_index("leaf")
+    block = leaf * COLS + lax.axis_index("col")
+    barrier = pltpu.get_barrier_semaphore()
+    each(LEAVES, lambda k: pl.semaphore_signal(barrier, inc=1, **mate(k)))
+    bring = pltpu.make_async_copy(feat_hbm, feat, feat_sem)
+    bring.start()
+    rank_all(target, owner, goals, rows, table)
+
+    def send_pivots(k):
+        return remote(pivots, held.at[k], (s_v, r_v), k, mate(k))
+
+    def send_slots(k):
+        return remote(picks.at[k], slots.at[k], (s_s, r_s), k, mate(k))
+
+    held[0] = pivots[...]
+    pl.semaphore_wait(barrier, LEAVES - 1)
+    each(LEAVES, lambda k: send_pivots(k).start())
+    each(LEAVES, lambda k: send_pivots(k).wait_recv())
+
+    place = jnp.concatenate([held[(LEAVES - b) % LEAVES] for b in range(LEAVES)], 0)
+    home = place % ROWS // PACKET
+    number = ((leaf + iota((LEAVES, RANK), 0)) % LEAVES) * 8 + place // ROWS
+    number = (number * PACKET + place % PACKET).astype(F32)
+    valid = home == block
+    order = dot(valid.astype(F32).astype(BF), ordering())
+    order = jnp.where(valid, order, -1.0)
+
+    def spread(table):
+        return jnp.concatenate(
+            [jnp.broadcast_to(table[b : b + 1], (SLOTS, RANK)) for b in range(LEAVES)], 0
+        )
+
+    shape = (LEAVES * SLOTS, RANK)
+    hit = spread(order) == (iota(shape, 0) % SLOTS).astype(F32)
+    wanted = jnp.sum(jnp.where(hit, spread(number) + 1.0, 0.0), 1, keepdims=True) - 1.0
+    which = jnp.sum(jnp.where(hit, iota(shape, 1).astype(F32) + 1.0, 0.0), 1, keepdims=True) - 1.0
+    wanted = jnp.broadcast_to(wanted, (LEAVES * SLOTS, CHUNK))
+    bring.wait()
+
+    def take(t, total):
+        chosen = (wanted == rows[t, 3:4, :]).astype(F32).astype(BF)
+        fill = jnp.zeros((128 - WIDE, CHUNK), BF)
+        return total + dot_nt(chosen, jnp.concatenate([joined_of(feat, rows, t), fill], 0))
+
+    shape = (LEAVES * SLOTS, 128)
+    taken = lax.fori_loop(0, CHUNKS, take, jnp.zeros(shape, F32), unroll=4)
+    taken = jnp.where(iota(shape, 1) == WHICH, which, taken).astype(BF)
+    for b in range(LEAVES):
+        picks[b] = taken[b * SLOTS : (b + 1) * SLOTS]
+    slots[0] = picks[0]
+    each(LEAVES, lambda k: send_slots(k).start())
+    sort_all(feat, rows, ybuf)
+
+    largest = jnp.zeros((OWNERS, 1), F32)
+    for b in range(LEAVES):
+        inside = (iota((OWNERS, RANK), 0) == home[b : b + 1]).astype(F32)
+        largest = jnp.maximum(largest, jnp.sum(inside, 1, keepdims=True))
+    most[...] = jnp.broadcast_to(jnp.max(largest, 0, keepdims=True), (8, 128))
+    each(LEAVES, lambda k: send_slots(k).wait_recv())
+    each(LEAVES, lambda k: (send_pivots(k).wait_send(), send_slots(k).wait_send()))
 
 
 def in_hbm(*arrays):
@@ -182,6 +276,44 @@
     )(*in_hbm(features, targets, owner))
 
 
+def prepare(features, targets, owner, pivots):
+    return pl.pallas_call(
+        prepare_kernel,
+        out_shape=(
+            pltpu.VMEM((ROWS + WINDOW, WIDE), F32),
+            pltpu.VMEM((40, 128), jnp.int32),
+            pltpu.VMEM((LEAVES, SLOTS, 128), BF),
+            jax.ShapeDtypeStruct((8, 128), F32),
+        ),
+        in_specs=[ANYWHERE, VMEM, VMEM, VMEM],
+        out_specs=[VMEM] * 4,
+        scratch_shapes=[
+            pltpu.VMEM((F, ROWS), BF),
+            pltpu.VMEM((ROWS // 128, 128), F32),
+            pltpu.VMEM((CHUNKS, 8, CHUNK), F32),
+            pltpu.VMEM((LEAVES, 1, RANK), jnp.int32),
+            pltpu.VMEM((LEAVES, SLOTS, 128), BF),
+            pltpu.SemaphoreType.DMA,
+            *dma(LEAVES),
+            *dma(LEAVES),
+        ],
+        compiler_params=params(0),
+        name="prepare",
+    )(*in_hbm(features, targets, owner, pivots))
+
+
+def merge(ybuf, table):
+    return pl.pallas_call(
+        merge_kernel,
+        out_shape=pltpu.VMEM((LEAVES * REGION, WIDE), F32),
+        in_specs=[VMEM] * 2,
+        out_specs=VMEM,
+        scratch_shapes=[pltpu.SMEM((40, 128), jnp.int32), pltpu.SemaphoreType.DMA],
+        compiler_params=params(),
+        name="merge",
+    )(ybuf, table)
+
+
 def split3(x):
     high = x.astype(BF)
     rest = x - high.astype(F32)
@@ -268,7 +400,7 @@
 
 
 def exchange_kernel(
-    merged, ridge, pivots_hbm, scales_hbm, parent_hbm, top_hbm, out_share, out_top, out_rhs,
+    early, merged, slots, ridge, pivots_hbm, scales_hbm, parent_hbm, top_hbm, out_share, out_top, out_rhs,
     pivots, scales, parent, top, spare, feat, aux, rx, ra, hot, side, sk, mine, sk4, left,
     even, odd, other_even, other_odd, gram, couple, rows, columns, fours, index, tops,
     pg, gr, pc, cr, pt, qr, rs, rr, t4, r4,
@@ -306,10 +438,25 @@
     def send_aux(k):
         return remote(aux.at[k], ra.at[k], (s_a, r_a), k, mate(k))
 
+    def send_skel(k):
+        return remote(sk.at[0], sk.at[k], (s_k, r_k), k, beside(k))
+
+    if early:
+        came = jnp.concatenate([slots[b] for b in range(LEAVES)], 0).astype(F32)
+        chosen = came[:, WHICH : WHICH + 1] == iota((LEAVES * SLOTS, RANK), 1).astype(F32)
+        picked = dot(came.T[:F].astype(BF), chosen.astype(F32).astype(BF))
+        sk[0] = picked.astype(BF)
+
     def four(j, _):
         for r in range(1, 5):
             turn((4 * j + r) % LEAVES)
-        pl.when(j == 0)(lambda: pl.semaphore_wait(barrier, LEAVES + COLS - 2))
+
+        @pl.when(j == 0)
+        def begin():
+            pl.semaphore_wait(barrier, LEAVES + COLS - 2)
+            if early:
+                each(COLS, lambda k: send_skel(k).start())
+
         for send in (send_aux, send_feat):
             for r in range(1, 4):
                 send(4 * j + r).start()
@@ -328,30 +475,6 @@
     scale = inverse * inverse * LOG2E
     scale2 = across(scale, RANK)
     scale4 = across(scale, PER)
-
-    place = pivots[...]
-    within = place % ROWS
-    block = within // PACKET
-    key = (block // COLS) * PER + (place // ROWS) * PACKET + within % PACKET
-    holder = block % COLS
-    crossed = (block // COLS) // 8 != leaf // 8
-    holder = jnp.where(crossed, holder + 1 - 2 * (holder % 2), holder)
-    key = jnp.where(holder == col, key, -PER)
-    key = across(to_column(key.astype(F32)), PER)
-
-    def mark(k):
-        source = (leaf + LEAVES - k) % LEAVES
-        tags = ra[k, 4:8, :]
-        tag = jnp.concatenate([tags[r : r + 1] for r in range(4)], 1)
-        wanted = tag + (PER // 2 + source * PER).astype(F32)
-        hot[k] = (key == wanted).astype(F32).astype(BF)
-
-    def mark_next(k, _):
-        pl.when(k > 0)(lambda: send_aux(k).wait_recv())
-        mark(k)
-        return 0
-
-    lax.fori_loop(0, LEAVES, mark_next, 0)
 
     index[...] = top_index(parent, top, leaf // 4)
     index2 = across(index[...], 2 * RANK)
@@ -365,31 +488,53 @@
     chosen = across(index[...], 4 * RANK) == iota((RANK, 4 * RANK), 1).astype(F32)
     fours[...] = chosen.astype(F32).astype(BF)
 
-    def pick(j, total):
-        for r in range(4):
-            k = 4 * j + r
-            if r:
-                send_feat(k).wait_recv()
-            else:
-                pl.when(k > 0)(lambda: send_feat(k).wait_recv())
-        for r in range(4):
-            total = total + dot_nt(hot[4 * j + r], rx[4 * j + r])
-        return total
-
-    picked = lax.fori_loop(0, LEAVES // 4, pick, jnp.zeros((RANK, F), F32))
-    picked = jnp.concatenate([picked, jnp.zeros((RANK, 128 - F), F32)], 1).T[:F]
-    sk[0] = picked.astype(BF)
-
-    def send_skel(k):
-        return remote(sk.at[0], sk.at[k], (s_k, r_k), k, beside(k))
-
-    each(COLS, lambda k: send_skel(k).start())
-
     def norms(k, _):
         side[k] = point_side(rx[k].astype(F32), scale4)
         return 0
 
-    lax.fori_loop(0, LEAVES, norms, 0)
+    if not early:
+        place = pivots[...]
+        within = place % ROWS
+        block = within // PACKET
+        key = (block // COLS) * PER + (place // ROWS) * PACKET + within % PACKET
+        holder = block % COLS
+        crossed = (block // COLS) // 8 != leaf // 8
+        holder = jnp.where(crossed, holder + 1 - 2 * (holder % 2), holder)
+        key = jnp.where(holder == col, key, -PER)
+        key = across(to_column(key.astype(F32)), PER)
+
+        def mark(k):
+            source = (leaf + LEAVES - k) % LEAVES
+            tags = ra[k, 4:8, :]
+            tag = jnp.concatenate([tags[r : r + 1] for r in range(4)], 1)
+            wanted = tag + (PER // 2 + source * PER).astype(F32)
+            hot[k] = (key == wanted).astype(F32).astype(BF)
+
+        def mark_next(k, _):
+            pl.when(k > 0)(lambda: send_aux(k).wait_recv())
+            mark(k)
+            return 0
+
+        lax.fori_loop(0, LEAVES, mark_next, 0)
+
+        def pick(j, total):
+            for r in range(4):
+                k = 4 * j + r
+                if r:
+                    send_feat(k).wait_recv()
+                else:
+                    pl.when(k > 0)(lambda: send_feat(k).wait_recv())
+            for r in range(4):
+                total = total + dot_nt(hot[4 * j + r], rx[4 * j + r])
+            return total
+
+        picked = lax.fori_loop(0, LEAVES // 4, pick, jnp.zeros((RANK, F), F32))
+        picked = jnp.concatenate([picked, jnp.zeros((RANK, 128 - F), F32)], 1).T[:F]
+        sk[0] = picked.astype(BF)
+
+        each(COLS, lambda k: send_skel(k).start())
+
+        lax.fori_loop(0, LEAVES, norms, 0)
 
     def add_skel(k, total):
         send_skel(k).wait_recv()
@@ -426,11 +571,20 @@
     last = LEAVES // 2 - 1
 
     def own_two(j, _):
+        if early:
+            pl.when(j > 0)(lambda: receive(2 * j))
+            receive(2 * j + 1)
+            norms(2 * j, 0)
+            norms(2 * j + 1, 0)
         own_of(2 * j, even.at[j])
         gram_of(odd.at[(j + last) % (last + 1)])
         own_of(2 * j + 1, odd.at[j])
         gram_of(even.at[j])
         return 0
+
+    def receive(k):
+        send_aux(k).wait_recv()
+        send_feat(k).wait_recv()
 
     def other_two(j, _):
         block_of(2 * j, other_even, RANK)
@@ -443,9 +597,6 @@
     couple[...] = jnp.zeros_like(couple)
     odd[last] = jnp.zeros((RANK + 16, PER), BF)
     other_odd[...] = jnp.zeros_like(other_odd)
-    lax.fori_loop(0, last + 1, own_two, 0)
-    gram_of(odd.at[last])
-
     def send_gram(k):
         return remote(pg.at[(col + k) % COLS], gr.at[k], (s_p, r_p), k, beside(k))
 
@@ -458,21 +609,33 @@
     def send_rhs(k):
         return remote(rs, rr.at[k], (s_r, r_r), k, beside(k))
 
-    part = gram[0:RANK, :].astype(BF)
-    for k in range(COLS):
-        pg[k] = part[k * SLAB : (k + 1) * SLAB]
-    rhs = gram[RANK : RANK + 1, :]
-    rhs = jnp.sum(dot_nt(stack16(split3(rhs), RANK), rows[...]), 0, keepdims=True)
-    rs[...] = jnp.zeros_like(rs)
-    rs[0:1, :] = rhs[:, :128]
-    rs[1:2, :] = rhs[:, 128:]
-    each(COLS, lambda k: send_gram(k).start())
-    each(COLS, lambda k: send_rhs(k).start())
-    tops[...] = dot_nt(dot(rows[...], part).astype(BF), columns[:, 0:RANK])
-
-    each(4, lambda k: remote(mine, sk4.at[(quarter + 4 - k) % 4], (s_4, r_4), k, cousin(k)).wait_recv())
-    left[RANK:, :] = skel_side(sk4[sibling].astype(F32), scale2)
-    lax.fori_loop(0, last + 1, other_two, 0)
+    def sibling_side():
+        each(4, lambda k: remote(mine, sk4.at[(quarter + 4 - k) % 4], (s_4, r_4), k, cousin(k)).wait_recv())
+        left[RANK:, :] = skel_side(sk4[sibling].astype(F32), scale2)
+
+    def give_gram():
+        gram_of(odd.at[last])
+        part = gram[0:RANK, :].astype(BF)
+        for k in range(COLS):
+            pg[k] = part[k * SLAB : (k + 1) * SLAB]
+        rhs = gram[RANK : RANK + 1, :]
+        rhs = jnp.sum(dot_nt(stack16(split3(rhs), RANK), rows[...]), 0, keepdims=True)
+        rs[...] = jnp.zeros_like(rs)
+        rs[0:1, :] = rhs[:, :128]
+        rs[1:2, :] = rhs[:, 128:]
+        each(COLS, lambda k: send_gram(k).start())
+        each(COLS, lambda k: send_rhs(k).start())
+        tops[...] = dot_nt(dot(rows[...], part).astype(BF), columns[:, 0:RANK])
+
+    def half(h, _):
+        pairs = LEAVES // 4
+        lax.fori_loop(pairs * h, pairs * (h + 1), own_two, 0)
+        pl.when(h == 0)(sibling_side)
+        pl.when(h == 1)(give_gram)
+        lax.fori_loop(pairs * h, pairs * (h + 1), other_two, 0)
+        return 0
+
+    lax.fori_loop(0, 2, half, 0)
     couple_of(other_odd, odd.at[last])
 
     part = couple[...].astype(BF)
@@ -550,11 +713,11 @@
 SHAPES = ((1, SLAB, 2 * RANK), (1, SLAB, RANK), (1, RANK))
 
 
-def exchange(merged, ridge, *smalls):
+def exchange(early, number, merged, slots, ridge, *smalls):
     return pl.pallas_call(
-        exchange_kernel,
+        functools.partial(exchange_kernel, early),
         out_shape=tuple(pltpu.VMEM(shape, F32) for shape in SHAPES),
-        in_specs=[VMEM, pl.BlockSpec(memory_space=pltpu.SMEM)] + [ANYWHERE] * 4,
+        in_specs=[VMEM, VMEM, pl.BlockSpec(memory_space=pltpu.SMEM)] + [ANYWHERE] * 4,
         out_specs=[VMEM] * 3,
         scratch_shapes=[
             pltpu.VMEM((1, RANK), jnp.int32),
@@ -605,9 +768,9 @@
             *dma(4),
             pltpu.SemaphoreType.DMA((4,)),
         ],
-        compiler_params=params(0, 40),
+        compiler_params=params(number, 40),
         name="exchange",
-    )(merged, ridge, *in_hbm(*smalls))
+    )(merged, slots, ridge, *in_hbm(*smalls))
 
 
 def emit_kernel(*refs):
@@ -632,9 +795,16 @@
 
 
 def local(features, targets, owner, length_scales, ridge, leaf_pivots, parent_pivots, top_pivots):
-    merged = pack(features, targets.reshape(ROWS // 128, 128), owner.reshape(ROWS // 128, 128))
+    samples = (features, targets.reshape(ROWS // 128, 128), owner.reshape(ROWS // 128, 128))
     smalls = (leaf_pivots, length_scales.reshape(1, F), parent_pivots, top_pivots)
-    return tuple(emit(exchange(merged, ridge, *smalls)))
+    ybuf, table, slots, most = prepare(*samples, leaf_pivots)
+    results = exchange(True, 1, merge(ybuf, table), slots, ridge, *smalls)
+
+    def again():
+        none = jnp.zeros((LEAVES, SLOTS, 128), BF)
+        return tuple(emit(exchange(False, 2, pack(*samples), none, ridge, *smalls)))
+
+    return lax.cond(most[0, 0] > SLOTS, again, lambda: tuple(emit(results)))
 
 
 def solution(mesh):

time: 54.1 us -> 59.9 us (1.11)
  Pallas kernels: 52.6 us -> 56.8 us
  between operations: 1.29 us -> 2.13 us
    pallas_call x2 -> x3, Pallas kernels: 52 us -> 56.2 us  [the longest x1 32.4 us: exchange(): pl.pallas_call(functools.partial(exchange_kernel, early), out_shape=tuple...]
where the time goes in v4:
time: 59.9 us; the launch traced here: 59.7 us
  Pallas kernels  56.8 us (95%)
  between operations  2.13 us (4%)
    pallas_call x1, Pallas kernels, exchange(): pl.pallas_call(functools.partial(exchange_kernel, early), out_shape=tuple...  32.4 us
    pallas_call x1, Pallas kernels, prepare(): pl.pallas_call(prepare_kernel, out_shape=(pltpu.VMEM((ROWS + WINDOW, WIDE...  20.9 us
    pallas_call x1, Pallas kernels, merge(): pl.pallas_call(merge_kernel, out_shape=pltpu.VMEM((LEAVES * REGION, WIDE)...  2.85 us

profile of v4, /device:TPU:1, one launch (start us, length us, event | category | flops | bytes accessed | tf_op | source)
XLA Modules:
  0.0 59.7 jit_solution(9836685575871875236)
XLA Ops:
  0.6 20.9 %prepare.1 = (f32[8232,64]{1,0:T(8,128)S(1)}, s32[40,128]{1,0:T(8,128)S(1)}, bf16[16,16,128]{2,1,0:T(8,128)(2,1)S(1)}, f32[8,128]{1,0:T(8,128)S(1)}) custom-call(bf16[48,8192]{1,0:T(8,128)(2,1)} %feat_hbm.1, bf16[64,128]{1,0:T(8,128)(2,1)} %bitcast.6, s32[64,128]{1,0:T(8,128)} %bitcast.4, s32[1,256]{1,0:T(1,128)} %pivots_hbm.1), custom_call_target="tpu_custom_call" | custom-call | tf_op jit(solution)/shard_map/prepare/pallas_call | solution.py:280
  21.5 0.5 slice.3
  22.7 2.9 %merge.1.merged = f32[8832,64]{1,0:T(8,128)S(1)} custom-call(f32[8232,64]{1,0:T(8,128)S(1)} %get-tuple-element.44.ybuf, s32[40,128]{1,0:T(8,128)S(1)} %get-tuple-element.45.table), custom_call_target="tpu_custom_call" | custom-call | tf_op jit(solution)/shard_map/merge/pallas_call | solution.py:306
  26.2 32.4 %exchange.3 = (f32[1,32,512]{2,1,0:T(8,128)S(1)}, f32[1,32,256]{2,1,0:T(8,128)S(1)}, f32[1,256]{1,0:T(1,128)S(1)}) custom-call(f32[8832,64]{1,0:T(8,128)S(1)} %merge.1.merged, bf16[16,16,128]{2,1,0:T(8,128)(2,1)S(1)} %get-tuple-element.46.slots, f32[1]{0:T(128)S(6)} %copy.23.ridge, s32[1,256]{1,0:T(1,128)} %pivots_hbm.1, f32[1,48]{1,0:T(1,128)} %bitcast.8, ...), custom_call_target="tpu_custom_call" | custom-call | tf_op jit(solution)/shard_map/exchange/pallas_call | solution.py:717
  58.6 0.9 %conditional.1 = ((f32[1,32,512]{2,1,0:T(8,128)}, f32[1,32,256]{2,1,0:T(8,128)}, f32[1,256]{1,0:T(1,128)})) conditional(s32[]{:T(128)} %bitcast.2, (f32[1,32,512]{2,1,0:T(8,128)S(1)}, f32[1,32,256]{2,1,0:T(8,128)S(1)}, f32[1,256]{1,0:T(1,128)S(1)}) %exchange.3, (bf16[48,8192]{1,0:T(8,128)(2,1)}, bf16[64,128]{1,0:T(8,128)(2,1)}, s32[64,128]{1,0:T(8,128)}, ...), branch_computations={%region_0.0_spmd, %region_1.0_spmd} | conditional | bytes 65546 | solution.py:807
  58.6 0.7 %emit.2 = (f32[1,32,512]{2,1,0:T(8,128)}, f32[1,32,256]{2,1,0:T(8,128)}, f32[1,256]{1,0:T(1,128)}) custom-call(f32[1,32,512]{2,1,0:T(8,128)S(1)} %get-tuple-element.22.refs_0_, f32[1,32,256]{2,1,0:T(8,128)S(1)} %get-tuple-element.23.refs_1_, f32[1,256]{1,0:T(1,128)S(1)} %get-tuple-element.24.refs_2_), custom_call_target="tpu_custom_call" | custom-call | tf_op jit(solution)/shard_map/cond/branch_0_fun/emit/pallas_call | solution.py:786

commit v5 on v3

--- a/solution.py
+++ b/solution.py
@@ -18,6 +18,7 @@
 PER = ROWS // LEAVES
 CHUNK = 256
 CHUNKS = ROWS // CHUNK
+GROUP = 8
 WINDOW = 40
 REGION = PER + WINDOW
 WIDE = 64
@@ -63,48 +64,57 @@
 
 
 def pack_kernel(
-    feat_hbm, target, owner, zbuf, feat, goals, rows, ybuf, table, scal, sem, feat_sem
+    feat_hbm, target, owner, zbuf, feat, goals, rows, cums, ybuf, table, scal, sem, feat_sem
 ):
     bring = pltpu.make_async_copy(feat_hbm, feat, feat_sem)
     bring.start()
     goals[...] = target[...].astype(F32)
     before = (iota((CHUNK, CHUNK), 0) < iota((CHUNK, CHUNK), 1)).astype(F32).astype(BF)
-    weights = jnp.concatenate([before, jnp.ones((CHUNK, 128), BF)], 1)
     lane = iota((LEAVES, 128), 1)
-
-    def ranks(t, carry):
+    kinds = OWNERS + 2 * LEAVES
+
+    def ranks(group, carry):
         seen, seen_leaf, most = carry
-        own = row_pair(owner[pl.ds(2 * t, 2), :])
-        leaf = own // 8
-        is_own = iota((OWNERS, CHUNK), 0) == own
-        is_leaf = iota((LEAVES, CHUNK), 0) == leaf
-        is_after = iota((LEAVES, CHUNK), 0) > leaf
-        marks = jnp.concatenate(
-            [m.astype(F32).astype(BF) for m in (is_own, is_leaf, is_after)], 0
-        )
-        sums = dot(marks, weights)
-        counts = sums[:OWNERS, CHUNK:]
-        leaf_counts = sums[OWNERS : OWNERS + LEAVES, CHUNK:]
-        base = sums[OWNERS + LEAVES :, CHUNK:]
-        prior = sums[:OWNERS, :CHUNK] + jnp.concatenate([seen, seen], 1)
-        rank = jnp.sum(jnp.where(is_own, prior, 0.0), 0, keepdims=True)
-        place = sums[OWNERS : OWNERS + LEAVES, :CHUNK] + jnp.concatenate([base, base], 1)
-        place = jnp.sum(jnp.where(is_leaf, place, 0.0), 0, keepdims=True)
-        tag = (own % 8).astype(F32) * PACKET + rank - (PER // 2)
-        rows[t, 0:1, :] = place
-        rows[t, 1:2, :] = row_pair(goals[pl.ds(2 * t, 2), :])
-        rows[t, 2:3, :] = tag
-        here = lane == t
-        table[0:LEAVES, :] = jnp.where(here, seen_leaf.astype(jnp.int32), table[0:LEAVES, :])
-        table[LEAVES : 2 * LEAVES, :] = jnp.where(
-            here, base.astype(jnp.int32), table[LEAVES : 2 * LEAVES, :]
-        )
-        return seen + counts, seen_leaf + leaf_counts, jnp.maximum(most, leaf_counts)
+        owners = []
+        marks = []
+        for r in range(GROUP):
+            own = row_pair(owner[pl.ds(2 * (group * GROUP + r), 2), :])
+            leaf = own // 8
+            owners.append(own)
+            marks.append((iota((OWNERS, CHUNK), 0) == own).astype(F32).astype(BF))
+            marks.append((iota((LEAVES, CHUNK), 0) == leaf).astype(F32).astype(BF))
+            marks.append((iota((LEAVES, CHUNK), 0) > leaf).astype(F32).astype(BF))
+        cums[...] = dot(jnp.concatenate(marks, 0), before)
+        for r in range(GROUP):
+            t = group * GROUP + r
+            own = owners[r]
+            leaf = own // 8
+            sums = cums[kinds * r : kinds * (r + 1), :]
+            final = jnp.concatenate([m[:, CHUNK - 1 :].astype(F32) for m in marks[3 * r : 3 * r + 3]], 0)
+            totals = sums[:, CHUNK - 1 :] + final
+            leaf_counts = totals[OWNERS : OWNERS + LEAVES]
+            base = totals[OWNERS + LEAVES :]
+            rank = jnp.where(iota((OWNERS, CHUNK), 0) == own, sums[:OWNERS] + seen, 0.0)
+            rank = jnp.sum(rank, 0, keepdims=True)
+            place = sums[OWNERS : OWNERS + LEAVES] + base
+            place = jnp.where(iota((LEAVES, CHUNK), 0) == leaf, place, 0.0)
+            rows[t, 0:1, :] = jnp.sum(place, 0, keepdims=True)
+            rows[t, 1:2, :] = row_pair(goals[pl.ds(2 * t, 2), :])
+            rows[t, 2:3, :] = (own % 8).astype(F32) * PACKET + rank - (PER // 2)
+            here = lane == t
+            table[0:LEAVES, :] = jnp.where(here, seen_leaf.astype(jnp.int32), table[0:LEAVES, :])
+            table[LEAVES : 2 * LEAVES, :] = jnp.where(
+                here, base.astype(jnp.int32), table[LEAVES : 2 * LEAVES, :]
+            )
+            seen = seen + totals[:OWNERS]
+            seen_leaf = seen_leaf + leaf_counts
+            most = jnp.maximum(most, leaf_counts)
+        return seen, seen_leaf, most
 
     table[0:LEAVES, :] = jnp.full((LEAVES, 128), PER, jnp.int32)
-    zero = jnp.zeros((LEAVES, 128), F32)
+    start = goals[0:16, 0:1] * 0.0
     _, _, most = lax.fori_loop(
-        0, CHUNKS, ranks, (jnp.zeros((OWNERS, 128), F32), zero, zero), unroll=16
+        0, CHUNKS // GROUP, ranks, (jnp.concatenate([start] * 8, 0), start, start), unroll=2
     )
     most = jnp.broadcast_to(jnp.max(most, 0, keepdims=True), (8, 128))
     table[2 * LEAVES :, :] = most.astype(jnp.int32)
@@ -171,6 +181,7 @@
             pltpu.VMEM((F, ROWS), BF),
             pltpu.VMEM((ROWS // 128, 128), F32),
             pltpu.VMEM((CHUNKS, 8, CHUNK), F32),
+            pltpu.VMEM((GROUP * (OWNERS + 2 * LEAVES), CHUNK), F32),
             pltpu.VMEM((ROWS + WINDOW, WIDE), F32),
             pltpu.VMEM((40, 128), jnp.int32),
             pltpu.SMEM((40, 128), jnp.int32),
@@ -270,7 +281,7 @@
 def exchange_kernel(
     merged, ridge, pivots_hbm, scales_hbm, parent_hbm, top_hbm, out_share, out_top, out_rhs,
     pivots, scales, parent, top, spare, feat, aux, rx, ra, hot, side, sk, mine, sk4, left,
-    even, odd, other_even, other_odd, gram, couple, rows, columns, fours, index, tops,
+    own_even, own_odd, even, odd, other_even, other_odd, gram, couple, rows, columns, fours, index, tops,
     pg, gr, pc, cr, pt, qr, rs, rr, t4, r4,
     s_f, r_f, s_a, r_a, s_k, r_k, s_4, r_4, s_p, r_p, s_c, r_c, s_o, r_o, s_r, r_r, s_t, r_t, s_q, r_q, local,
 ):
@@ -412,24 +423,25 @@
         power = dot(left[begin : begin + RANK, :], right)
         out[0:RANK, :] = jnp.exp2(jnp.minimum(power, 0.0)).astype(BF)
 
-    def own_of(k, out):
+    def own_of(k, out, turned):
         block_of(k, out, 0)
+        turned[...] = out[0:RANK, :].T
         value = jnp.concatenate([ra[k, r : r + 1, :] for r in range(4)], 1)
         out[RANK:, :] = jnp.broadcast_to(value, (16, PER)).astype(BF)
 
-    def gram_of(u):
-        gram[...] += dot_nt(u[...], u[0:RANK, :])
-
-    def couple_of(v, u):
-        couple[...] += dot_nt(v[...], u[0:RANK, :])
+    def gram_of(u, turned):
+        gram[...] += dot(u[...], turned[...])
+
+    def couple_of(v, turned):
+        couple[...] += dot(v[...], turned[...])
 
     last = LEAVES // 2 - 1
 
     def own_two(j, _):
-        own_of(2 * j, even.at[j])
-        gram_of(odd.at[(j + last) % (last + 1)])
-        own_of(2 * j + 1, odd.at[j])
-        gram_of(even.at[j])
+        own_of(2 * j, own_even, even.at[j])
+        gram_of(own_odd, odd.at[(j + last) % (last + 1)])
+        own_of(2 * j + 1, own_odd, odd.at[j])
+        gram_of(own_even, even.at[j])
         return 0
 
     def other_two(j, _):
@@ -441,10 +453,11 @@
 
     gram[...] = jnp.zeros_like(gram)
     couple[...] = jnp.zeros_like(couple)
-    odd[last] = jnp.zeros((RANK + 16, PER), BF)
+    odd[last] = jnp.zeros((PER, RANK), BF)
+    own_odd[...] = jnp.zeros_like(own_odd)
     other_odd[...] = jnp.zeros_like(other_odd)
     lax.fori_loop(0, last + 1, own_two, 0)
-    gram_of(odd.at[last])
+    gram_of(own_odd, odd.at[last])
 
     def send_gram(k):
         return remote(pg.at[(col + k) % COLS], gr.at[k], (s_p, r_p), k, beside(k))
@@ -496,6 +509,13 @@
     square = iota((RANK, RANK), 0) == iota((RANK, RANK), 1)
     tops[...] = jnp.where(crossing, value, 0.0) + jnp.where(square, ridge[0], 0.0)
 
+    def finish(sends):
+        return lambda k: [send(k).wait_send() for send in sends]
+
+    each(LEAVES, finish((send_aux, send_feat)))
+    each(COLS, finish((send_skel, send_gram, send_rhs)))
+    each(4, finish((send_four,)))
+
     def add_chosen(k, totals):
         send_chosen(k).wait_recv()
         send_rhs(k).wait_recv()
@@ -539,12 +559,8 @@
     out_top[0] = result
     out_rhs[...] = jnp.concatenate([rhs[0:1], rhs[1:2]], 1)
 
-    def finish(sends):
-        return lambda k: [send(k).wait_send() for send in sends]
-
-    each(LEAVES, finish((send_aux, send_feat)))
-    each(COLS, finish((send_skel, send_gram, send_couple, send_chosen, send_rhs)))
-    each(4, finish((send_four, send_top, send_top_rhs)))
+    each(COLS, finish((send_couple, send_chosen)))
+    each(4, finish((send_top, send_top_rhs)))
 
 
 SHAPES = ((1, SLAB, 2 * RANK), (1, SLAB, RANK), (1, RANK))
@@ -572,8 +588,10 @@
             pltpu.VMEM((F, RANK), BF),
             pltpu.VMEM((4, F, RANK), BF),
             pltpu.VMEM((2 * RANK, 256), BF),
-            pltpu.VMEM((LEAVES // 2, RANK + 16, PER), BF),
-            pltpu.VMEM((LEAVES // 2, RANK + 16, PER), BF),
+            pltpu.VMEM((RANK + 16, PER), BF),
+            pltpu.VMEM((RANK + 16, PER), BF),
+            pltpu.VMEM((LEAVES // 2, PER, RANK), BF),
+            pltpu.VMEM((LEAVES // 2, PER, RANK), BF),
             pltpu.VMEM((RANK, PER), BF),
             pltpu.VMEM((RANK, PER), BF),
             pltpu.VMEM((RANK + 16, RANK), F32),

time: 54.1 us -> 55 us (1.017)
  Pallas kernels: 52.6 us -> 53.6 us
where the time goes in v5:
time: 55 us; the launch traced here: 54.9 us
  Pallas kernels  53.6 us (97%)
  between operations  1.29 us (2%)
    pallas_call x1, Pallas kernels, exchange(): pl.pallas_call(exchange_kernel, out_shape=tuple((pltpu.VMEM(shape, F32) f...  45.8 us
    pallas_call x1, Pallas kernels, pack(): pl.pallas_call(pack_kernel, out_shape=pltpu.VMEM((LEAVES * REGION, WIDE),...  7.13 us

profile of v5, /device:TPU:1, one launch (start us, length us, event | category | flops | bytes accessed | tf_op | source)
XLA Modules:
  0.0 54.9 jit_solution(12896111381706399526)
XLA Ops:
  1.3 7.1 %pack.1.merged = f32[8832,64]{1,0:T(8,128)S(1)} custom-call(bf16[48,8192]{1,0:T(8,128)(2,1)} %feat_hbm.1, bf16[64,128]{1,0:T(8,128)(2,1)} %bitcast.4, s32[64,128]{1,0:T(8,128)} %bitcast.3), custom_call_target="tpu_custom_call" | custom-call | tf_op jit(solution)/shard_map/pack/pallas_call | solution.py:175
  8.4 45.8 %exchange.1 = (f32[1,32,512]{2,1,0:T(8,128)S(1)}, f32[1,32,256]{2,1,0:T(8,128)S(1)}, f32[1,256]{1,0:T(1,128)S(1)}) custom-call(f32[8832,64]{1,0:T(8,128)S(1)} %pack.1.merged, f32[1]{0:T(128)S(6)} %copy.11.ridge, s32[1,256]{1,0:T(1,128)} %pivots_hbm.1, f32[1,48]{1,0:T(1,128)} %bitcast.5, s32[8,256]{1,0:T(8,128)} %parent_hbm.1, s32[4,256]{1,0:T(4,128)} %top_hbm.1), custom_call_target="tpu_custom_call" | custom-call | tf_op jit(solution)/shard_map/exchange/pallas_call | solution.py:570
  54.2 0.7 %emit.1 = (f32[1,32,512]{2,1,0:T(8,128)}, f32[1,32,256]{2,1,0:T(8,128)}, f32[1,256]{1,0:T(1,128)}) custom-call(f32[1,32,512]{2,1,0:T(8,128)S(1)} %get-tuple-element.6.refs_0_, f32[1,32,256]{2,1,0:T(8,128)S(1)} %get-tuple-element.7.refs_1_, f32[1,256]{1,0:T(1,128)S(1)} %get-tuple-element.8.refs_2_), custom_call_target="tpu_custom_call" | custom-call | tf_op jit(solution)/shard_map/emit/pallas_call | solution.py:641

commit v6 on v4

--- a/solution.py
+++ b/solution.py
@@ -186,11 +186,8 @@
 
 
 def prepare_kernel(
-    feat_hbm, target, owner, pivots, ybuf, table, slots, most,
-    feat, goals, rows, held, picks, feat_sem, s_v, r_v, s_s, r_s,
+    feat_hbm, target, owner, pivots, ybuf, table, held, feat, goals, rows, feat_sem, s_v, r_v
 ):
-    leaf = lax.axis_index("leaf")
-    block = leaf * COLS + lax.axis_index("col")
     barrier = pltpu.get_barrier_semaphore()
     each(LEAVES, lambda k: pl.semaphore_signal(barrier, inc=1, **mate(k)))
     bring = pltpu.make_async_copy(feat_hbm, feat, feat_sem)
@@ -200,55 +197,12 @@
     def send_pivots(k):
         return remote(pivots, held.at[k], (s_v, r_v), k, mate(k))
 
-    def send_slots(k):
-        return remote(picks.at[k], slots.at[k], (s_s, r_s), k, mate(k))
-
     held[0] = pivots[...]
     pl.semaphore_wait(barrier, LEAVES - 1)
     each(LEAVES, lambda k: send_pivots(k).start())
-    each(LEAVES, lambda k: send_pivots(k).wait_recv())
-
-    place = jnp.concatenate([held[(LEAVES - b) % LEAVES] for b in range(LEAVES)], 0)
-    home = place % ROWS // PACKET
-    number = ((leaf + iota((LEAVES, RANK), 0)) % LEAVES) * 8 + place // ROWS
-    number = (number * PACKET + place % PACKET).astype(F32)
-    valid = home == block
-    order = dot(valid.astype(F32).astype(BF), ordering())
-    order = jnp.where(valid, order, -1.0)
-
-    def spread(table):
-        return jnp.concatenate(
-            [jnp.broadcast_to(table[b : b + 1], (SLOTS, RANK)) for b in range(LEAVES)], 0
-        )
-
-    shape = (LEAVES * SLOTS, RANK)
-    hit = spread(order) == (iota(shape, 0) % SLOTS).astype(F32)
-    wanted = jnp.sum(jnp.where(hit, spread(number) + 1.0, 0.0), 1, keepdims=True) - 1.0
-    which = jnp.sum(jnp.where(hit, iota(shape, 1).astype(F32) + 1.0, 0.0), 1, keepdims=True) - 1.0
-    wanted = jnp.broadcast_to(wanted, (LEAVES * SLOTS, CHUNK))
     bring.wait()
-
-    def take(t, total):
-        chosen = (wanted == rows[t, 3:4, :]).astype(F32).astype(BF)
-        fill = jnp.zeros((128 - WIDE, CHUNK), BF)
-        return total + dot_nt(chosen, jnp.concatenate([joined_of(feat, rows, t), fill], 0))
-
-    shape = (LEAVES * SLOTS, 128)
-    taken = lax.fori_loop(0, CHUNKS, take, jnp.zeros(shape, F32), unroll=4)
-    taken = jnp.where(iota(shape, 1) == WHICH, which, taken).astype(BF)
-    for b in range(LEAVES):
-        picks[b] = taken[b * SLOTS : (b + 1) * SLOTS]
-    slots[0] = picks[0]
-    each(LEAVES, lambda k: send_slots(k).start())
     sort_all(feat, rows, ybuf)
-
-    largest = jnp.zeros((OWNERS, 1), F32)
-    for b in range(LEAVES):
-        inside = (iota((OWNERS, RANK), 0) == home[b : b + 1]).astype(F32)
-        largest = jnp.maximum(largest, jnp.sum(inside, 1, keepdims=True))
-    most[...] = jnp.broadcast_to(jnp.max(largest, 0, keepdims=True), (8, 128))
-    each(LEAVES, lambda k: send_slots(k).wait_recv())
-    each(LEAVES, lambda k: (send_pivots(k).wait_send(), send_slots(k).wait_send()))
+    each(LEAVES, lambda k: (send_pivots(k).wait_send(), send_pivots(k).wait_recv()))
 
 
 def in_hbm(*arrays):
@@ -282,19 +236,15 @@
         out_shape=(
             pltpu.VMEM((ROWS + WINDOW, WIDE), F32),
             pltpu.VMEM((40, 128), jnp.int32),
-            pltpu.VMEM((LEAVES, SLOTS, 128), BF),
-            jax.ShapeDtypeStruct((8, 128), F32),
+            pltpu.VMEM((LEAVES, 1, RANK), jnp.int32),
         ),
         in_specs=[ANYWHERE, VMEM, VMEM, VMEM],
-        out_specs=[VMEM] * 4,
+        out_specs=[VMEM] * 3,
         scratch_shapes=[
             pltpu.VMEM((F, ROWS), BF),
             pltpu.VMEM((ROWS // 128, 128), F32),
             pltpu.VMEM((CHUNKS, 8, CHUNK), F32),
-            pltpu.VMEM((LEAVES, 1, RANK), jnp.int32),
-            pltpu.VMEM((LEAVES, SLOTS, 128), BF),
             pltpu.SemaphoreType.DMA,
-            *dma(LEAVES),
             *dma(LEAVES),
         ],
         compiler_params=params(0),
@@ -364,25 +314,38 @@
     return dict(device_id=(leaf, col), device_id_type=MESH)
 
 
+def rem(a, b):
+    return lax.rem(jnp.int32(a), jnp.int32(b))
+
+
+def div(a, b):
+    return lax.div(jnp.int32(a), jnp.int32(b))
+
+
 def mate(k):
     leaf, col = lax.axis_index("leaf"), lax.axis_index("col")
-    to = (leaf + k) % LEAVES
-    cross = (to // 8 + leaf // 8) % 2
-    return place_of(to, col + cross * (1 - 2 * (col % 2)))
+    to = rem(leaf + k, LEAVES)
+    cross = rem(div(to, 8) + div(leaf, 8), 2)
+    return place_of(to, col + cross * (1 - 2 * rem(col, 2)))
 
 
 def beside(k):
     leaf, col = lax.axis_index("leaf"), lax.axis_index("col")
-    return place_of(leaf, (col + k) % COLS)
+    return place_of(leaf, rem(col + k, COLS))
 
 
 def cousin(k):
     leaf, col = lax.axis_index("leaf"), lax.axis_index("col")
-    return place_of(leaf - leaf % 4 + (leaf + k) % 4, col)
+    return place_of(leaf - rem(leaf, 4) + rem(leaf + k, 4), col)
 
 
 def each(count, step, unroll=1):
     lax.fori_loop(1, count, lambda k, _: (step(k), 0)[1], 0, unroll=unroll)
+
+
+def turn_of(n):
+    odd = rem(n, 2)
+    return rem(odd * div(n + 1, 2) + (1 - odd) * (LEAVES - div(n, 2)), LEAVES)
 
 
 def remote(src, dst, sems, k, peer):
@@ -400,8 +363,8 @@
 
 
 def exchange_kernel(
-    early, merged, slots, ridge, pivots_hbm, scales_hbm, parent_hbm, top_hbm, out_share, out_top, out_rhs,
-    pivots, scales, parent, top, spare, feat, aux, rx, ra, hot, side, sk, mine, sk4, left,
+    early, merged, held, ridge, pivots_hbm, scales_hbm, parent_hbm, top_hbm, out_share, out_top, out_rhs, most,
+    pivots, scales, parent, top, spare, feat, aux, rx, ra, wants, small, got, hot, side, sk, mine, sk4, left,
     even, odd, other_even, other_odd, gram, couple, rows, columns, fours, index, tops,
     pg, gr, pc, cr, pt, qr, rs, rr, t4, r4,
     s_f, r_f, s_a, r_a, s_k, r_k, s_4, r_4, s_p, r_p, s_c, r_c, s_o, r_o, s_r, r_r, s_t, r_t, s_q, r_q, local,
@@ -424,13 +387,43 @@
 
     eye = (iota((WIDE, WIDE), 0) == iota((WIDE, WIDE), 1)).astype(F32).astype(BF)
 
+    if early:
+        place = jnp.concatenate([held[(LEAVES - b) % LEAVES] for b in range(LEAVES)], 0)
+        home = place % ROWS // PACKET
+        valid = home == leaf * COLS + col
+        number = (place // ROWS * PACKET + place % PACKET - PER // 2).astype(F32)
+        order = dot(valid.astype(F32).astype(BF), ordering())
+        order = jnp.where(valid, order, -1.0)
+
+        def spread(table):
+            return jnp.concatenate(
+                [jnp.broadcast_to(table[b : b + 1], (SLOTS, RANK)) for b in range(LEAVES)], 0
+            )
+
+        shape = (LEAVES * SLOTS, RANK)
+        hit = spread(order) == (iota(shape, 0) % SLOTS).astype(F32)
+        wanted = jnp.where(hit, spread(number) + PER, 0.0)
+        which = jnp.where(hit, iota(shape, 1).astype(F32) + 1.0, 0.0)
+        shape = (LEAVES * SLOTS, 128)
+        wants[0] = jnp.broadcast_to(jnp.sum(wanted, 1, keepdims=True) - PER, shape)
+        wants[1] = jnp.broadcast_to(jnp.sum(which, 1, keepdims=True) - 1.0, shape)
+
     def turn(k):
         start = pl.multiple_of((leaf + k) % LEAVES * REGION, 8)
         turned = dot_nt(eye, merged[pl.ds(start, PER), :].astype(BF))
         feat[k] = turned[:F].astype(BF)
-        aux[k] = jnp.concatenate(
-            [turned[F + r : F + r + 1, 128 * c : 128 * c + 128] for r in range(2) for c in range(4)], 0
+        goals, tags = (
+            [turned[F + r : F + r + 1, 128 * c : 128 * c + 128] for c in range(4)] for r in range(2)
         )
+        if early:
+            slots = pl.ds(pl.multiple_of(k * SLOTS, SLOTS), SLOTS)
+            chosen = (across(wants[0, slots, :], PER) == turned[F + 1 : F + 2]).astype(F32).astype(BF)
+            taken = dot_nt(chosen, jnp.concatenate([turned, turned], 0).astype(BF))
+            taken = jnp.where(iota((SLOTS, 128), 1) == WHICH, wants[1, slots, :], taken)
+            zero = jnp.zeros((12, 128), F32)
+            small[k] = jnp.concatenate([taken, *goals, zero], 0).astype(BF)
+        else:
+            aux[k] = jnp.concatenate(goals + tags, 0)
 
     def send_feat(k):
         return remote(feat.at[k], rx.at[k], (s_f, r_f), k, mate(k))
@@ -441,31 +434,23 @@
     def send_skel(k):
         return remote(sk.at[0], sk.at[k], (s_k, r_k), k, beside(k))
 
+    def send_small(k):
+        return remote(small.at[k], got.at[k], (s_a, r_a), k, mate(k))
+
+    def turn_four(j, _):
+        for r in range(4):
+            turn(4 * j + r)
+        return 0
+
+    lax.fori_loop(0, LEAVES // 4, turn_four, 0)
+    rx[0] = feat[0]
     if early:
-        came = jnp.concatenate([slots[b] for b in range(LEAVES)], 0).astype(F32)
-        chosen = came[:, WHICH : WHICH + 1] == iota((LEAVES * SLOTS, RANK), 1).astype(F32)
-        picked = dot(came.T[:F].astype(BF), chosen.astype(F32).astype(BF))
-        sk[0] = picked.astype(BF)
-
-    def four(j, _):
-        for r in range(1, 5):
-            turn((4 * j + r) % LEAVES)
-
-        @pl.when(j == 0)
-        def begin():
-            pl.semaphore_wait(barrier, LEAVES + COLS - 2)
-            if early:
-                each(COLS, lambda k: send_skel(k).start())
-
-        for send in (send_aux, send_feat):
-            for r in range(1, 4):
-                send(4 * j + r).start()
-            pl.when(j < 3)(lambda: send(4 * j + 4).start())
-        return 0
-
-    lax.fori_loop(0, LEAVES // 4, four, 0)
-    rx[0] = feat[0]
-    ra[0] = aux[0]
+        got[0] = small[0]
+    else:
+        ra[0] = aux[0]
+    pl.semaphore_wait(barrier, LEAVES + COLS - 2)
+    each(LEAVES, lambda n: (send_small if early else send_aux)(turn_of(n)).start())
+    lax.fori_loop(1, 9 if early else LEAVES, lambda n, _: (send_feat(turn_of(n)).start(), 0)[1], 0)
 
     for copy in smalls:
         copy.wait()
@@ -533,8 +518,21 @@
         sk[0] = picked.astype(BF)
 
         each(COLS, lambda k: send_skel(k).start())
-
         lax.fori_loop(0, LEAVES, norms, 0)
+    else:
+        each(LEAVES, lambda n: send_small(turn_of(n)).wait_recv())
+        came = jnp.concatenate([got[k, 0:SLOTS, :] for k in range(LEAVES)], 0).astype(F32)
+        chosen = came[:, WHICH : WHICH + 1] == iota((LEAVES * SLOTS, RANK), 1).astype(F32)
+        picked = dot(came.T[:F].astype(BF), chosen.astype(F32).astype(BF))
+        sk[0] = picked.astype(BF)
+        each(COLS, lambda k: send_skel(k).start())
+        lax.fori_loop(9, LEAVES, lambda n, _: (send_feat(turn_of(n)).start(), 0)[1], 0)
+
+        largest = jnp.zeros((OWNERS, 1), F32)
+        for b in range(LEAVES):
+            inside = (iota((OWNERS, RANK), 0) == home[b : b + 1]).astype(F32)
+            largest = jnp.maximum(largest, jnp.sum(inside, 1, keepdims=True))
+    most[0] = jnp.max(largest).astype(jnp.int32) if early else 0
 
     def add_skel(k, total):
         send_skel(k).wait_recv()
@@ -559,7 +557,8 @@
 
     def own_of(k, out):
         block_of(k, out, 0)
-        value = jnp.concatenate([ra[k, r : r + 1, :] for r in range(4)], 1)
+        value = got[k, SLOTS : 2 * SLOTS, :].astype(F32) if early else ra[k]
+        value = jnp.concatenate([value[r : r + 1] for r in range(4)], 1)
         out[RANK:, :] = jnp.broadcast_to(value, (16, PER)).astype(BF)
 
     def gram_of(u):
@@ -571,25 +570,22 @@
     last = LEAVES // 2 - 1
 
     def own_two(j, _):
+        k, l = turn_of(2 * j), turn_of(2 * j + 1)
         if early:
-            pl.when(j > 0)(lambda: receive(2 * j))
-            receive(2 * j + 1)
-            norms(2 * j, 0)
-            norms(2 * j + 1, 0)
-        own_of(2 * j, even.at[j])
-        gram_of(odd.at[(j + last) % (last + 1)])
-        own_of(2 * j + 1, odd.at[j])
+            pl.when(j > 0)(lambda: send_feat(k).wait_recv())
+            send_feat(l).wait_recv()
+            norms(k, 0)
+            norms(l, 0)
+        own_of(k, even.at[j])
+        gram_of(odd.at[rem(j + last, last + 1)])
+        own_of(l, odd.at[j])
         gram_of(even.at[j])
         return 0
 
-    def receive(k):
-        send_aux(k).wait_recv()
-        send_feat(k).wait_recv()
-
     def other_two(j, _):
-        block_of(2 * j, other_even, RANK)
-        couple_of(other_odd, odd.at[(j + last) % (last + 1)])
-        block_of(2 * j + 1, other_odd, RANK)
+        block_of(turn_of(2 * j), other_even, RANK)
+        couple_of(other_odd, odd.at[rem(j + last, last + 1)])
+        block_of(turn_of(2 * j + 1), other_odd, RANK)
         couple_of(other_even, even.at[j])
         return 0
 
@@ -659,6 +655,13 @@
     square = iota((RANK, RANK), 0) == iota((RANK, RANK), 1)
     tops[...] = jnp.where(crossing, value, 0.0) + jnp.where(square, ridge[0], 0.0)
 
+    def finish(sends):
+        return lambda k: [send(k).wait_send() for send in sends]
+
+    each(LEAVES, finish((send_small if early else send_aux, send_feat)))
+    each(COLS, finish((send_skel, send_gram, send_rhs)))
+    each(4, finish((send_four,)))
+
     def add_chosen(k, totals):
         send_chosen(k).wait_recv()
         send_rhs(k).wait_recv()
@@ -702,23 +705,22 @@
     out_top[0] = result
     out_rhs[...] = jnp.concatenate([rhs[0:1], rhs[1:2]], 1)
 
-    def finish(sends):
-        return lambda k: [send(k).wait_send() for send in sends]
-
-    each(LEAVES, finish((send_aux, send_feat)))
-    each(COLS, finish((send_skel, send_gram, send_couple, send_chosen, send_rhs)))
-    each(4, finish((send_four, send_top, send_top_rhs)))
+    each(COLS, finish((send_couple, send_chosen)))
+    each(4, finish((send_top, send_top_rhs)))
 
 
 SHAPES = ((1, SLAB, 2 * RANK), (1, SLAB, RANK), (1, RANK))
 
 
-def exchange(early, number, merged, slots, ridge, *smalls):
+def exchange(early, number, merged, held, ridge, *smalls):
     return pl.pallas_call(
         functools.partial(exchange_kernel, early),
-        out_shape=tuple(pltpu.VMEM(shape, F32) for shape in SHAPES),
+        out_shape=(
+            *(pltpu.VMEM(shape, F32) for shape in SHAPES),
+            jax.ShapeDtypeStruct((1,), jnp.int32),
+        ),
         in_specs=[VMEM, VMEM, pl.BlockSpec(memory_space=pltpu.SMEM)] + [ANYWHERE] * 4,
-        out_specs=[VMEM] * 3,
+        out_specs=[VMEM] * 3 + [pl.BlockSpec(memory_space=pltpu.SMEM)],
         scratch_shapes=[
             pltpu.VMEM((1, RANK), jnp.int32),
             pltpu.VMEM((1, F), F32),
@@ -729,6 +731,9 @@
             pltpu.VMEM((LEAVES, 8, 128), F32),
             pltpu.VMEM((LEAVES, F, PER), BF),
             pltpu.VMEM((LEAVES, 8, 128), F32),
+            pltpu.VMEM((2, LEAVES * SLOTS, 128), F32),
+            pltpu.VMEM((LEAVES, 2 * SLOTS, 128), BF),
+            pltpu.VMEM((LEAVES, 2 * SLOTS, 128), BF),
             pltpu.VMEM((LEAVES, RANK, PER), BF),
             pltpu.VMEM((LEAVES, 16, PER), BF),
             pltpu.VMEM((COLS, F, RANK), BF),
@@ -770,7 +775,7 @@
         ],
         compiler_params=params(number, 40),
         name="exchange",
-    )(merged, slots, ridge, *in_hbm(*smalls))
+    )(merged, held, ridge, *in_hbm(*smalls))
 
 
 def emit_kernel(*refs):
@@ -797,14 +802,14 @@
 def local(features, targets, owner, length_scales, ridge, leaf_pivots, parent_pivots, top_pivots):
     samples = (features, targets.reshape(ROWS // 128, 128), owner.reshape(ROWS // 128, 128))
     smalls = (leaf_pivots, length_scales.reshape(1, F), parent_pivots, top_pivots)
-    ybuf, table, slots, most = prepare(*samples, leaf_pivots)
-    results = exchange(True, 1, merge(ybuf, table), slots, ridge, *smalls)
+    ybuf, table, held = prepare(*samples, leaf_pivots)
+    *results, most = exchange(True, 1, merge(ybuf, table), held, ridge, *smalls)
 
     def again():
-        none = jnp.zeros((LEAVES, SLOTS, 128), BF)
-        return tuple(emit(exchange(False, 2, pack(*samples), none, ridge, *smalls)))
-
-    return lax.cond(most[0, 0] > SLOTS, again, lambda: tuple(emit(results)))
+        none = jnp.zeros((LEAVES, 1, RANK), jnp.int32)
+        return tuple(emit(exchange(False, 2, pack(*samples), none, ridge, *smalls)[:3]))
+
+    return lax.cond(most[0] > SLOTS, again, lambda: tuple(emit(results)))
 
 
 def solution(mesh):

time: 59.9 us -> 53.6 us (0.89)
  Pallas kernels: 56.8 us -> 51.6 us
    pallas_call x1, Pallas kernels: 20.9 us -> 12.7 us  [prepare(): pl.pallas_call(prepare_kernel, out_shape=(pltpu.VMEM((ROWS + WINDOW, WIDE...]
    pallas_call x1, Pallas kernels: 32.4 us -> 35.3 us  [exchange(): pl.pallas_call(functools.partial(exchange_kernel, early), out_shape=(*(pl...]
where the time goes in v6:
time: 53.6 us; the launch traced here: 53.4 us
  Pallas kernels  51.6 us (96%)
  between operations  1.86 us (3%)
    pallas_call x1, Pallas kernels, exchange(): pl.pallas_call(functools.partial(exchange_kernel, early), out_shape=(*(pl...  35.3 us
    pallas_call x1, Pallas kernels, prepare(): pl.pallas_call(prepare_kernel, out_shape=(pltpu.VMEM((ROWS + WINDOW, WIDE...  12.7 us
    pallas_call x1, Pallas kernels, merge(): pl.pallas_call(merge_kernel, out_shape=pltpu.VMEM((LEAVES * REGION, WIDE)...  2.85 us

profile of v6, /device:TPU:1, one launch (start us, length us, event | category | flops | bytes accessed | tf_op | source)
XLA Modules:
  0.0 53.4 jit_solution(14454770398967909315)
XLA Ops:
  0.6 12.7 %prepare.1 = (f32[8232,64]{1,0:T(8,128)S(1)}, s32[40,128]{1,0:T(8,128)S(1)}, s32[16,1,256]{2,1,0:T(1,128)S(1)}) custom-call(bf16[48,8192]{1,0:T(8,128)(2,1)} %feat_hbm.1, bf16[64,128]{1,0:T(8,128)(2,1)} %bitcast.6, s32[64,128]{1,0:T(8,128)} %bitcast.4, s32[1,256]{1,0:T(1,128)} %pivots_hbm.1), custom_call_target="tpu_custom_call" | custom-call | tf_op jit(solution)/shard_map/prepare/pallas_call | solution.py:234
  13.4 2.9 %merge.1.merged = f32[8832,64]{1,0:T(8,128)S(1)} custom-call(f32[8232,64]{1,0:T(8,128)S(1)} %get-tuple-element.46.ybuf, s32[40,128]{1,0:T(8,128)S(1)} %get-tuple-element.47.table), custom_call_target="tpu_custom_call" | custom-call | tf_op jit(solution)/shard_map/merge/pallas_call | solution.py:256
  16.9 35.3 %exchange.3 = (f32[1,32,512]{2,1,0:T(8,128)S(1)}, f32[1,32,256]{2,1,0:T(8,128)S(1)}, f32[1,256]{1,0:T(1,128)S(1)}, s32[1]{0:T(128)}) custom-call(f32[8832,64]{1,0:T(8,128)S(1)} %merge.1.merged, s32[16,1,256]{2,1,0:T(1,128)S(1)} %get-tuple-element.48.held, f32[1]{0:T(128)S(6)} %copy.23.ridge, s32[1,256]{1,0:T(1,128)} %pivots_hbm.1, f32[1,48]{1,0:T(1,128)} %bitcast.8, ...), custom_call_target="tpu_custom_call" | custom-call | tf_op jit(solution)/shard_map/exchange/pallas_call | solution.py:716
  52.8 0.7 %conditional.1 = ((f32[1,32,512]{2,1,0:T(8,128)}, f32[1,32,256]{2,1,0:T(8,128)}, f32[1,256]{1,0:T(1,128)})) conditional(s32[]{:T(128)} %bitcast.3, (f32[1,32,512]{2,1,0:T(8,128)S(1)}, f32[1,32,256]{2,1,0:T(8,128)S(1)}, f32[1,256]{1,0:T(1,128)S(1)}) %tuple.13, (bf16[48,8192]{1,0:T(8,128)(2,1)}, bf16[64,128]{1,0:T(8,128)(2,1)}, s32[64,128]{1,0:T(8,128)}, ...), branch_computations={%region_0.0_spmd, %region_1.0_spmd} | conditional | bytes 16396 | solution.py:812
  52.8 0.7 %emit.2 = (f32[1,32,512]{2,1,0:T(8,128)}, f32[1,32,256]{2,1,0:T(8,128)}, f32[1,256]{1,0:T(1,128)}) custom-call(f32[1,32,512]{2,1,0:T(8,128)S(1)} %get-tuple-element.22.refs_0_, f32[1,32,256]{2,1,0:T(8,128)S(1)} %get-tuple-element.23.refs_1_, f32[1,256]{1,0:T(1,128)S(1)} %get-tuple-element.24.refs_2_), custom_call_target="tpu_custom_call" | custom-call | tf_op jit(solution)/shard_map/cond/branch_0_fun/emit/pallas_call | solution.py:791

commit v7 on v3

--- a/solution.py
+++ b/solution.py
@@ -253,6 +253,13 @@
     lax.fori_loop(1, count, lambda k, _: (step(k), 0)[1], 0, unroll=unroll)
 
 
+def turn_of(n):
+    n = jnp.int32(n)
+    odd = lax.rem(n, jnp.int32(2))
+    half = lax.div(n + odd, jnp.int32(2))
+    return lax.rem(odd * half + (1 - odd) * (LEAVES - half), jnp.int32(LEAVES))
+
+
 def remote(src, dst, sems, k, peer):
     return pltpu.make_async_remote_copy(src, dst, sems[0].at[k], sems[1].at[k], **peer)
 
@@ -307,13 +314,14 @@
         return remote(aux.at[k], ra.at[k], (s_a, r_a), k, mate(k))
 
     def four(j, _):
-        for r in range(1, 5):
-            turn((4 * j + r) % LEAVES)
+        steps = [turn_of(lax.rem(4 * j + r, LEAVES)) for r in range(1, 5)]
+        for k in steps:
+            turn(k)
         pl.when(j == 0)(lambda: pl.semaphore_wait(barrier, LEAVES + COLS - 2))
         for send in (send_aux, send_feat):
-            for r in range(1, 4):
-                send(4 * j + r).start()
-            pl.when(j < 3)(lambda: send(4 * j + 4).start())
+            for k in steps[:3]:
+                send(k).start()
+            pl.when(j < 3)(lambda: send(steps[3]).start())
         return 0
 
     lax.fori_loop(0, LEAVES // 4, four, 0)
@@ -346,8 +354,9 @@
         wanted = tag + (PER // 2 + source * PER).astype(F32)
         hot[k] = (key == wanted).astype(F32).astype(BF)
 
-    def mark_next(k, _):
-        pl.when(k > 0)(lambda: send_aux(k).wait_recv())
+    def mark_next(n, _):
+        k = turn_of(n)
+        pl.when(n > 0)(lambda: send_aux(k).wait_recv())
         mark(k)
         return 0
 
@@ -366,14 +375,12 @@
     fours[...] = chosen.astype(F32).astype(BF)
 
     def pick(j, total):
-        for r in range(4):
-            k = 4 * j + r
-            if r:
-                send_feat(k).wait_recv()
-            else:
-                pl.when(k > 0)(lambda: send_feat(k).wait_recv())
-        for r in range(4):
-            total = total + dot_nt(hot[4 * j + r], rx[4 * j + r])
+        steps = [turn_of(4 * j + r) for r in range(4)]
+        pl.when(j > 0)(lambda: send_feat(steps[0]).wait_recv())
+        for k in steps[1:]:
+            send_feat(k).wait_recv()
+        for k in steps:
+            total = total + dot_nt(hot[k], rx[k])
         return total
 
     picked = lax.fori_loop(0, LEAVES // 4, pick, jnp.zeros((RANK, F), F32))
@@ -494,7 +501,14 @@
     value = jnp.exp2(jnp.minimum(dot(skel_side(points, scale2), right), 0.0))
     crossing = (across(index[...], RANK) >= 2.0 * RANK) != (index[...].T[0:1, :] >= 2.0 * RANK)
     square = iota((RANK, RANK), 0) == iota((RANK, RANK), 1)
-    tops[...] = jnp.where(crossing, value, 0.0) + jnp.where(square, ridge[0], 0.0)
+    tops[...] = jnp.where(crossing, value, 0.0) + jnp.where(square, ridge[...], 0.0)
+
+    def finish(sends):
+        return lambda k: [send(k).wait_send() for send in sends]
+
+    each(LEAVES, finish((send_aux, send_feat)))
+    each(COLS, finish((send_skel, send_gram, send_rhs)))
+    each(4, finish((send_four,)))
 
     def add_chosen(k, totals):
         send_chosen(k).wait_recv()
@@ -525,7 +539,7 @@
 
     total = lax.fori_loop(1, COLS, add_gram, pg[col].astype(F32))
     diagonal = iota((SLAB, RANK), 0) + col * SLAB == iota((SLAB, RANK), 1)
-    out_share[0, :, 0:RANK] = total * (1.0 / NODE) + jnp.where(diagonal, ridge[0], 0.0)
+    out_share[0, :, 0:RANK] = total * (1.0 / NODE) + jnp.where(diagonal, ridge[...], 0.0)
     total = lax.fori_loop(1, COLS, add_couple, pc[col].astype(F32))
     out_share[0, :, RANK:] = total * (1.0 / NODE)
     result = chosen + tops[pl.ds(pl.multiple_of(col * SLAB, SLAB), SLAB), :]
@@ -539,12 +553,8 @@
     out_top[0] = result
     out_rhs[...] = jnp.concatenate([rhs[0:1], rhs[1:2]], 1)
 
-    def finish(sends):
-        return lambda k: [send(k).wait_send() for send in sends]
-
-    each(LEAVES, finish((send_aux, send_feat)))
-    each(COLS, finish((send_skel, send_gram, send_couple, send_chosen, send_rhs)))
-    each(4, finish((send_four, send_top, send_top_rhs)))
+    each(COLS, finish((send_couple, send_chosen)))
+    each(4, finish((send_top, send_top_rhs)))
 
 
 SHAPES = ((1, SLAB, 2 * RANK), (1, SLAB, RANK), (1, RANK))
@@ -554,7 +564,7 @@
     return pl.pallas_call(
         exchange_kernel,
         out_shape=tuple(pltpu.VMEM(shape, F32) for shape in SHAPES),
-        in_specs=[VMEM, pl.BlockSpec(memory_space=pltpu.SMEM)] + [ANYWHERE] * 4,
+        in_specs=[VMEM, VMEM] + [ANYWHERE] * 4,
         out_specs=[VMEM] * 3,
         scratch_shapes=[
             pltpu.VMEM((1, RANK), jnp.int32),
@@ -634,7 +644,7 @@
 def local(features, targets, owner, length_scales, ridge, leaf_pivots, parent_pivots, top_pivots):
     merged = pack(features, targets.reshape(ROWS // 128, 128), owner.reshape(ROWS // 128, 128))
     smalls = (leaf_pivots, length_scales.reshape(1, F), parent_pivots, top_pivots)
-    return tuple(emit(exchange(merged, ridge, *smalls)))
+    return tuple(emit(exchange(merged, ridge.reshape(1, 1), *smalls)))
 
 
 def solution(mesh):

time: 54.1 us -> 54.3 us (level)
  no operation moved by 1% of the time
where the time goes in v7:
time: 54.3 us; the launch traced here: 54.1 us
  Pallas kernels  52.8 us (97%)
  between operations  1.29 us (2%)
    pallas_call x1, Pallas kernels, exchange(): pl.pallas_call(exchange_kernel, out_shape=tuple((pltpu.VMEM(shape, F32) f...  45.5 us
    pallas_call x1, Pallas kernels, pack(): pl.pallas_call(pack_kernel, out_shape=pltpu.VMEM((LEAVES * REGION, WIDE),...  6.63 us

profile of v7, /device:TPU:1, one launch (start us, length us, event | category | flops | bytes accessed | tf_op | source)
XLA Modules:
  0.0 54.1 jit_solution(15093376816560687404)
XLA Ops:
  1.3 6.6 %pack.1.merged = f32[8832,64]{1,0:T(8,128)S(1)} custom-call(bf16[48,8192]{1,0:T(8,128)(2,1)} %feat_hbm.1, bf16[64,128]{1,0:T(8,128)(2,1)} %bitcast.6, s32[64,128]{1,0:T(8,128)} %bitcast.5), custom_call_target="tpu_custom_call" | custom-call | tf_op jit(solution)/shard_map/pack/pallas_call | solution.py:165
  7.9 45.5 %exchange.1 = (f32[1,32,512]{2,1,0:T(8,128)S(1)}, f32[1,32,256]{2,1,0:T(8,128)S(1)}, f32[1,256]{1,0:T(1,128)S(1)}) custom-call(f32[8832,64]{1,0:T(8,128)S(1)} %pack.1.merged, f32[1,1]{1,0:T(1,128)} %bitcast.4.ridge, s32[1,256]{1,0:T(1,128)} %pivots_hbm.1, f32[1,48]{1,0:T(1,128)} %bitcast.7, s32[8,256]{1,0:T(8,128)} %parent_hbm.1, s32[4,256]{1,0:T(4,128)} %top_hbm.1), custom_call_target="tpu_custom_call" | custom-call | tf_op jit(solution)/shard_map/exchange/pallas_call | solution.py:564
  53.5 0.7 %emit.1 = (f32[1,32,512]{2,1,0:T(8,128)}, f32[1,32,256]{2,1,0:T(8,128)}, f32[1,256]{1,0:T(1,128)}) custom-call(f32[1,32,512]{2,1,0:T(8,128)S(1)} %get-tuple-element.6.refs_0_, f32[1,32,256]{2,1,0:T(8,128)S(1)} %get-tuple-element.7.refs_1_, f32[1,256]{1,0:T(1,128)S(1)} %get-tuple-element.8.refs_2_), custom_call_target="tpu_custom_call" | custom-call | tf_op jit(solution)/shard_map/emit/pallas_call | solution.py:633

commit v8 on v7

--- a/solution.py
+++ b/solution.py
@@ -20,6 +20,11 @@
 CHUNKS = ROWS // CHUNK
 WINDOW = 40
 REGION = PER + WINDOW
+BIN = 40
+BINS = BIN * CHUNKS
+SLOTS = 16
+WHICH = 50
+FULL = 51
 WIDE = 64
 SLAB = RANK // COLS
 NODE = ROWS * COLS
@@ -253,6 +258,10 @@
     lax.fori_loop(1, count, lambda k, _: (step(k), 0)[1], 0, unroll=unroll)
 
 
+def rem(a, b):
+    return lax.rem(jnp.int32(a), jnp.int32(b))
+
+
 def turn_of(n):
     n = jnp.int32(n)
     odd = lax.rem(n, jnp.int32(2))
@@ -516,6 +525,387 @@
         return totals[0] + qr[k].astype(F32), totals[1] + rr[k]
 
     chosen, rhs = lax.fori_loop(1, COLS, add_chosen, (pt[col].astype(F32), rs[...]))
+    chosen = chosen * (1.0 / NODE)
+    t4[0] = chosen.astype(BF)
+    r4[0] = rhs * (1.0 / NODE)
+
+    def send_top(k):
+        return remote(t4.at[0], t4.at[k], (s_t, r_t), k, cousin(k))
+
+    def send_top_rhs(k):
+        return remote(r4.at[0], r4.at[k], (s_q, r_q), k, cousin(k))
+
+    each(4, lambda k: send_top(k).start())
+    each(4, lambda k: send_top_rhs(k).start())
+
+    def add_gram(k, total):
+        send_gram(k).wait_recv()
+        return total + gr[k].astype(F32)
+
+    def add_couple(k, total):
+        send_couple(k).wait_recv()
+        return total + cr[k].astype(F32)
+
+    total = lax.fori_loop(1, COLS, add_gram, pg[col].astype(F32))
+    diagonal = iota((SLAB, RANK), 0) + col * SLAB == iota((SLAB, RANK), 1)
+    out_share[0, :, 0:RANK] = total * (1.0 / NODE) + jnp.where(diagonal, ridge[...], 0.0)
+    total = lax.fori_loop(1, COLS, add_couple, pc[col].astype(F32))
+    out_share[0, :, RANK:] = total * (1.0 / NODE)
+    result = chosen + tops[pl.ds(pl.multiple_of(col * SLAB, SLAB), SLAB), :]
+
+    def add_top(k, totals):
+        send_top(k).wait_recv()
+        send_top_rhs(k).wait_recv()
+        return totals[0] + t4[k].astype(F32), totals[1] + r4[k]
+
+    result, rhs = lax.fori_loop(1, 4, add_top, (result, r4[0]))
+    out_top[0] = result
+    out_rhs[...] = jnp.concatenate([rhs[0:1], rhs[1:2]], 1)
+
+    each(COLS, finish((send_couple, send_chosen)))
+    each(4, finish((send_top, send_top_rhs)))
+
+
+def stream_kernel(
+    feat_hbm, target, owner, pivots, ridge, scales_hbm, parent_hbm, top_hbm,
+    out_share, out_top, out_rhs, flag,
+    feat_in, goals, ranked, starts, counts, places, bins, held, slots, came, scales, parent, top, spare,
+    feat, aux, rx, ra, side, sk, mine, sk4, left, even, odd, other_even, other_odd, gram, couple,
+    rows, columns, fours, index, tops, pg, gr, pc, cr, pt, qr, rs, rr, t4, r4,
+    s_v, r_v, s_s, r_s, s_f, r_f, s_a, r_a, s_k, r_k, s_4, r_4, s_p, r_p, s_c, r_c, s_o, r_o,
+    s_r, r_r, s_t, r_t, s_q, r_q, local,
+):
+    leaf = lax.axis_index("leaf")
+    col = lax.axis_index("col")
+    quarter = leaf % 4
+    sibling = quarter + 1 - 2 * (quarter % 2)
+    barrier = pltpu.get_barrier_semaphore()
+    each(LEAVES, lambda k: pl.semaphore_signal(barrier, inc=1, **mate(k)))
+    each(COLS, lambda k: pl.semaphore_signal(barrier, inc=1, **beside(k)))
+    bring = pltpu.make_async_copy(feat_hbm, feat_in, local.at[3])
+    bring.start()
+    smalls = [
+        pltpu.make_async_copy(a, b, local.at[k])
+        for k, (a, b) in enumerate([(scales_hbm, scales), (parent_hbm, parent), (top_hbm, top)])
+    ]
+    for copy in smalls:
+        copy.start()
+
+    def send_pivots(k):
+        return remote(pivots, held.at[k], (s_v, r_v), k, mate(k))
+
+    def send_slots(k):
+        return remote(slots.at[k], came.at[k], (s_s, r_s), k, mate(k))
+
+    def send_feat(k):
+        return remote(feat.at[k], rx.at[k], (s_f, r_f), k, mate(k))
+
+    def send_aux(k):
+        return remote(aux.at[k], ra.at[k], (s_a, r_a), k, mate(k))
+
+    def send_skel(k):
+        return remote(sk.at[0], sk.at[k], (s_k, r_k), k, beside(k))
+
+    goals[...] = target[...].astype(F32)
+    before = (iota((CHUNK, CHUNK), 0) < iota((CHUNK, CHUNK), 1)).astype(F32).astype(BF)
+    weights = jnp.concatenate([before, jnp.ones((CHUNK, 128), BF)], 1)
+    lane = iota((LEAVES, 128), 1)
+
+    def rank(t, carry):
+        seen, seen_leaf, most = carry
+        own = row_pair(owner[pl.ds(2 * t, 2), :])
+        group = own // 8
+        is_own = iota((OWNERS, CHUNK), 0) == own
+        is_leaf = iota((LEAVES, CHUNK), 0) == group
+        marks = jnp.concatenate([m.astype(F32).astype(BF) for m in (is_own, is_leaf)], 0)
+        sums = dot(marks, weights)
+        leaf_counts = sums[OWNERS:, CHUNK:]
+        prior = sums[:OWNERS, :CHUNK] + jnp.concatenate([seen, seen], 1)
+        place = jnp.sum(jnp.where(is_own, prior, 0.0), 0, keepdims=True)
+        ranked[t, 0:1, :] = (group * BIN).astype(F32) + jnp.sum(
+            jnp.where(is_leaf, sums[OWNERS:, :CHUNK], 0.0), 0, keepdims=True
+        )
+        ranked[t, 1:2, :] = row_pair(goals[pl.ds(2 * t, 2), :])
+        ranked[t, 2:3, :] = own.astype(F32) * PACKET + place
+        starts[...] = jnp.where(lane == t, seen_leaf, starts[...])
+        counts[...] = jnp.where(lane == t, leaf_counts, counts[...])
+        return seen + sums[:OWNERS, CHUNK:], seen_leaf + leaf_counts, jnp.maximum(most, leaf_counts)
+
+    starts[...] = jnp.zeros_like(starts)
+    counts[...] = jnp.zeros_like(counts)
+    zero = jnp.zeros((LEAVES, 128), F32)
+    _, _, most = lax.fori_loop(
+        0, CHUNKS, rank, (jnp.zeros((OWNERS, 128), F32), zero, zero), unroll=16
+    )
+    full = jnp.maximum(jnp.max(most, 0, keepdims=True) - BIN, 0.0)
+
+    held[0] = pivots[...]
+    pl.semaphore_wait(barrier, LEAVES + COLS - 2)
+    each(LEAVES, lambda k: send_pivots(k).start())
+
+    def joined_of(t):
+        row = iota((16, CHUNK), 0)
+        extra = jnp.where(row == 0, ranked[t, 1:2, :], 0.0).astype(BF)
+        return jnp.concatenate([feat_in[:, pl.ds(pl.multiple_of(t * CHUNK, CHUNK), CHUNK)], extra], 0)
+
+    def fill_bins(t, _):
+        place = ranked[t, 0:1, :].astype(jnp.int32)
+        chosen = (iota((LEAVES * BIN, CHUNK), 0) == place).astype(F32).astype(BF)
+        binned = dot_nt(chosen, joined_of(t))
+        for i in range(LEAVES):
+            bins[i, pl.ds(pl.multiple_of(t * BIN, 8), BIN), :] = binned[i * BIN : (i + 1) * BIN]
+        return 0
+
+    bring.wait()
+    lax.fori_loop(0, CHUNKS, fill_bins, 0, unroll=4)
+
+    spot, chunk = iota((128, BINS), 1), iota((128, BINS), 0)
+    inside = (spot >= chunk * BIN) & (spot < chunk * BIN + BIN)
+    offset = spot[0:1] - jnp.sum(jnp.where(inside, chunk * BIN, 0), 0, keepdims=True)
+    offset = offset.astype(F32)
+    high = jnp.where(starts[...] >= 256.0, 256.0, 0.0)
+    parts = jnp.concatenate([high, starts[...] - high, counts[...]], 0).astype(BF)
+    parts = dot(parts, inside.astype(F32).astype(BF))
+    table = parts[:LEAVES] + parts[LEAVES : 2 * LEAVES] + offset
+    table = jnp.where(offset < parts[2 * LEAVES :], table, -1.0)
+    for i in range(LEAVES):
+        places[i] = table[i : i + 1]
+
+    eye = (iota((WIDE, WIDE), 0) == iota((WIDE, WIDE), 1)).astype(F32).astype(BF)
+
+    def packet(k):
+        to = lax.rem(leaf + k, jnp.int32(LEAVES))
+        chosen = (iota((PER, BINS), 0).astype(F32) == places[to]).astype(F32).astype(BF)
+        packed = dot(chosen, bins[to].astype(BF)).astype(BF)
+        turned = dot_nt(eye, packed)
+        feat[k] = turned[:F].astype(BF)
+        aux[k] = jnp.concatenate([turned[F : F + 1, 128 * c : 128 * c + 128] for c in range(4)] * 2, 0)
+
+    def give(n, _):
+        k = turn_of(n)
+        packet(k)
+        send_aux(k).start()
+        send_feat(k).start()
+        return 0
+
+    lax.fori_loop(1, 4, give, 0)
+
+    each(LEAVES, lambda k: send_pivots(k).wait_recv())
+    place = jnp.concatenate([held[(LEAVES - b) % LEAVES] for b in range(LEAVES)], 0)
+    home = place % ROWS // PACKET
+    number = ((leaf + iota((LEAVES, RANK), 0)) % LEAVES) * 8 + place // ROWS
+    number = (number * PACKET + place % PACKET).astype(F32)
+    valid = home == leaf * COLS + col
+    order = dot(valid.astype(F32).astype(BF), before)
+    order = jnp.where(valid, order, -1.0)
+
+    def spread(table):
+        return jnp.concatenate(
+            [jnp.broadcast_to(table[b : b + 1], (SLOTS, RANK)) for b in range(LEAVES)], 0
+        )
+
+    shape = (LEAVES * SLOTS, RANK)
+    hit = spread(order) == (iota(shape, 0) % SLOTS).astype(F32)
+    wanted = jnp.sum(jnp.where(hit, spread(number) + 1.0, 0.0), 1, keepdims=True) - 1.0
+    which = jnp.sum(jnp.where(hit, iota(shape, 1).astype(F32) + 1.0, 0.0), 1, keepdims=True) - 1.0
+    wanted = jnp.broadcast_to(wanted, (LEAVES * SLOTS, CHUNK))
+
+    def take(t, total):
+        chosen = (wanted == ranked[t, 2:3, :]).astype(F32).astype(BF)
+        rest = jnp.zeros((128 - WIDE, CHUNK), BF)
+        return total + dot_nt(chosen, jnp.concatenate([joined_of(t), rest], 0))
+
+    shape = (LEAVES * SLOTS, 128)
+    taken = lax.fori_loop(0, CHUNKS, take, jnp.zeros(shape, F32), unroll=4)
+    taken = jnp.where(iota(shape, 1) == WHICH, which, taken)
+    taken = jnp.where(iota(shape, 1) == FULL, full, taken).astype(BF)
+    for b in range(LEAVES):
+        slots[b] = taken[b * SLOTS : (b + 1) * SLOTS]
+    came[0] = slots[0]
+    each(LEAVES, lambda k: send_slots(k).start())
+    lax.fori_loop(4, 11, give, 0)
+
+    each(LEAVES, lambda k: send_slots(k).wait_recv())
+    got = jnp.concatenate([came[b] for b in range(LEAVES)], 0).astype(F32)
+    chosen = got[:, WHICH : WHICH + 1] == iota((LEAVES * SLOTS, RANK), 1).astype(F32)
+    picked = dot(got.T[:F].astype(BF), chosen.astype(F32).astype(BF))
+    full = jnp.broadcast_to(jnp.max(got[:, FULL : FULL + 1], 0, keepdims=True), (1, 128))
+    sk[0] = picked.astype(BF)
+    each(COLS, lambda k: send_skel(k).start())
+    lax.fori_loop(11, LEAVES, give, 0)
+    packet(0)
+    rx[0] = feat[0]
+    ra[0] = aux[0]
+
+    largest = jnp.zeros((OWNERS, 1), F32)
+    for b in range(LEAVES):
+        held_here = (iota((OWNERS, RANK), 0) == home[b : b + 1]).astype(F32)
+        largest = jnp.maximum(largest, jnp.sum(held_here, 1, keepdims=True))
+
+    for copy in smalls:
+        copy.wait()
+    spare[...] = jnp.ones((8, 128), F32)
+    spare[0:1, 0:F] = scales[...]
+    inverse = 1.0 / to_column(spare[0:1, :])[:F]
+    scale = inverse * inverse * LOG2E
+    scale2 = across(scale, RANK)
+    scale4 = across(scale, PER)
+
+    index[...] = top_index(parent, top, leaf // 4)
+    index2 = across(index[...], 2 * RANK)
+    number = iota((RANK, 2 * RANK), 1)
+    base = (quarter * RANK).astype(F32)
+    other = (sibling * RANK).astype(F32)
+    chosen = index2[:, :RANK] == iota((RANK, RANK), 1).astype(F32) + base
+    rows[...] = chosen.astype(F32).astype(BF)
+    lanes = number.astype(F32) + jnp.where(number < RANK, base, other - RANK)
+    columns[...] = (index2 == lanes).astype(F32).astype(BF)
+    chosen = across(index[...], 4 * RANK) == iota((RANK, 4 * RANK), 1).astype(F32)
+    fours[...] = chosen.astype(F32).astype(BF)
+
+    def norms(k):
+        side[k] = point_side(rx[k].astype(F32), scale4)
+
+    def add_skel(k, total):
+        send_skel(k).wait_recv()
+        return total + sk[k].astype(F32)
+
+    picked = lax.fori_loop(1, COLS, add_skel, picked)
+    mine[...] = picked.astype(BF)
+    sk4[quarter] = picked.astype(BF)
+
+    def send_four(k):
+        return remote(mine, sk4.at[quarter], (s_4, r_4), k, cousin(k))
+
+    each(4, lambda k: send_four(k).start())
+    left[0:RANK, :] = skel_side(picked, scale2)
+
+    def block_of(k, out, begin):
+        p = rx[k]
+        fill = jnp.zeros((256 - 3 * F - 16, PER), BF)
+        right = jnp.concatenate([p, p, p, side[k], fill], 0)
+        power = dot(left[begin : begin + RANK, :], right)
+        out[0:RANK, :] = jnp.exp2(jnp.minimum(power, 0.0)).astype(BF)
+
+    def own_of(k, out):
+        block_of(k, out, 0)
+        value = ra[k]
+        value = jnp.concatenate([value[r : r + 1] for r in range(4)], 1)
+        out[RANK:, :] = jnp.broadcast_to(value, (16, PER)).astype(BF)
+
+    def gram_of(u):
+        gram[...] += dot_nt(u[...], u[0:RANK, :])
+
+    def couple_of(v, u):
+        couple[...] += dot_nt(v[...], u[0:RANK, :])
+
+    last = LEAVES // 2 - 1
+
+    def own_two(j, _):
+        k, l = turn_of(2 * j), turn_of(2 * j + 1)
+        pl.when(j > 0)(lambda: receive(k))
+        receive(l)
+        norms(k)
+        norms(l)
+        own_of(k, even.at[j])
+        gram_of(odd.at[rem(j + last, last + 1)])
+        own_of(l, odd.at[j])
+        gram_of(even.at[j])
+        return 0
+
+    def receive(k):
+        send_aux(k).wait_recv()
+        send_feat(k).wait_recv()
+
+    def other_two(j, _):
+        block_of(turn_of(2 * j), other_even, RANK)
+        couple_of(other_odd, odd.at[rem(j + last, last + 1)])
+        block_of(turn_of(2 * j + 1), other_odd, RANK)
+        couple_of(other_even, even.at[j])
+        return 0
+
+    gram[...] = jnp.zeros_like(gram)
+    couple[...] = jnp.zeros_like(couple)
+    odd[last] = jnp.zeros((RANK + 16, PER), BF)
+    other_odd[...] = jnp.zeros_like(other_odd)
+    def send_gram(k):
+        return remote(pg.at[(col + k) % COLS], gr.at[k], (s_p, r_p), k, beside(k))
+
+    def send_couple(k):
+        return remote(pc.at[(col + k) % COLS], cr.at[k], (s_c, r_c), k, beside(k))
+
+    def send_chosen(k):
+        return remote(pt.at[(col + k) % COLS], qr.at[k], (s_o, r_o), k, beside(k))
+
+    def send_rhs(k):
+        return remote(rs, rr.at[k], (s_r, r_r), k, beside(k))
+
+    def sibling_side():
+        each(4, lambda k: remote(mine, sk4.at[(quarter + 4 - k) % 4], (s_4, r_4), k, cousin(k)).wait_recv())
+        left[RANK:, :] = skel_side(sk4[sibling].astype(F32), scale2)
+
+    def give_gram():
+        gram_of(odd.at[last])
+        part = gram[0:RANK, :].astype(BF)
+        for k in range(COLS):
+            pg[k] = part[k * SLAB : (k + 1) * SLAB]
+        rhs = gram[RANK : RANK + 1, :]
+        rhs = jnp.sum(dot_nt(stack16(split3(rhs), RANK), rows[...]), 0, keepdims=True)
+        rs[...] = jnp.zeros_like(rs)
+        rs[0:1, :] = rhs[:, :128]
+        rs[1:2, :] = rhs[:, 128:]
+        rs[2:3, :] = full
+        each(COLS, lambda k: send_gram(k).start())
+        each(COLS, lambda k: send_rhs(k).start())
+        tops[...] = dot_nt(dot(rows[...], part).astype(BF), columns[:, 0:RANK])
+
+    def half(h, _):
+        pairs = LEAVES // 4
+        lax.fori_loop(pairs * h, pairs * (h + 1), own_two, 0)
+        pl.when(h == 0)(sibling_side)
+        pl.when(h == 1)(give_gram)
+        lax.fori_loop(pairs * h, pairs * (h + 1), other_two, 0)
+        return 0
+
+    lax.fori_loop(0, 2, half, 0)
+    couple_of(other_odd, odd.at[last])
+
+    part = couple[...].astype(BF)
+    chosen = dot_nt(dot_nt(rows[...], part).astype(BF), columns[:, RANK:]) + tops[...]
+    chosen = chosen.astype(BF)
+    for k in range(COLS):
+        pt[k] = chosen[k * SLAB : (k + 1) * SLAB]
+    each(COLS, lambda k: send_chosen(k).start())
+    part = couple[...].T.astype(BF)
+    for k in range(COLS):
+        pc[k] = part[k * SLAB : (k + 1) * SLAB]
+    each(COLS, lambda k: send_couple(k).start())
+
+    whole = jnp.concatenate([sk4[k] for k in range(4)], 1)
+    points = dot_nt(whole, fours[...])
+    fill = jnp.zeros((256 - 3 * F - 16, RANK), BF)
+    points_b = points.astype(BF)
+    right = jnp.concatenate([points_b, points_b, points_b, point_side(points, scale2), fill], 0)
+    value = jnp.exp2(jnp.minimum(dot(skel_side(points, scale2), right), 0.0))
+    crossing = (across(index[...], RANK) >= 2.0 * RANK) != (index[...].T[0:1, :] >= 2.0 * RANK)
+    square = iota((RANK, RANK), 0) == iota((RANK, RANK), 1)
+    tops[...] = jnp.where(crossing, value, 0.0) + jnp.where(square, ridge[...], 0.0)
+
+    def finish(sends):
+        return lambda k: [send(k).wait_send() for send in sends]
+
+    each(LEAVES, finish((send_pivots, send_slots, send_aux, send_feat)))
+    each(COLS, finish((send_skel, send_gram, send_rhs)))
+    each(4, finish((send_four,)))
+
+    def add_chosen(k, totals):
+        send_chosen(k).wait_recv()
+        send_rhs(k).wait_recv()
+        return totals[0] + qr[k].astype(F32), totals[1] + rr[k]
+
+    chosen, rhs = lax.fori_loop(1, COLS, add_chosen, (pt[col].astype(F32), rs[...]))
+    over = jnp.maximum(jnp.max(rhs[2:3, :]), jnp.max(largest) - SLOTS)
+    flag[0] = (over > 0.0).astype(jnp.int32)
     chosen = chosen * (1.0 / NODE)
     t4[0] = chosen.astype(BF)
     r4[0] = rhs * (1.0 / NODE)
@@ -620,6 +1010,79 @@
     )(merged, ridge, *in_hbm(*smalls))
 
 
+def stream(samples, pivots, ridge, *smalls):
+    return pl.pallas_call(
+        stream_kernel,
+        out_shape=(
+            *(pltpu.VMEM(shape, F32) for shape in SHAPES),
+            jax.ShapeDtypeStruct((1,), jnp.int32),
+        ),
+        in_specs=[ANYWHERE, VMEM, VMEM, VMEM, VMEM] + [ANYWHERE] * 3,
+        out_specs=[VMEM] * 3 + [pl.BlockSpec(memory_space=pltpu.SMEM)],
+        scratch_shapes=[
+            pltpu.VMEM((F, ROWS), BF),
+            pltpu.VMEM((ROWS // 128, 128), F32),
+            pltpu.VMEM((CHUNKS, 8, CHUNK), F32),
+            pltpu.VMEM((LEAVES, 128), F32),
+            pltpu.VMEM((LEAVES, 128), F32),
+            pltpu.VMEM((LEAVES, 1, BINS), F32),
+            pltpu.VMEM((LEAVES, BINS, WIDE), F32),
+            pltpu.VMEM((LEAVES, 1, RANK), jnp.int32),
+            pltpu.VMEM((LEAVES, SLOTS, 128), BF),
+            pltpu.VMEM((LEAVES, SLOTS, 128), BF),
+            pltpu.VMEM((1, F), F32),
+            pltpu.VMEM((8, RANK), jnp.int32),
+            pltpu.VMEM((4, RANK), jnp.int32),
+            pltpu.VMEM((8, 128), F32),
+            pltpu.VMEM((LEAVES, F, PER), BF),
+            pltpu.VMEM((LEAVES, 8, 128), F32),
+            pltpu.VMEM((LEAVES, F, PER), BF),
+            pltpu.VMEM((LEAVES, 8, 128), F32),
+            pltpu.VMEM((LEAVES, 16, PER), BF),
+            pltpu.VMEM((COLS, F, RANK), BF),
+            pltpu.VMEM((F, RANK), BF),
+            pltpu.VMEM((4, F, RANK), BF),
+            pltpu.VMEM((2 * RANK, 256), BF),
+            pltpu.VMEM((LEAVES // 2, RANK + 16, PER), BF),
+            pltpu.VMEM((LEAVES // 2, RANK + 16, PER), BF),
+            pltpu.VMEM((RANK, PER), BF),
+            pltpu.VMEM((RANK, PER), BF),
+            pltpu.VMEM((RANK + 16, RANK), F32),
+            pltpu.VMEM((RANK, RANK), F32),
+            pltpu.VMEM((RANK, RANK), BF),
+            pltpu.VMEM((RANK, 2 * RANK), BF),
+            pltpu.VMEM((RANK, 4 * RANK), BF),
+            pltpu.VMEM((RANK, 128), F32),
+            pltpu.VMEM((RANK, RANK), F32),
+            pltpu.VMEM((COLS, SLAB, RANK), BF),
+            pltpu.VMEM((COLS, SLAB, RANK), BF),
+            pltpu.VMEM((COLS, SLAB, RANK), BF),
+            pltpu.VMEM((COLS, SLAB, RANK), BF),
+            pltpu.VMEM((COLS, SLAB, RANK), BF),
+            pltpu.VMEM((COLS, SLAB, RANK), BF),
+            pltpu.VMEM((8, 128), F32),
+            pltpu.VMEM((COLS, 8, 128), F32),
+            pltpu.VMEM((4, SLAB, RANK), BF),
+            pltpu.VMEM((4, 8, 128), F32),
+            *dma(LEAVES),
+            *dma(LEAVES),
+            *dma(LEAVES),
+            *dma(LEAVES),
+            *dma(COLS),
+            *dma(4),
+            *dma(COLS),
+            *dma(COLS),
+            *dma(COLS),
+            *dma(COLS),
+            *dma(4),
+            *dma(4),
+            pltpu.SemaphoreType.DMA((4,)),
+        ],
+        compiler_params=params(1, 40),
+        name="stream",
+    )(*in_hbm(*samples, pivots), ridge, *in_hbm(*smalls))
+
+
 def emit_kernel(*refs):
     ins, outs, sem = refs[:3], refs[3:6], refs[6]
     copies = [pltpu.make_async_copy(a, b, sem.at[k]) for k, (a, b) in enumerate(zip(ins, outs))]
@@ -642,9 +1105,15 @@
 
 
 def local(features, targets, owner, length_scales, ridge, leaf_pivots, parent_pivots, top_pivots):
-    merged = pack(features, targets.reshape(ROWS // 128, 128), owner.reshape(ROWS // 128, 128))
-    smalls = (leaf_pivots, length_scales.reshape(1, F), parent_pivots, top_pivots)
-    return tuple(emit(exchange(merged, ridge.reshape(1, 1), *smalls)))
+    samples = (features, targets.reshape(ROWS // 128, 128), owner.reshape(ROWS // 128, 128))
+    ridge = ridge.reshape(1, 1)
+    smalls = (length_scales.reshape(1, F), parent_pivots, top_pivots)
+    *results, flag = stream(samples, leaf_pivots, ridge, *smalls)
+
+    def again():
+        return tuple(emit(exchange(pack(*samples), ridge, leaf_pivots, *smalls)))
+
+    return lax.switch(flag[0], [lambda: tuple(emit(results)), again])
 
 
 def solution(mesh):

time: 54.3 us -> 53.5 us (0.985)
  Pallas kernels: 52.8 us -> 51 us
  between operations: 1.29 us -> 2.08 us
    pallas_call x2 -> x1, Pallas kernels: 52.2 us -> 50.3 us  [stream(): pl.pallas_call(stream_kernel, out_shape=(*(pltpu.VMEM(shape, F32) for sha...]
where the time goes in v8:
time: 53.5 us; the launch traced here: 53.3 us
  Pallas kernels  51 us (95%)
  between operations  2.08 us (4%)
    pallas_call x1, Pallas kernels, stream(): pl.pallas_call(stream_kernel, out_shape=(*(pltpu.VMEM(shape, F32) for sha...  50.3 us

profile of v8, /device:TPU:1, one launch (start us, length us, event | category | flops | bytes accessed | tf_op | source)
XLA Modules:
  0.0 53.3 jit_solution(3941691283223829295)
XLA Ops:
  1.3 50.3 %stream.1 = (f32[1,32,512]{2,1,0:T(8,128)S(1)}, f32[1,32,256]{2,1,0:T(8,128)S(1)}, f32[1,256]{1,0:T(1,128)S(1)}, s32[1]{0:T(128)}) custom-call(bf16[48,8192]{1,0:T(8,128)(2,1)} %feat_hbm.1, bf16[64,128]{1,0:T(8,128)(2,1)} %bitcast.8, s32[64,128]{1,0:T(8,128)} %bitcast.6, s32[1,256]{1,0:T(1,128)} %pivots.1, f32[1,1]{1,0:T(1,128)} %bitcast.5.ridge, ...), custom_call_target="tpu_custom_call" | custom-call | tf_op jit(solution)/shard_map/stream/pallas_call | solution.py:1014
  52.2 0.9 %conditional.1 = ((f32[1,32,512]{2,1,0:T(8,128)}, f32[1,32,256]{2,1,0:T(8,128)}, f32[1,256]{1,0:T(1,128)})) conditional(s32[]{:T(128)} %bitcast.4, (f32[1,32,512]{2,1,0:T(8,128)S(1)}, f32[1,32,256]{2,1,0:T(8,128)S(1)}, f32[1,256]{1,0:T(1,128)S(1)}) %tuple.13, (bf16[48,8192]{1,0:T(8,128)(2,1)}, bf16[64,128]{1,0:T(8,128)(2,1)}, s32[64,128]{1,0:T(8,128)}, ...), branch_computations={%region_0.0_spmd, %region_1.0_spmd} | conditional | bytes 8 | solution.py:1116
  52.3 0.7 %emit.2 = (f32[1,32,512]{2,1,0:T(8,128)}, f32[1,32,256]{2,1,0:T(8,128)}, f32[1,256]{1,0:T(1,128)}) custom-call(f32[1,32,512]{2,1,0:T(8,128)S(1)} %get-tuple-element.22.refs_0_, f32[1,32,256]{2,1,0:T(8,128)S(1)} %get-tuple-element.23.refs_1_, f32[1,256]{1,0:T(1,128)S(1)} %get-tuple-element.24.refs_2_), custom_call_target="tpu_custom_call" | custom-call | tf_op jit(solution)/shard_map/cond/branch_0_fun/emit/pallas_call | solution.py:1096

commit v9 on v8

--- a/solution.py
+++ b/solution.py
@@ -20,8 +20,7 @@
 CHUNKS = ROWS // CHUNK
 WINDOW = 40
 REGION = PER + WINDOW
-BIN = 40
-BINS = BIN * CHUNKS
+TILES = PER // 8
 SLOTS = 16
 WHICH = 50
 FULL = 51
@@ -569,7 +568,7 @@
 def stream_kernel(
     feat_hbm, target, owner, pivots, ridge, scales_hbm, parent_hbm, top_hbm,
     out_share, out_top, out_rhs, flag,
-    feat_in, goals, ranked, starts, counts, places, bins, held, slots, came, scales, parent, top, spare,
+    feat_in, goals, ranked, starts, bases, ybuf, table, scal, held, slots, came, scales, parent, top, spare,
     feat, aux, rx, ra, side, sk, mine, sk4, left, even, odd, other_even, other_odd, gram, couple,
     rows, columns, fours, index, tops, pg, gr, pc, cr, pt, qr, rs, rr, t4, r4,
     s_v, r_v, s_s, r_s, s_f, r_f, s_a, r_a, s_k, r_k, s_4, r_4, s_p, r_p, s_c, r_c, s_o, r_o,
@@ -612,32 +611,65 @@
     lane = iota((LEAVES, 128), 1)
 
     def rank(t, carry):
-        seen, seen_leaf, most = carry
+        seen, seen_leaf = carry
         own = row_pair(owner[pl.ds(2 * t, 2), :])
         group = own // 8
         is_own = iota((OWNERS, CHUNK), 0) == own
         is_leaf = iota((LEAVES, CHUNK), 0) == group
-        marks = jnp.concatenate([m.astype(F32).astype(BF) for m in (is_own, is_leaf)], 0)
+        is_after = iota((LEAVES, CHUNK), 0) > group
+        marks = jnp.concatenate([m.astype(F32).astype(BF) for m in (is_own, is_leaf, is_after)], 0)
         sums = dot(marks, weights)
-        leaf_counts = sums[OWNERS:, CHUNK:]
+        leaf_counts = sums[OWNERS : OWNERS + LEAVES, CHUNK:]
+        base = sums[OWNERS + LEAVES :, CHUNK:]
         prior = sums[:OWNERS, :CHUNK] + jnp.concatenate([seen, seen], 1)
         place = jnp.sum(jnp.where(is_own, prior, 0.0), 0, keepdims=True)
-        ranked[t, 0:1, :] = (group * BIN).astype(F32) + jnp.sum(
-            jnp.where(is_leaf, sums[OWNERS:, :CHUNK], 0.0), 0, keepdims=True
-        )
+        order = sums[OWNERS : OWNERS + LEAVES, :CHUNK] + jnp.concatenate([base, base], 1)
+        ranked[t, 0:1, :] = jnp.sum(jnp.where(is_leaf, order, 0.0), 0, keepdims=True)
         ranked[t, 1:2, :] = row_pair(goals[pl.ds(2 * t, 2), :])
         ranked[t, 2:3, :] = own.astype(F32) * PACKET + place
         starts[...] = jnp.where(lane == t, seen_leaf, starts[...])
-        counts[...] = jnp.where(lane == t, leaf_counts, counts[...])
-        return seen + sums[:OWNERS, CHUNK:], seen_leaf + leaf_counts, jnp.maximum(most, leaf_counts)
+        bases[...] = jnp.where(lane == t, base, bases[...])
+        return seen + sums[:OWNERS, CHUNK:], seen_leaf + leaf_counts
 
     starts[...] = jnp.zeros_like(starts)
-    counts[...] = jnp.zeros_like(counts)
-    zero = jnp.zeros((LEAVES, 128), F32)
-    _, _, most = lax.fori_loop(
-        0, CHUNKS, rank, (jnp.zeros((OWNERS, 128), F32), zero, zero), unroll=16
+    bases[...] = jnp.zeros_like(bases)
+    lax.fori_loop(
+        0, CHUNKS, rank, (jnp.zeros((OWNERS, 128), F32), jnp.zeros((LEAVES, 128), F32)), unroll=16
     )
-    full = jnp.maximum(jnp.max(most, 0, keepdims=True) - BIN, 0.0)
+
+    rest = jnp.zeros((128 - LEAVES, 128), F32)
+    start_of = jnp.concatenate([starts[...], rest], 0).T[:CHUNKS]
+    base_of = jnp.concatenate([bases[...], rest], 0).T[:CHUNKS]
+    chunk = iota((CHUNKS, 128), 0)
+    base_of = base_of + (chunk * CHUNK).astype(F32)
+    chunk = chunk.astype(F32)
+    first = 8.0 * iota((1, 128), 1).astype(F32)
+    used = iota((1, 128), 1) < TILES
+    full = jnp.zeros((1, 128), F32)
+    table[...] = jnp.zeros_like(table)
+    for i in range(LEAVES):
+        begin = jnp.broadcast_to(start_of[:, i : i + 1], (CHUNKS, 128))
+        place = jnp.broadcast_to(base_of[:, i : i + 1], (CHUNKS, 128))
+        passed = (begin <= first) & (chunk > 0.0)
+        current = jnp.sum(jnp.where(passed, 1.0, 0.0), 0, keepdims=True)
+        for r in range(4):
+            here = chunk == current + r
+            row = jnp.sum(jnp.where(here, place, 0.0), 0, keepdims=True)
+            edge = jnp.sum(jnp.where(here, begin, 0.0), 0, keepdims=True)
+            edge = jnp.where(current + r < CHUNKS, edge, float(PER)) - first
+            if r == 0:
+                row = jnp.clip(jnp.where(used, row - edge, 0.0), 0.0, float(ROWS))
+                table[i, 0:1, :] = row.astype(jnp.int32)
+            elif r < 3:
+                edge = jnp.where(used, jnp.clip(edge, 0.0, 8.0), 8.0)
+                row = jnp.where(used & (current + r < CHUNKS), row - edge, 0.0)
+                table[i, r : r + 1, :] = jnp.clip(row, 0.0, float(ROWS)).astype(jnp.int32)
+                table[i, r + 2 : r + 3, :] = edge.astype(jnp.int32)
+            else:
+                full = jnp.maximum(full, jnp.where(used & (edge < 8.0), 1.0, 0.0))
+    full = jnp.broadcast_to(jnp.max(full, 1, keepdims=True), (1, 128))
+    tell = pltpu.make_async_copy(table, scal, local.at[4])
+    tell.start()
 
     held[0] = pivots[...]
     pl.semaphore_wait(barrier, LEAVES + COLS - 2)
@@ -648,47 +680,48 @@
         extra = jnp.where(row == 0, ranked[t, 1:2, :], 0.0).astype(BF)
         return jnp.concatenate([feat_in[:, pl.ds(pl.multiple_of(t * CHUNK, CHUNK), CHUNK)], extra], 0)
 
-    def fill_bins(t, _):
+    def sort(t, _):
         place = ranked[t, 0:1, :].astype(jnp.int32)
-        chosen = (iota((LEAVES * BIN, CHUNK), 0) == place).astype(F32).astype(BF)
-        binned = dot_nt(chosen, joined_of(t))
-        for i in range(LEAVES):
-            bins[i, pl.ds(pl.multiple_of(t * BIN, 8), BIN), :] = binned[i * BIN : (i + 1) * BIN]
+        chosen = (iota((CHUNK, CHUNK), 0) == place).astype(F32).astype(BF)
+        ybuf[pl.ds(pl.multiple_of(t * CHUNK, CHUNK), CHUNK), :] = dot_nt(chosen, joined_of(t))
         return 0
 
     bring.wait()
-    lax.fori_loop(0, CHUNKS, fill_bins, 0, unroll=4)
-
-    spot, chunk = iota((128, BINS), 1), iota((128, BINS), 0)
-    inside = (spot >= chunk * BIN) & (spot < chunk * BIN + BIN)
-    offset = spot[0:1] - jnp.sum(jnp.where(inside, chunk * BIN, 0), 0, keepdims=True)
-    offset = offset.astype(F32)
-    high = jnp.where(starts[...] >= 256.0, 256.0, 0.0)
-    parts = jnp.concatenate([high, starts[...] - high, counts[...]], 0).astype(BF)
-    parts = dot(parts, inside.astype(F32).astype(BF))
-    table = parts[:LEAVES] + parts[LEAVES : 2 * LEAVES] + offset
-    table = jnp.where(offset < parts[2 * LEAVES :], table, -1.0)
-    for i in range(LEAVES):
-        places[i] = table[i : i + 1]
+    lax.fori_loop(0, CHUNKS, sort, 0, unroll=8)
+    ybuf[ROWS:, :] = jnp.zeros((16, WIDE), F32)
+    tell.wait()
 
     eye = (iota((WIDE, WIDE), 0) == iota((WIDE, WIDE), 1)).astype(F32).astype(BF)
+    sub = iota((8, WIDE), 0)
 
     def packet(k):
         to = lax.rem(leaf + k, jnp.int32(LEAVES))
-        chosen = (iota((PER, BINS), 0).astype(F32) == places[to]).astype(F32).astype(BF)
-        packed = dot(chosen, bins[to].astype(BF)).astype(BF)
-        turned = dot_nt(eye, packed)
+        tiles = []
+        for q in range(TILES):
+            tile = ybuf[pl.ds(jnp.clip(scal[to, 0, q], 0, ROWS), 8), :]
+            for r in (1, 2):
+                later = ybuf[pl.ds(jnp.clip(scal[to, r, q], 0, ROWS), 8), :]
+                tile = jnp.where(sub >= scal[to, r + 2, q], later, tile)
+            tiles.append(tile)
+        turned = dot_nt(eye, jnp.concatenate(tiles, 0).astype(BF))
         feat[k] = turned[:F].astype(BF)
         aux[k] = jnp.concatenate([turned[F : F + 1, 128 * c : 128 * c + 128] for c in range(4)] * 2, 0)
 
-    def give(n, _):
-        k = turn_of(n)
-        packet(k)
-        send_aux(k).start()
-        send_feat(k).start()
+    def give(j, _):
+        steps = turn_of(2 * j + 1), turn_of(rem(2 * j + 2, LEAVES))
+        for k in steps:
+            packet(k)
+        send_aux(steps[0]).start()
+        send_feat(steps[0]).start()
+
+        @pl.when(j < LEAVES // 2 - 1)
+        def second():
+            send_aux(steps[1]).start()
+            send_feat(steps[1]).start()
+
         return 0
 
-    lax.fori_loop(1, 4, give, 0)
+    lax.fori_loop(0, 2, give, 0)
 
     each(LEAVES, lambda k: send_pivots(k).wait_recv())
     place = jnp.concatenate([held[(LEAVES - b) % LEAVES] for b in range(LEAVES)], 0)
@@ -723,7 +756,7 @@
         slots[b] = taken[b * SLOTS : (b + 1) * SLOTS]
     came[0] = slots[0]
     each(LEAVES, lambda k: send_slots(k).start())
-    lax.fori_loop(4, 11, give, 0)
+    lax.fori_loop(2, 5, give, 0)
 
     each(LEAVES, lambda k: send_slots(k).wait_recv())
     got = jnp.concatenate([came[b] for b in range(LEAVES)], 0).astype(F32)
@@ -732,8 +765,7 @@
     full = jnp.broadcast_to(jnp.max(got[:, FULL : FULL + 1], 0, keepdims=True), (1, 128))
     sk[0] = picked.astype(BF)
     each(COLS, lambda k: send_skel(k).start())
-    lax.fori_loop(11, LEAVES, give, 0)
-    packet(0)
+    lax.fori_loop(5, LEAVES // 2, give, 0)
     rx[0] = feat[0]
     ra[0] = aux[0]
 
@@ -1003,7 +1035,7 @@
             *dma(COLS),
             *dma(4),
             *dma(4),
-            pltpu.SemaphoreType.DMA((4,)),
+            pltpu.SemaphoreType.DMA((5,)),
         ],
         compiler_params=params(0, 40),
         name="exchange",
@@ -1025,8 +1057,9 @@
             pltpu.VMEM((CHUNKS, 8, CHUNK), F32),
             pltpu.VMEM((LEAVES, 128), F32),
             pltpu.VMEM((LEAVES, 128), F32),
-            pltpu.VMEM((LEAVES, 1, BINS), F32),
-            pltpu.VMEM((LEAVES, BINS, WIDE), F32),
+            pltpu.VMEM((ROWS + 16, WIDE), F32),
+            pltpu.VMEM((LEAVES, 8, 128), jnp.int32),
+            pltpu.SMEM((LEAVES, 8, 128), jnp.int32),
             pltpu.VMEM((LEAVES, 1, RANK), jnp.int32),
             pltpu.VMEM((LEAVES, SLOTS, 128), BF),
             pltpu.VMEM((LEAVES, SLOTS, 128), BF),
@@ -1076,7 +1109,7 @@
             *dma(COLS),
             *dma(4),
             *dma(4),
-            pltpu.SemaphoreType.DMA((4,)),
+            pltpu.SemaphoreType.DMA((5,)),
         ],
         compiler_params=params(1, 40),
         name="stream",

time: 53.5 us -> 50.9 us (0.951)
  Pallas kernels: 51 us -> 48.3 us
    pallas_call x1, Pallas kernels: 50.3 us -> 47.7 us  [stream(): pl.pallas_call(stream_kernel, out_shape=(*(pltpu.VMEM(shape, F32) for sha...]
where the time goes in v9:
time: 50.9 us; the launch traced here: 50.7 us
  Pallas kernels  48.3 us (95%)
  between operations  2.08 us (4%)
    pallas_call x1, Pallas kernels, stream(): pl.pallas_call(stream_kernel, out_shape=(*(pltpu.VMEM(shape, F32) for sha...  47.7 us

profile of v9, /device:TPU:1, one launch (start us, length us, event | category | flops | bytes accessed | tf_op | source)
XLA Modules:
  0.0 50.7 jit_solution(12788377761689029736)
XLA Ops:
  1.3 47.7 %stream.1 = (f32[1,32,512]{2,1,0:T(8,128)S(1)}, f32[1,32,256]{2,1,0:T(8,128)S(1)}, f32[1,256]{1,0:T(1,128)S(1)}, s32[1]{0:T(128)}) custom-call(bf16[48,8192]{1,0:T(8,128)(2,1)} %feat_hbm.1, bf16[64,128]{1,0:T(8,128)(2,1)} %bitcast.8, s32[64,128]{1,0:T(8,128)} %bitcast.6, s32[1,256]{1,0:T(1,128)} %pivots.1, f32[1,1]{1,0:T(1,128)} %bitcast.5.ridge, ...), custom_call_target="tpu_custom_call" | custom-call | tf_op jit(solution)/shard_map/stream/pallas_call | solution.py:1046
  49.6 0.9 %conditional.1 = ((f32[1,32,512]{2,1,0:T(8,128)}, f32[1,32,256]{2,1,0:T(8,128)}, f32[1,256]{1,0:T(1,128)})) conditional(s32[]{:T(128)} %bitcast.4, (f32[1,32,512]{2,1,0:T(8,128)S(1)}, f32[1,32,256]{2,1,0:T(8,128)S(1)}, f32[1,256]{1,0:T(1,128)S(1)}) %tuple.13, (bf16[48,8192]{1,0:T(8,128)(2,1)}, bf16[64,128]{1,0:T(8,128)(2,1)}, s32[64,128]{1,0:T(8,128)}, ...), branch_computations={%region_0.0_spmd, %region_1.0_spmd} | conditional | bytes 8 | solution.py:1149
  49.6 0.7 %emit.2 = (f32[1,32,512]{2,1,0:T(8,128)}, f32[1,32,256]{2,1,0:T(8,128)}, f32[1,256]{1,0:T(1,128)}) custom-call(f32[1,32,512]{2,1,0:T(8,128)S(1)} %get-tuple-element.22.refs_0_, f32[1,32,256]{2,1,0:T(8,128)S(1)} %get-tuple-element.23.refs_1_, f32[1,256]{1,0:T(1,128)S(1)} %get-tuple-element.24.refs_2_), custom_call_target="tpu_custom_call" | custom-call | tf_op jit(solution)/shard_map/cond/branch_0_fun/emit/pallas_call | solution.py:1129

commit v10 on v9

--- a/solution.py
+++ b/solution.py
@@ -20,7 +20,10 @@
 CHUNKS = ROWS // CHUNK
 WINDOW = 40
 REGION = PER + WINDOW
-TILES = PER // 8
+TILE = 32
+TILES = PER // TILE
+PIECES = 6
+AT_ONCE = 128 // TILES
 SLOTS = 16
 WHICH = 50
 FULL = 51
@@ -640,33 +643,32 @@
     rest = jnp.zeros((128 - LEAVES, 128), F32)
     start_of = jnp.concatenate([starts[...], rest], 0).T[:CHUNKS]
     base_of = jnp.concatenate([bases[...], rest], 0).T[:CHUNKS]
-    chunk = iota((CHUNKS, 128), 0)
-    base_of = base_of + (chunk * CHUNK).astype(F32)
-    chunk = chunk.astype(F32)
-    first = 8.0 * iota((1, 128), 1).astype(F32)
-    used = iota((1, 128), 1) < TILES
+    high = jnp.where(start_of >= 256.0, 256.0, 0.0)
+    columns_of = jnp.concatenate([high, start_of - high, base_of], 0).astype(BF)
+    chunk = iota((CHUNKS, 128), 0).astype(F32)
+    first = (iota((1, 128), 1) % TILES * TILE).astype(F32)
     full = jnp.zeros((1, 128), F32)
     table[...] = jnp.zeros_like(table)
-    for i in range(LEAVES):
-        begin = jnp.broadcast_to(start_of[:, i : i + 1], (CHUNKS, 128))
-        place = jnp.broadcast_to(base_of[:, i : i + 1], (CHUNKS, 128))
+    for g in range(LEAVES // AT_ONCE):
+        one = iota((128, 128), 0) == iota((128, 128), 1) // TILES + g * AT_ONCE
+        spread_out = dot(columns_of, one.astype(F32).astype(BF))
+        begin = spread_out[:CHUNKS] + spread_out[CHUNKS : 2 * CHUNKS]
+        place = spread_out[2 * CHUNKS :] + chunk * CHUNK
         passed = (begin <= first) & (chunk > 0.0)
         current = jnp.sum(jnp.where(passed, 1.0, 0.0), 0, keepdims=True)
-        for r in range(4):
+        for r in range(PIECES + 1):
             here = chunk == current + r
             row = jnp.sum(jnp.where(here, place, 0.0), 0, keepdims=True)
             edge = jnp.sum(jnp.where(here, begin, 0.0), 0, keepdims=True)
             edge = jnp.where(current + r < CHUNKS, edge, float(PER)) - first
-            if r == 0:
-                row = jnp.clip(jnp.where(used, row - edge, 0.0), 0.0, float(ROWS))
-                table[i, 0:1, :] = row.astype(jnp.int32)
-            elif r < 3:
-                edge = jnp.where(used, jnp.clip(edge, 0.0, 8.0), 8.0)
-                row = jnp.where(used & (current + r < CHUNKS), row - edge, 0.0)
-                table[i, r : r + 1, :] = jnp.clip(row, 0.0, float(ROWS)).astype(jnp.int32)
-                table[i, r + 2 : r + 3, :] = edge.astype(jnp.int32)
-            else:
-                full = jnp.maximum(full, jnp.where(used & (edge < 8.0), 1.0, 0.0))
+            if r == PIECES:
+                full = jnp.maximum(full, jnp.where(edge < TILE, 1.0, 0.0))
+                continue
+            if r:
+                edge = jnp.clip(edge, 0.0, float(TILE))
+                table[g, PIECES + r : PIECES + r + 1, :] = edge.astype(jnp.int32)
+            row = jnp.clip(jnp.where(current + r < CHUNKS, row - edge, 0.0), 0.0, float(ROWS))
+            table[g, r : r + 1, :] = row.astype(jnp.int32)
     full = jnp.broadcast_to(jnp.max(full, 1, keepdims=True), (1, 128))
     tell = pltpu.make_async_copy(table, scal, local.at[4])
     tell.start()
@@ -688,20 +690,25 @@
 
     bring.wait()
     lax.fori_loop(0, CHUNKS, sort, 0, unroll=8)
-    ybuf[ROWS:, :] = jnp.zeros((16, WIDE), F32)
+    ybuf[ROWS:, :] = jnp.zeros((TILE, WIDE), F32)
     tell.wait()
 
     eye = (iota((WIDE, WIDE), 0) == iota((WIDE, WIDE), 1)).astype(F32).astype(BF)
-    sub = iota((8, WIDE), 0)
+    sub = iota((TILE, WIDE), 0)
 
     def packet(k):
         to = lax.rem(leaf + k, jnp.int32(LEAVES))
+        group = lax.div(to, jnp.int32(AT_ONCE))
+        lane = lax.rem(to, jnp.int32(AT_ONCE)) * TILES
+
+        def piece(r, q):
+            return ybuf[pl.ds(jnp.clip(scal[group, r, lane + q], 0, ROWS), TILE), :]
+
         tiles = []
         for q in range(TILES):
-            tile = ybuf[pl.ds(jnp.clip(scal[to, 0, q], 0, ROWS), 8), :]
-            for r in (1, 2):
-                later = ybuf[pl.ds(jnp.clip(scal[to, r, q], 0, ROWS), 8), :]
-                tile = jnp.where(sub >= scal[to, r + 2, q], later, tile)
+            tile = piece(0, q)
+            for r in range(1, PIECES):
+                tile = jnp.where(sub >= scal[group, PIECES + r, lane + q], piece(r, q), tile)
             tiles.append(tile)
         turned = dot_nt(eye, jnp.concatenate(tiles, 0).astype(BF))
         feat[k] = turned[:F].astype(BF)
@@ -1057,9 +1064,9 @@
             pltpu.VMEM((CHUNKS, 8, CHUNK), F32),
             pltpu.VMEM((LEAVES, 128), F32),
             pltpu.VMEM((LEAVES, 128), F32),
-            pltpu.VMEM((ROWS + 16, WIDE), F32),
-            pltpu.VMEM((LEAVES, 8, 128), jnp.int32),
-            pltpu.SMEM((LEAVES, 8, 128), jnp.int32),
+            pltpu.VMEM((ROWS + TILE, WIDE), F32),
+            pltpu.VMEM((LEAVES // AT_ONCE, 16, 128), jnp.int32),
+            pltpu.SMEM((LEAVES // AT_ONCE, 16, 128), jnp.int32),
             pltpu.VMEM((LEAVES, 1, RANK), jnp.int32),
             pltpu.VMEM((LEAVES, SLOTS, 128), BF),
             pltpu.VMEM((LEAVES, SLOTS, 128), BF),

time: 50.9 us -> 50.8 us (level)
  no operation moved by 1% of the time
where the time goes in v10:
time: 50.8 us; the launch traced here: 50.6 us
  Pallas kernels  48.3 us (95%)
  between operations  2.08 us (4%)
    pallas_call x1, Pallas kernels, stream(): pl.pallas_call(stream_kernel, out_shape=(*(pltpu.VMEM(shape, F32) for sha...  47.6 us

profile of v10, /device:TPU:1, one launch (start us, length us, event | category | flops | bytes accessed | tf_op | source)
XLA Modules:
  0.0 50.6 jit_solution(9821633317060504744)
XLA Ops:
  1.3 47.6 %stream.1 = (f32[1,32,512]{2,1,0:T(8,128)S(1)}, f32[1,32,256]{2,1,0:T(8,128)S(1)}, f32[1,256]{1,0:T(1,128)S(1)}, s32[1]{0:T(128)}) custom-call(bf16[48,8192]{1,0:T(8,128)(2,1)} %feat_hbm.1, bf16[64,128]{1,0:T(8,128)(2,1)} %bitcast.8, s32[64,128]{1,0:T(8,128)} %bitcast.6, s32[1,256]{1,0:T(1,128)} %pivots.1, f32[1,1]{1,0:T(1,128)} %bitcast.5.ridge, ...), custom_call_target="tpu_custom_call" | custom-call | tf_op jit(solution)/shard_map/stream/pallas_call | solution.py:1053
  49.5 0.9 %conditional.1 = ((f32[1,32,512]{2,1,0:T(8,128)}, f32[1,32,256]{2,1,0:T(8,128)}, f32[1,256]{1,0:T(1,128)})) conditional(s32[]{:T(128)} %bitcast.4, (f32[1,32,512]{2,1,0:T(8,128)S(1)}, f32[1,32,256]{2,1,0:T(8,128)S(1)}, f32[1,256]{1,0:T(1,128)S(1)}) %tuple.13, (bf16[48,8192]{1,0:T(8,128)(2,1)}, bf16[64,128]{1,0:T(8,128)(2,1)}, s32[64,128]{1,0:T(8,128)}, ...), branch_computations={%region_0.0_spmd, %region_1.0_spmd} | conditional | bytes 8 | solution.py:1156
  49.5 0.7 %emit.2 = (f32[1,32,512]{2,1,0:T(8,128)}, f32[1,32,256]{2,1,0:T(8,128)}, f32[1,256]{1,0:T(1,128)}) custom-call(f32[1,32,512]{2,1,0:T(8,128)S(1)} %get-tuple-element.22.refs_0_, f32[1,32,256]{2,1,0:T(8,128)S(1)} %get-tuple-element.23.refs_1_, f32[1,256]{1,0:T(1,128)S(1)} %get-tuple-element.24.refs_2_), custom_call_target="tpu_custom_call" | custom-call | tf_op jit(solution)/shard_map/cond/branch_0_fun/emit/pallas_call | solution.py:1136

commit v11 on v10

--- a/solution.py
+++ b/solution.py
@@ -568,6 +568,9 @@
     each(4, finish((send_top, send_top_rhs)))
 
 
+FAR_FIRST = (12, 13, 4, 5, 11, 14, 3, 6, 10, 15, 2, 7, 9, 8, 1)
+
+
 def stream_kernel(
     feat_hbm, target, owner, pivots, ridge, scales_hbm, parent_hbm, top_hbm,
     out_share, out_top, out_rhs, flag,
@@ -636,9 +639,14 @@
 
     starts[...] = jnp.zeros_like(starts)
     bases[...] = jnp.zeros_like(bases)
-    lax.fori_loop(
-        0, CHUNKS, rank, (jnp.zeros((OWNERS, 128), F32), jnp.zeros((LEAVES, 128), F32)), unroll=16
-    )
+    seen = (jnp.zeros((OWNERS, 128), F32), jnp.zeros((LEAVES, 128), F32))
+    seen = lax.fori_loop(0, CHUNKS // 2, rank, seen, unroll=16)
+
+    held[0] = pivots[...]
+    pl.semaphore_wait(barrier, LEAVES + COLS - 2)
+    for k in FAR_FIRST:
+        send_pivots(k).start()
+    lax.fori_loop(CHUNKS // 2, CHUNKS, rank, seen, unroll=16)
 
     rest = jnp.zeros((128 - LEAVES, 128), F32)
     start_of = jnp.concatenate([starts[...], rest], 0).T[:CHUNKS]
@@ -673,10 +681,6 @@
     tell = pltpu.make_async_copy(table, scal, local.at[4])
     tell.start()
 
-    held[0] = pivots[...]
-    pl.semaphore_wait(barrier, LEAVES + COLS - 2)
-    each(LEAVES, lambda k: send_pivots(k).start())
-
     def joined_of(t):
         row = iota((16, CHUNK), 0)
         extra = jnp.where(row == 0, ranked[t, 1:2, :], 0.0).astype(BF)
@@ -728,7 +732,7 @@
 
         return 0
 
-    lax.fori_loop(0, 2, give, 0)
+    lax.fori_loop(0, 3, give, 0)
 
     each(LEAVES, lambda k: send_pivots(k).wait_recv())
     place = jnp.concatenate([held[(LEAVES - b) % LEAVES] for b in range(LEAVES)], 0)
@@ -762,8 +766,9 @@
     for b in range(LEAVES):
         slots[b] = taken[b * SLOTS : (b + 1) * SLOTS]
     came[0] = slots[0]
-    each(LEAVES, lambda k: send_slots(k).start())
-    lax.fori_loop(2, 5, give, 0)
+    for k in FAR_FIRST:
+        send_slots(k).start()
+    lax.fori_loop(3, 6, give, 0)
 
     each(LEAVES, lambda k: send_slots(k).wait_recv())
     got = jnp.concatenate([came[b] for b in range(LEAVES)], 0).astype(F32)
@@ -771,8 +776,9 @@
     picked = dot(got.T[:F].astype(BF), chosen.astype(F32).astype(BF))
     full = jnp.broadcast_to(jnp.max(got[:, FULL : FULL + 1], 0, keepdims=True), (1, 128))
     sk[0] = picked.astype(BF)
-    each(COLS, lambda k: send_skel(k).start())
-    lax.fori_loop(5, LEAVES // 2, give, 0)
+    for k in (5, 3, 4, 6, 2, 7, 1):
+        send_skel(k).start()
+    lax.fori_loop(6, LEAVES // 2, give, 0)
     rx[0] = feat[0]
     ra[0] = aux[0]
 
@@ -805,6 +811,18 @@
     def norms(k):
         side[k] = point_side(rx[k].astype(F32), scale4)
 
+    def receive(k):
+        send_aux(k).wait_recv()
+        send_feat(k).wait_recv()
+
+    def early_norms(n, _):
+        k = turn_of(n)
+        pl.when(n > 0)(lambda: receive(k))
+        norms(k)
+        return 0
+
+    lax.fori_loop(0, LEAVES // 2, early_norms, 0)
+
     def add_skel(k, total):
         send_skel(k).wait_recv()
         return total + sk[k].astype(F32)
@@ -842,19 +860,18 @@
 
     def own_two(j, _):
         k, l = turn_of(2 * j), turn_of(2 * j + 1)
-        pl.when(j > 0)(lambda: receive(k))
-        receive(l)
-        norms(k)
-        norms(l)
+        @pl.when(j >= LEAVES // 4)
+        def late():
+            receive(k)
+            receive(l)
+            norms(k)
+            norms(l)
+
         own_of(k, even.at[j])
         gram_of(odd.at[rem(j + last, last + 1)])
         own_of(l, odd.at[j])
         gram_of(even.at[j])
         return 0
-
-    def receive(k):
-        send_aux(k).wait_recv()
-        send_feat(k).wait_recv()
 
     def other_two(j, _):
         block_of(turn_of(2 * j), other_even, RANK)

time: 50.8 us -> 51.7 us (1.018)
  Pallas kernels: 48.3 us -> 49.2 us
    pallas_call x1, Pallas kernels: 47.6 us -> 48.5 us  [stream(): pl.pallas_call(stream_kernel, out_shape=(*(pltpu.VMEM(shape, F32) for sha...]
where the time goes in v11:
time: 51.7 us; the launch traced here: 51.5 us
  Pallas kernels  49.2 us (95%)
  between operations  2.08 us (4%)
    pallas_call x1, Pallas kernels, stream(): pl.pallas_call(stream_kernel, out_shape=(*(pltpu.VMEM(shape, F32) for sha...  48.5 us

profile of v11, /device:TPU:1, one launch (start us, length us, event | category | flops | bytes accessed | tf_op | source)
XLA Modules:
  0.0 51.5 jit_solution(15741769160310442462)
XLA Ops:
  1.3 48.5 %stream.1 = (f32[1,32,512]{2,1,0:T(8,128)S(1)}, f32[1,32,256]{2,1,0:T(8,128)S(1)}, f32[1,256]{1,0:T(1,128)S(1)}, s32[1]{0:T(128)}) custom-call(bf16[48,8192]{1,0:T(8,128)(2,1)} %feat_hbm.1, bf16[64,128]{1,0:T(8,128)(2,1)} %bitcast.8, s32[64,128]{1,0:T(8,128)} %bitcast.6, s32[1,256]{1,0:T(1,128)} %pivots.1, f32[1,1]{1,0:T(1,128)} %bitcast.5.ridge, ...), custom_call_target="tpu_custom_call" | custom-call | tf_op jit(solution)/shard_map/stream/pallas_call | solution.py:1070
  50.4 0.9 %conditional.1 = ((f32[1,32,512]{2,1,0:T(8,128)}, f32[1,32,256]{2,1,0:T(8,128)}, f32[1,256]{1,0:T(1,128)})) conditional(s32[]{:T(128)} %bitcast.4, (f32[1,32,512]{2,1,0:T(8,128)S(1)}, f32[1,32,256]{2,1,0:T(8,128)S(1)}, f32[1,256]{1,0:T(1,128)S(1)}) %tuple.13, (bf16[48,8192]{1,0:T(8,128)(2,1)}, bf16[64,128]{1,0:T(8,128)(2,1)}, s32[64,128]{1,0:T(8,128)}, ...), branch_computations={%region_0.0_spmd, %region_1.0_spmd} | conditional | bytes 8 | solution.py:1173
  50.4 0.7 %emit.2 = (f32[1,32,512]{2,1,0:T(8,128)}, f32[1,32,256]{2,1,0:T(8,128)}, f32[1,256]{1,0:T(1,128)}) custom-call(f32[1,32,512]{2,1,0:T(8,128)S(1)} %get-tuple-element.22.refs_0_, f32[1,32,256]{2,1,0:T(8,128)S(1)} %get-tuple-element.23.refs_1_, f32[1,256]{1,0:T(1,128)S(1)} %get-tuple-element.24.refs_2_), custom_call_target="tpu_custom_call" | custom-call | tf_op jit(solution)/shard_map/cond/branch_0_fun/emit/pallas_call | solution.py:1153

commit v12 on v10

--- a/solution.py
+++ b/solution.py
@@ -728,7 +728,7 @@
 
         return 0
 
-    lax.fori_loop(0, 2, give, 0)
+    lax.fori_loop(0, 1, give, 0)
 
     each(LEAVES, lambda k: send_pivots(k).wait_recv())
     place = jnp.concatenate([held[(LEAVES - b) % LEAVES] for b in range(LEAVES)], 0)
@@ -763,7 +763,7 @@
         slots[b] = taken[b * SLOTS : (b + 1) * SLOTS]
     came[0] = slots[0]
     each(LEAVES, lambda k: send_slots(k).start())
-    lax.fori_loop(2, 5, give, 0)
+    lax.fori_loop(1, 3, give, 0)
 
     each(LEAVES, lambda k: send_slots(k).wait_recv())
     got = jnp.concatenate([came[b] for b in range(LEAVES)], 0).astype(F32)
@@ -772,7 +772,7 @@
     full = jnp.broadcast_to(jnp.max(got[:, FULL : FULL + 1], 0, keepdims=True), (1, 128))
     sk[0] = picked.astype(BF)
     each(COLS, lambda k: send_skel(k).start())
-    lax.fori_loop(5, LEAVES // 2, give, 0)
+    lax.fori_loop(3, LEAVES // 2, give, 0)
     rx[0] = feat[0]
     ra[0] = aux[0]
 

time: 50.8 us -> 52.5 us (1.033)
  Pallas kernels: 48.3 us -> 50 us
    pallas_call x1, Pallas kernels: 47.6 us -> 49.3 us  [stream(): pl.pallas_call(stream_kernel, out_shape=(*(pltpu.VMEM(shape, F32) for sha...]
where the time goes in v12:
time: 52.5 us; the launch traced here: 52.3 us
  Pallas kernels  50 us (95%)
  between operations  2.08 us (4%)
    pallas_call x1, Pallas kernels, stream(): pl.pallas_call(stream_kernel, out_shape=(*(pltpu.VMEM(shape, F32) for sha...  49.3 us

profile of v12, /device:TPU:1, one launch (start us, length us, event | category | flops | bytes accessed | tf_op | source)
XLA Modules:
  0.0 52.3 jit_solution(15647314496299843265)
XLA Ops:
  1.3 49.3 %stream.1 = (f32[1,32,512]{2,1,0:T(8,128)S(1)}, f32[1,32,256]{2,1,0:T(8,128)S(1)}, f32[1,256]{1,0:T(1,128)S(1)}, s32[1]{0:T(128)}) custom-call(bf16[48,8192]{1,0:T(8,128)(2,1)} %feat_hbm.1, bf16[64,128]{1,0:T(8,128)(2,1)} %bitcast.8, s32[64,128]{1,0:T(8,128)} %bitcast.6, s32[1,256]{1,0:T(1,128)} %pivots.1, f32[1,1]{1,0:T(1,128)} %bitcast.5.ridge, ...), custom_call_target="tpu_custom_call" | custom-call | tf_op jit(solution)/shard_map/stream/pallas_call | solution.py:1053
  51.2 0.9 %conditional.1 = ((f32[1,32,512]{2,1,0:T(8,128)}, f32[1,32,256]{2,1,0:T(8,128)}, f32[1,256]{1,0:T(1,128)})) conditional(s32[]{:T(128)} %bitcast.4, (f32[1,32,512]{2,1,0:T(8,128)S(1)}, f32[1,32,256]{2,1,0:T(8,128)S(1)}, f32[1,256]{1,0:T(1,128)S(1)}) %tuple.13, (bf16[48,8192]{1,0:T(8,128)(2,1)}, bf16[64,128]{1,0:T(8,128)(2,1)}, s32[64,128]{1,0:T(8,128)}, ...), branch_computations={%region_0.0_spmd, %region_1.0_spmd} | conditional | bytes 8 | solution.py:1156
  51.2 0.7 %emit.2 = (f32[1,32,512]{2,1,0:T(8,128)}, f32[1,32,256]{2,1,0:T(8,128)}, f32[1,256]{1,0:T(1,128)}) custom-call(f32[1,32,512]{2,1,0:T(8,128)S(1)} %get-tuple-element.22.refs_0_, f32[1,32,256]{2,1,0:T(8,128)S(1)} %get-tuple-element.23.refs_1_, f32[1,256]{1,0:T(1,128)S(1)} %get-tuple-element.24.refs_2_), custom_call_target="tpu_custom_call" | custom-call | tf_op jit(solution)/shard_map/cond/branch_0_fun/emit/pallas_call | solution.py:1136

commit v13 on v10

--- a/solution.py
+++ b/solution.py
@@ -805,6 +805,18 @@
     def norms(k):
         side[k] = point_side(rx[k].astype(F32), scale4)
 
+    def receive(k):
+        send_aux(k).wait_recv()
+        send_feat(k).wait_recv()
+
+    def early_norms(n, _):
+        k = turn_of(n)
+        pl.when(n > 0)(lambda: receive(k))
+        norms(k)
+        return 0
+
+    lax.fori_loop(0, LEAVES // 2, early_norms, 0)
+
     def add_skel(k, total):
         send_skel(k).wait_recv()
         return total + sk[k].astype(F32)
@@ -842,19 +854,18 @@
 
     def own_two(j, _):
         k, l = turn_of(2 * j), turn_of(2 * j + 1)
-        pl.when(j > 0)(lambda: receive(k))
-        receive(l)
-        norms(k)
-        norms(l)
+        @pl.when(j >= LEAVES // 4)
+        def late():
+            receive(k)
+            receive(l)
+            norms(k)
+            norms(l)
+
         own_of(k, even.at[j])
         gram_of(odd.at[rem(j + last, last + 1)])
         own_of(l, odd.at[j])
         gram_of(even.at[j])
         return 0
-
-    def receive(k):
-        send_aux(k).wait_recv()
-        send_feat(k).wait_recv()
 
     def other_two(j, _):
         block_of(turn_of(2 * j), other_even, RANK)
@@ -888,15 +899,7 @@
         part = gram[0:RANK, :].astype(BF)
         for k in range(COLS):
             pg[k] = part[k * SLAB : (k + 1) * SLAB]
-        rhs = gram[RANK : RANK + 1, :]
-        rhs = jnp.sum(dot_nt(stack16(split3(rhs), RANK), rows[...]), 0, keepdims=True)
-        rs[...] = jnp.zeros_like(rs)
-        rs[0:1, :] = rhs[:, :128]
-        rs[1:2, :] = rhs[:, 128:]
-        rs[2:3, :] = full
         each(COLS, lambda k: send_gram(k).start())
-        each(COLS, lambda k: send_rhs(k).start())
-        tops[...] = dot_nt(dot(rows[...], part).astype(BF), columns[:, 0:RANK])
 
     def half(h, _):
         pairs = LEAVES // 4
@@ -909,12 +912,21 @@
     lax.fori_loop(0, 2, half, 0)
     couple_of(other_odd, odd.at[last])
 
-    part = couple[...].astype(BF)
-    chosen = dot_nt(dot_nt(rows[...], part).astype(BF), columns[:, RANK:]) + tops[...]
+    rhs = gram[RANK : RANK + 1, :]
+    rhs = jnp.sum(dot_nt(stack16(split3(rhs), RANK), rows[...]), 0, keepdims=True)
+    rs[...] = jnp.zeros_like(rs)
+    rs[0:1, :] = rhs[:, :128]
+    rs[1:2, :] = rhs[:, 128:]
+    rs[2:3, :] = full
+    part = dot(rows[...], gram[0:RANK, :].astype(BF)).astype(BF)
+    chosen = dot_nt(part, columns[:, 0:RANK])
+    part = dot_nt(rows[...], couple[...].astype(BF)).astype(BF)
+    chosen = chosen + dot_nt(part, columns[:, RANK:])
     chosen = chosen.astype(BF)
     for k in range(COLS):
         pt[k] = chosen[k * SLAB : (k + 1) * SLAB]
     each(COLS, lambda k: send_chosen(k).start())
+    each(COLS, lambda k: send_rhs(k).start())
     part = couple[...].T.astype(BF)
     for k in range(COLS):
         pc[k] = part[k * SLAB : (k + 1) * SLAB]

time: 50.8 us -> 51 us (level)
  no operation moved by 1% of the time
where the time goes in v13:
time: 51 us; the launch traced here: 50.8 us
  Pallas kernels  48.5 us (95%)
  between operations  2.08 us (4%)
    pallas_call x1, Pallas kernels, stream(): pl.pallas_call(stream_kernel, out_shape=(*(pltpu.VMEM(shape, F32) for sha...  47.8 us

profile of v13, /device:TPU:1, one launch (start us, length us, event | category | flops | bytes accessed | tf_op | source)
XLA Modules:
  0.0 50.8 jit_solution(16384098240527764749)
XLA Ops:
  1.3 47.8 %stream.1 = (f32[1,32,512]{2,1,0:T(8,128)S(1)}, f32[1,32,256]{2,1,0:T(8,128)S(1)}, f32[1,256]{1,0:T(1,128)S(1)}, s32[1]{0:T(128)}) custom-call(bf16[48,8192]{1,0:T(8,128)(2,1)} %feat_hbm.1, bf16[64,128]{1,0:T(8,128)(2,1)} %bitcast.8, s32[64,128]{1,0:T(8,128)} %bitcast.6, s32[1,256]{1,0:T(1,128)} %pivots.1, f32[1,1]{1,0:T(1,128)} %bitcast.5.ridge, ...), custom_call_target="tpu_custom_call" | custom-call | tf_op jit(solution)/shard_map/stream/pallas_call | solution.py:1065
  49.7 0.9 %conditional.1 = ((f32[1,32,512]{2,1,0:T(8,128)}, f32[1,32,256]{2,1,0:T(8,128)}, f32[1,256]{1,0:T(1,128)})) conditional(s32[]{:T(128)} %bitcast.4, (f32[1,32,512]{2,1,0:T(8,128)S(1)}, f32[1,32,256]{2,1,0:T(8,128)S(1)}, f32[1,256]{1,0:T(1,128)S(1)}) %tuple.13, (bf16[48,8192]{1,0:T(8,128)(2,1)}, bf16[64,128]{1,0:T(8,128)(2,1)}, s32[64,128]{1,0:T(8,128)}, ...), branch_computations={%region_0.0_spmd, %region_1.0_spmd} | conditional | bytes 8 | solution.py:1168
  49.7 0.7 %emit.2 = (f32[1,32,512]{2,1,0:T(8,128)}, f32[1,32,256]{2,1,0:T(8,128)}, f32[1,256]{1,0:T(1,128)}) custom-call(f32[1,32,512]{2,1,0:T(8,128)S(1)} %get-tuple-element.22.refs_0_, f32[1,32,256]{2,1,0:T(8,128)S(1)} %get-tuple-element.23.refs_1_, f32[1,256]{1,0:T(1,128)S(1)} %get-tuple-element.24.refs_2_), custom_call_target="tpu_custom_call" | custom-call | tf_op jit(solution)/shard_map/cond/branch_0_fun/emit/pallas_call | solution.py:1148

commit v14 on v13

--- a/solution.py
+++ b/solution.py
@@ -571,7 +571,7 @@
 def stream_kernel(
     feat_hbm, target, owner, pivots, ridge, scales_hbm, parent_hbm, top_hbm,
     out_share, out_top, out_rhs, flag,
-    feat_in, goals, ranked, starts, bases, ybuf, table, scal, held, slots, came, scales, parent, top, spare,
+    feat_in, bad, goals, ranked, starts, bases, ybuf, table, scal, held, slots, came, scales, parent, top, spare,
     feat, aux, rx, ra, side, sk, mine, sk4, left, even, odd, other_even, other_odd, gram, couple,
     rows, columns, fours, index, tops, pg, gr, pc, cr, pt, qr, rs, rr, t4, r4,
     s_v, r_v, s_s, r_s, s_f, r_f, s_a, r_a, s_k, r_k, s_4, r_4, s_p, r_p, s_c, r_c, s_o, r_o,
@@ -728,54 +728,61 @@
 
         return 0
 
-    lax.fori_loop(0, 2, give, 0)
-
-    each(LEAVES, lambda k: send_pivots(k).wait_recv())
+    def take_slots():
+        each(LEAVES, lambda k: send_pivots(k).wait_recv())
+        place = jnp.concatenate([held[(LEAVES - b) % LEAVES] for b in range(LEAVES)], 0)
+        home = place % ROWS // PACKET
+        number = ((leaf + iota((LEAVES, RANK), 0)) % LEAVES) * 8 + place // ROWS
+        number = (number * PACKET + place % PACKET).astype(F32)
+        valid = home == leaf * COLS + col
+        order = dot(valid.astype(F32).astype(BF), before)
+        order = jnp.where(valid, order, -1.0)
+
+        def spread(table):
+            return jnp.concatenate(
+                [jnp.broadcast_to(table[b : b + 1], (SLOTS, RANK)) for b in range(LEAVES)], 0
+            )
+
+        shape = (LEAVES * SLOTS, RANK)
+        hit = spread(order) == (iota(shape, 0) % SLOTS).astype(F32)
+        wanted = jnp.sum(jnp.where(hit, spread(number) + 1.0, 0.0), 1, keepdims=True) - 1.0
+        which = jnp.sum(jnp.where(hit, iota(shape, 1).astype(F32) + 1.0, 0.0), 1, keepdims=True) - 1.0
+        wanted = jnp.broadcast_to(wanted, (LEAVES * SLOTS, CHUNK))
+
+        def take(t, total):
+            chosen = (wanted == ranked[t, 2:3, :]).astype(F32).astype(BF)
+            rest = jnp.zeros((128 - WIDE, CHUNK), BF)
+            return total + dot_nt(chosen, jnp.concatenate([joined_of(t), rest], 0))
+
+        shape = (LEAVES * SLOTS, 128)
+        taken = lax.fori_loop(0, CHUNKS, take, jnp.zeros(shape, F32), unroll=4)
+        taken = jnp.where(iota(shape, 1) == WHICH, which, taken)
+        taken = jnp.where(iota(shape, 1) == FULL, full, taken).astype(BF)
+        for b in range(LEAVES):
+            slots[b] = taken[b * SLOTS : (b + 1) * SLOTS]
+        came[0] = slots[0]
+        each(LEAVES, lambda k: send_slots(k).start())
+
+    def place_points():
+        each(LEAVES, lambda k: send_slots(k).wait_recv())
+        got = jnp.concatenate([came[b] for b in range(LEAVES)], 0).astype(F32)
+        chosen = got[:, WHICH : WHICH + 1] == iota((LEAVES * SLOTS, RANK), 1).astype(F32)
+        picked = dot(got.T[:F].astype(BF), chosen.astype(F32).astype(BF))
+        bad[...] = jnp.broadcast_to(jnp.max(got[:, FULL : FULL + 1], 0, keepdims=True), (8, 128))
+        sk[0] = picked.astype(BF)
+        each(COLS, lambda k: send_skel(k).start())
+
+    def work(j, _):
+        pl.when(j == 2)(take_slots)
+        pl.when(j == 5)(place_points)
+        return give(j, 0)
+
+    lax.fori_loop(0, LEAVES // 2, work, 0)
+    rx[0] = feat[0]
+    ra[0] = aux[0]
+
     place = jnp.concatenate([held[(LEAVES - b) % LEAVES] for b in range(LEAVES)], 0)
     home = place % ROWS // PACKET
-    number = ((leaf + iota((LEAVES, RANK), 0)) % LEAVES) * 8 + place // ROWS
-    number = (number * PACKET + place % PACKET).astype(F32)
-    valid = home == leaf * COLS + col
-    order = dot(valid.astype(F32).astype(BF), before)
-    order = jnp.where(valid, order, -1.0)
-
-    def spread(table):
-        return jnp.concatenate(
-            [jnp.broadcast_to(table[b : b + 1], (SLOTS, RANK)) for b in range(LEAVES)], 0
-        )
-
-    shape = (LEAVES * SLOTS, RANK)
-    hit = spread(order) == (iota(shape, 0) % SLOTS).astype(F32)
-    wanted = jnp.sum(jnp.where(hit, spread(number) + 1.0, 0.0), 1, keepdims=True) - 1.0
-    which = jnp.sum(jnp.where(hit, iota(shape, 1).astype(F32) + 1.0, 0.0), 1, keepdims=True) - 1.0
-    wanted = jnp.broadcast_to(wanted, (LEAVES * SLOTS, CHUNK))
-
-    def take(t, total):
-        chosen = (wanted == ranked[t, 2:3, :]).astype(F32).astype(BF)
-        rest = jnp.zeros((128 - WIDE, CHUNK), BF)
-        return total + dot_nt(chosen, jnp.concatenate([joined_of(t), rest], 0))
-
-    shape = (LEAVES * SLOTS, 128)
-    taken = lax.fori_loop(0, CHUNKS, take, jnp.zeros(shape, F32), unroll=4)
-    taken = jnp.where(iota(shape, 1) == WHICH, which, taken)
-    taken = jnp.where(iota(shape, 1) == FULL, full, taken).astype(BF)
-    for b in range(LEAVES):
-        slots[b] = taken[b * SLOTS : (b + 1) * SLOTS]
-    came[0] = slots[0]
-    each(LEAVES, lambda k: send_slots(k).start())
-    lax.fori_loop(2, 5, give, 0)
-
-    each(LEAVES, lambda k: send_slots(k).wait_recv())
-    got = jnp.concatenate([came[b] for b in range(LEAVES)], 0).astype(F32)
-    chosen = got[:, WHICH : WHICH + 1] == iota((LEAVES * SLOTS, RANK), 1).astype(F32)
-    picked = dot(got.T[:F].astype(BF), chosen.astype(F32).astype(BF))
-    full = jnp.broadcast_to(jnp.max(got[:, FULL : FULL + 1], 0, keepdims=True), (1, 128))
-    sk[0] = picked.astype(BF)
-    each(COLS, lambda k: send_skel(k).start())
-    lax.fori_loop(5, LEAVES // 2, give, 0)
-    rx[0] = feat[0]
-    ra[0] = aux[0]
-
     largest = jnp.zeros((OWNERS, 1), F32)
     for b in range(LEAVES):
         held_here = (iota((OWNERS, RANK), 0) == home[b : b + 1]).astype(F32)
@@ -817,6 +824,8 @@
 
     lax.fori_loop(0, LEAVES // 2, early_norms, 0)
 
+    picked = sk[0].astype(F32)
+
     def add_skel(k, total):
         send_skel(k).wait_recv()
         return total + sk[k].astype(F32)
@@ -917,7 +926,7 @@
     rs[...] = jnp.zeros_like(rs)
     rs[0:1, :] = rhs[:, :128]
     rs[1:2, :] = rhs[:, 128:]
-    rs[2:3, :] = full
+    rs[2:3, :] = bad[0:1, :]
     part = dot(rows[...], gram[0:RANK, :].astype(BF)).astype(BF)
     chosen = dot_nt(part, columns[:, 0:RANK])
     part = dot_nt(rows[...], couple[...].astype(BF)).astype(BF)
@@ -1072,6 +1081,7 @@
         out_specs=[VMEM] * 3 + [pl.BlockSpec(memory_space=pltpu.SMEM)],
         scratch_shapes=[
             pltpu.VMEM((F, ROWS), BF),
+            pltpu.VMEM((8, 128), F32),
             pltpu.VMEM((ROWS // 128, 128), F32),
             pltpu.VMEM((CHUNKS, 8, CHUNK), F32),
             pltpu.VMEM((LEAVES, 128), F32),

time: 51 us -> 51 us (level)
  no operation moved by 1% of the time
where the time goes in v14:
time: 51 us; the launch traced here: 50.8 us
  Pallas kernels  48.5 us (95%)
  between operations  2.08 us (4%)
    pallas_call x1, Pallas kernels, stream(): pl.pallas_call(stream_kernel, out_shape=(*(pltpu.VMEM(shape, F32) for sha...  47.8 us

profile of v14, /device:TPU:1, one launch (start us, length us, event | category | flops | bytes accessed | tf_op | source)
XLA Modules:
  0.0 50.8 jit_solution(5510285794462642068)
XLA Ops:
  1.3 47.8 %stream.1 = (f32[1,32,512]{2,1,0:T(8,128)S(1)}, f32[1,32,256]{2,1,0:T(8,128)S(1)}, f32[1,256]{1,0:T(1,128)S(1)}, s32[1]{0:T(128)}) custom-call(bf16[48,8192]{1,0:T(8,128)(2,1)} %feat_hbm.1, bf16[64,128]{1,0:T(8,128)(2,1)} %bitcast.8, s32[64,128]{1,0:T(8,128)} %bitcast.6, s32[1,256]{1,0:T(1,128)} %pivots.1, f32[1,1]{1,0:T(1,128)} %bitcast.5.ridge, ...), custom_call_target="tpu_custom_call" | custom-call | tf_op jit(solution)/shard_map/stream/pallas_call | solution.py:1074
  49.7 0.9 %conditional.1 = ((f32[1,32,512]{2,1,0:T(8,128)}, f32[1,32,256]{2,1,0:T(8,128)}, f32[1,256]{1,0:T(1,128)})) conditional(s32[]{:T(128)} %bitcast.4, (f32[1,32,512]{2,1,0:T(8,128)S(1)}, f32[1,32,256]{2,1,0:T(8,128)S(1)}, f32[1,256]{1,0:T(1,128)S(1)}) %tuple.13, (bf16[48,8192]{1,0:T(8,128)(2,1)}, bf16[64,128]{1,0:T(8,128)(2,1)}, s32[64,128]{1,0:T(8,128)}, ...), branch_computations={%region_0.0_spmd, %region_1.0_spmd} | conditional | bytes 8 | solution.py:1178
  49.8 0.7 %emit.2 = (f32[1,32,512]{2,1,0:T(8,128)}, f32[1,32,256]{2,1,0:T(8,128)}, f32[1,256]{1,0:T(1,128)}) custom-call(f32[1,32,512]{2,1,0:T(8,128)S(1)} %get-tuple-element.22.refs_0_, f32[1,32,256]{2,1,0:T(8,128)S(1)} %get-tuple-element.23.refs_1_, f32[1,256]{1,0:T(1,128)S(1)} %get-tuple-element.24.refs_2_), custom_call_target="tpu_custom_call" | custom-call | tf_op jit(solution)/shard_map/cond/branch_0_fun/emit/pallas_call | solution.py:1158

commit v15 on v14

--- a/solution.py
+++ b/solution.py
@@ -781,13 +781,6 @@
     rx[0] = feat[0]
     ra[0] = aux[0]
 
-    place = jnp.concatenate([held[(LEAVES - b) % LEAVES] for b in range(LEAVES)], 0)
-    home = place % ROWS // PACKET
-    largest = jnp.zeros((OWNERS, 1), F32)
-    for b in range(LEAVES):
-        held_here = (iota((OWNERS, RANK), 0) == home[b : b + 1]).astype(F32)
-        largest = jnp.maximum(largest, jnp.sum(held_here, 1, keepdims=True))
-
     for copy in smalls:
         copy.wait()
     spare[...] = jnp.ones((8, 128), F32)
@@ -806,8 +799,6 @@
     rows[...] = chosen.astype(F32).astype(BF)
     lanes = number.astype(F32) + jnp.where(number < RANK, base, other - RANK)
     columns[...] = (index2 == lanes).astype(F32).astype(BF)
-    chosen = across(index[...], 4 * RANK) == iota((RANK, 4 * RANK), 1).astype(F32)
-    fours[...] = chosen.astype(F32).astype(BF)
 
     def norms(k):
         side[k] = point_side(rx[k].astype(F32), scale4)
@@ -941,6 +932,8 @@
         pc[k] = part[k * SLAB : (k + 1) * SLAB]
     each(COLS, lambda k: send_couple(k).start())
 
+    chosen = across(index[...], 4 * RANK) == iota((RANK, 4 * RANK), 1).astype(F32)
+    fours[...] = chosen.astype(F32).astype(BF)
     whole = jnp.concatenate([sk4[k] for k in range(4)], 1)
     points = dot_nt(whole, fours[...])
     fill = jnp.zeros((256 - 3 * F - 16, RANK), BF)
@@ -950,6 +943,13 @@
     crossing = (across(index[...], RANK) >= 2.0 * RANK) != (index[...].T[0:1, :] >= 2.0 * RANK)
     square = iota((RANK, RANK), 0) == iota((RANK, RANK), 1)
     tops[...] = jnp.where(crossing, value, 0.0) + jnp.where(square, ridge[...], 0.0)
+
+    place = jnp.concatenate([held[(LEAVES - b) % LEAVES] for b in range(LEAVES)], 0)
+    home = place % ROWS // PACKET
+    largest = jnp.zeros((OWNERS, 1), F32)
+    for b in range(LEAVES):
+        held_here = (iota((OWNERS, RANK), 0) == home[b : b + 1]).astype(F32)
+        largest = jnp.maximum(largest, jnp.sum(held_here, 1, keepdims=True))
 
     def finish(sends):
         return lambda k: [send(k).wait_send() for send in sends]

time: 51 us -> 51 us (level)
  no operation moved by 1% of the time
where the time goes in v15:
time: 51 us; the launch traced here: 50.8 us
  Pallas kernels  48.5 us (95%)
  between operations  2.08 us (4%)
    pallas_call x1, Pallas kernels, stream(): pl.pallas_call(stream_kernel, out_shape=(*(pltpu.VMEM(shape, F32) for sha...  47.8 us

profile of v15, /device:TPU:1, one launch (start us, length us, event | category | flops | bytes accessed | tf_op | source)
XLA Modules:
  0.0 50.8 jit_solution(3247879275559512834)
XLA Ops:
  1.3 47.8 %stream.1 = (f32[1,32,512]{2,1,0:T(8,128)S(1)}, f32[1,32,256]{2,1,0:T(8,128)S(1)}, f32[1,256]{1,0:T(1,128)S(1)}, s32[1]{0:T(128)}) custom-call(bf16[48,8192]{1,0:T(8,128)(2,1)} %feat_hbm.1, bf16[64,128]{1,0:T(8,128)(2,1)} %bitcast.8, s32[64,128]{1,0:T(8,128)} %bitcast.6, s32[1,256]{1,0:T(1,128)} %pivots.1, f32[1,1]{1,0:T(1,128)} %bitcast.5.ridge, ...), custom_call_target="tpu_custom_call" | custom-call | tf_op jit(solution)/shard_map/stream/pallas_call | solution.py:1074
  49.7 0.9 %conditional.1 = ((f32[1,32,512]{2,1,0:T(8,128)}, f32[1,32,256]{2,1,0:T(8,128)}, f32[1,256]{1,0:T(1,128)})) conditional(s32[]{:T(128)} %bitcast.4, (f32[1,32,512]{2,1,0:T(8,128)S(1)}, f32[1,32,256]{2,1,0:T(8,128)S(1)}, f32[1,256]{1,0:T(1,128)S(1)}) %tuple.13, (bf16[48,8192]{1,0:T(8,128)(2,1)}, bf16[64,128]{1,0:T(8,128)(2,1)}, s32[64,128]{1,0:T(8,128)}, ...), branch_computations={%region_0.0_spmd, %region_1.0_spmd} | conditional | bytes 8 | solution.py:1178
  49.8 0.7 %emit.2 = (f32[1,32,512]{2,1,0:T(8,128)}, f32[1,32,256]{2,1,0:T(8,128)}, f32[1,256]{1,0:T(1,128)}) custom-call(f32[1,32,512]{2,1,0:T(8,128)S(1)} %get-tuple-element.22.refs_0_, f32[1,32,256]{2,1,0:T(8,128)S(1)} %get-tuple-element.23.refs_1_, f32[1,256]{1,0:T(1,128)S(1)} %get-tuple-element.24.refs_2_), custom_call_target="tpu_custom_call" | custom-call | tf_op jit(solution)/shard_map/cond/branch_0_fun/emit/pallas_call | solution.py:1158

commit v16 on v14

--- a/solution.py
+++ b/solution.py
@@ -755,7 +755,7 @@
             return total + dot_nt(chosen, jnp.concatenate([joined_of(t), rest], 0))
 
         shape = (LEAVES * SLOTS, 128)
-        taken = lax.fori_loop(0, CHUNKS, take, jnp.zeros(shape, F32), unroll=4)
+        taken = lax.fori_loop(0, CHUNKS, take, jnp.zeros(shape, F32), unroll=8)
         taken = jnp.where(iota(shape, 1) == WHICH, which, taken)
         taken = jnp.where(iota(shape, 1) == FULL, full, taken).astype(BF)
         for b in range(LEAVES):

time: 51 us -> 50.3 us (0.986)
  Pallas kernels: 48.5 us -> 47.8 us
    pallas_call x1, Pallas kernels: 47.8 us -> 47.1 us  [stream(): pl.pallas_call(stream_kernel, out_shape=(*(pltpu.VMEM(shape, F32) for sha...]
where the time goes in v16:
time: 50.3 us; the launch traced here: 50.1 us
  Pallas kernels  47.8 us (95%)
  between operations  2.08 us (4%)
    pallas_call x1, Pallas kernels, stream(): pl.pallas_call(stream_kernel, out_shape=(*(pltpu.VMEM(shape, F32) for sha...  47.1 us

profile of v16, /device:TPU:1, one launch (start us, length us, event | category | flops | bytes accessed | tf_op | source)
XLA Modules:
  0.0 50.1 jit_solution(10599415348368785448)
XLA Ops:
  1.3 47.1 %stream.1 = (f32[1,32,512]{2,1,0:T(8,128)S(1)}, f32[1,32,256]{2,1,0:T(8,128)S(1)}, f32[1,256]{1,0:T(1,128)S(1)}, s32[1]{0:T(128)}) custom-call(bf16[48,8192]{1,0:T(8,128)(2,1)} %feat_hbm.1, bf16[64,128]{1,0:T(8,128)(2,1)} %bitcast.8, s32[64,128]{1,0:T(8,128)} %bitcast.6, s32[1,256]{1,0:T(1,128)} %pivots.1, f32[1,1]{1,0:T(1,128)} %bitcast.5.ridge, ...), custom_call_target="tpu_custom_call" | custom-call | tf_op jit(solution)/shard_map/stream/pallas_call | solution.py:1074
  49.0 0.9 %conditional.1 = ((f32[1,32,512]{2,1,0:T(8,128)}, f32[1,32,256]{2,1,0:T(8,128)}, f32[1,256]{1,0:T(1,128)})) conditional(s32[]{:T(128)} %bitcast.4, (f32[1,32,512]{2,1,0:T(8,128)S(1)}, f32[1,32,256]{2,1,0:T(8,128)S(1)}, f32[1,256]{1,0:T(1,128)S(1)}) %tuple.13, (bf16[48,8192]{1,0:T(8,128)(2,1)}, bf16[64,128]{1,0:T(8,128)(2,1)}, s32[64,128]{1,0:T(8,128)}, ...), branch_computations={%region_0.0_spmd, %region_1.0_spmd} | conditional | bytes 8 | solution.py:1178
  49.0 0.7 %emit.2 = (f32[1,32,512]{2,1,0:T(8,128)}, f32[1,32,256]{2,1,0:T(8,128)}, f32[1,256]{1,0:T(1,128)}) custom-call(f32[1,32,512]{2,1,0:T(8,128)S(1)} %get-tuple-element.22.refs_0_, f32[1,32,256]{2,1,0:T(8,128)S(1)} %get-tuple-element.23.refs_1_, f32[1,256]{1,0:T(1,128)S(1)} %get-tuple-element.24.refs_2_), custom_call_target="tpu_custom_call" | custom-call | tf_op jit(solution)/shard_map/cond/branch_0_fun/emit/pallas_call | solution.py:1158
